TPU v7x, 256 devices: a whole 4x4x8 slice. The times are simulated.
256 devices in a mesh: dp: 8 (over z_hi, core), tile: 32 (over y, x, z_lo).
Axes of the slice: x: 4, y: 4, z: 8 (z_hi: 4, z_lo: 2; z = z_hi * 2 + z_lo), core: 2. Of those that a mesh axis runs over, the one named last changes fastest.
Arguments:
- tokens: bfloat16 [8, 4096, 1024], P('dp', 'tile'), may hold values from -13 to 13
- timestep: int32 [8], P('dp'), may hold values from 0 to 999
- table: bfloat16 [1000, 2048], replicated, may hold values from -2.5 to 2.5
- w_qkv: bfloat16 [1024, 3072], replicated, may hold values from -0.197858 to 0.197858
- grad_out: bfloat16 [8, 4096, 1024], P('dp', 'tile'), may hold values from -6 to 6
Outputs:
- attended: bfloat16 [8, 4096, 1024], P('dp', 'tile')
- token_gradient: bfloat16 [8, 4096, 1024], P('dp', 'tile')
- modulation_grads: float32 [8, 2048], P('dp')
- grad_wqkv: float32 [1024, 3072], P('tile')
All inputs are finite; a program needn't handle non-finite values.
Results may differ from a plain program's by a relative error of at most 0.019.
The roundings to bfloat16 on the way count: a program that leaves them out, or rounds other values in their place, can miss the bound.
Values may be sent and summed in bfloat16 or wider, within the bound.
No kernel may reach another device: no remote copies, remote signals or barrier semaphores. Data moves between devices by JAX's collectives and lax.ppermute only.
A program may use at most 128 MiB of HBM per device.

v0:
```python
import math

import jax
import jax.numpy as jnp
from jax import lax
from jax.sharding import PartitionSpec as P

HEADS = 16


def head_pass(queries, keys, values, grads):
    rows = queries.shape[0]
    depth = queries.shape[1]
    factor = depth ** (-0.5)
    block = math.gcd(rows, 512)
    count = rows // block
    q_blocks = queries.reshape(count, block, depth)
    g_blocks = grads.reshape(count, block, depth)

    def step(carry, item):
        key_grad, value_grad = carry
        q_part, g_part = item
        scores = (
            lax.dot_general(
                q_part, keys, (((1,), (1,)), ((), ())), preferred_element_type=jnp.float32
            )
            * factor
        )
        top = jnp.max(scores, axis=1, keepdims=True)
        expo = jnp.exp(scores - top)
        probs = expo / jnp.sum(expo, axis=1, keepdims=True)
        probs_low = probs.astype(jnp.bfloat16)
        output = jnp.dot(probs_low, values, preferred_element_type=jnp.float32)
        dprob = lax.dot_general(
            g_part, values, (((1,), (1,)), ((), ())), preferred_element_type=jnp.float32
        )
        delta = jnp.sum(g_part.astype(jnp.float32) * output, axis=1, keepdims=True)
        dscore = (probs * (dprob - delta)).astype(jnp.bfloat16)
        query_grad = jnp.dot(dscore, keys, preferred_element_type=jnp.float32) * factor
        key_grad = (
            key_grad
            + lax.dot_general(
                dscore, q_part, (((0,), (0,)), ((), ())), preferred_element_type=jnp.float32
            )
            * factor
        )
        value_grad = value_grad + lax.dot_general(
            probs_low, g_part, (((0,), (0,)), ((), ())), preferred_element_type=jnp.float32
        )
        return ((key_grad, value_grad), (output, query_grad))

    start = (jnp.zeros(keys.shape, jnp.float32), jnp.zeros(values.shape, jnp.float32))
    (key_grad, value_grad), (output, query_grad) = lax.scan(step, start, (q_blocks, g_blocks))
    return (output.reshape(rows, depth), query_grad.reshape(rows, depth), key_grad, value_grad)


def on_device(tokens, timestep, table, w_qkv, grad_out):
    x_in = tokens[0]
    ntok = x_in.shape[0]
    width = x_in.shape[1]
    depth = width // HEADS
    group = lax.axis_size("tile")
    copies = group // HEADS
    share = ntok // copies
    onehot = (lax.iota(jnp.int32, table.shape[0])[None, :] == timestep[:, None]).astype(
        jnp.bfloat16
    )
    mod = jnp.dot(onehot, table, preferred_element_type=jnp.float32)[0]
    scale_factor = mod[:width]
    shift_offset = mod[width:]
    tokens_float = x_in.astype(jnp.float32)
    inverse_deviation = 1.0 / jnp.sqrt(
        jnp.mean(tokens_float * tokens_float, axis=1, keepdims=True) + 1e-06
    )
    centered_scaled = tokens_float * inverse_deviation
    normalized_tokens = (centered_scaled * (1.0 + scale_factor) + shift_offset).astype(jnp.bfloat16)
    qkv = jnp.dot(normalized_tokens, w_qkv, preferred_element_type=jnp.float32).astype(jnp.bfloat16)

    def to_heads(block):
        return (
            block.reshape(copies, share, HEADS, depth)
            .transpose(2, 0, 1, 3)
            .reshape(group, share, depth)
        )

    key_val = jnp.concatenate(
        [
            qkv[:, width : 2 * width].reshape(ntok, HEADS, depth),
            qkv[:, 2 * width :].reshape(ntok, HEADS, depth),
        ],
        axis=2,
    )
    key_val = jnp.repeat(key_val.transpose(1, 0, 2), copies, axis=0)
    q_recv, g_recv, kv_recv = (
        lax.all_to_all(to_heads(qkv[:, :width]), "tile", split_axis=0, concat_axis=1, tiled=True),
        lax.all_to_all(to_heads(grad_out[0]), "tile", split_axis=0, concat_axis=1, tiled=True),
        lax.all_to_all(key_val, "tile", split_axis=0, concat_axis=1, tiled=True),
    )
    output, query_grad, key_grad, value_grad = head_pass(
        q_recv[0], kv_recv[0, :, :depth], kv_recv[0, :, depth:], g_recv[0]
    )
    first = jnp.concatenate([output, query_grad], axis=1)[None]
    second = jnp.concatenate([key_grad, value_grad], axis=1)[None]
    back_one, back_two = (
        lax.all_to_all(first, "tile", split_axis=1, concat_axis=0, tiled=True),
        lax.all_to_all(second, "tile", split_axis=1, concat_axis=0, tiled=True),
    )
    back_one = (
        back_one.reshape(HEADS, copies, share, 2 * depth)
        .transpose(1, 2, 0, 3)
        .reshape(ntok, HEADS, 2 * depth)
    )
    back_two = jnp.sum(back_two.reshape(HEADS, copies, ntok, 2 * depth), axis=1).transpose(1, 0, 2)
    attended = back_one[:, :, :depth].reshape(ntok, width).astype(jnp.bfloat16)
    dqkv = jnp.concatenate(
        [
            back_one[:, :, depth:].reshape(ntok, width),
            back_two[:, :, :depth].reshape(ntok, width),
            back_two[:, :, depth:].reshape(ntok, width),
        ],
        axis=1,
    ).astype(jnp.bfloat16)
    normalized_grad = lax.dot_general(
        dqkv, w_qkv, (((1,), (1,)), ((), ())), preferred_element_type=jnp.float32
    )
    columns = lax.all_to_all(normalized_tokens, "tile", split_axis=1, concat_axis=0, tiled=True)
    partial_grad = lax.dot_general(
        columns,
        lax.all_gather(dqkv, "tile", axis=0, tiled=True),
        (((0,), (0,)), ((), ())),
        preferred_element_type=jnp.float32,
    )
    grad_wqkv = lax.psum(partial_grad.astype(jnp.bfloat16), "dp").astype(jnp.float32)
    local_modulation = jnp.concatenate(
        [jnp.sum(normalized_grad * centered_scaled, axis=0), jnp.sum(normalized_grad, axis=0)]
    )
    modulation_grads = lax.psum(local_modulation, "tile")
    norm_input_grad = normalized_grad * (1.0 + scale_factor)
    token_gradient = (
        inverse_deviation
        * (
            norm_input_grad
            - centered_scaled * jnp.mean(norm_input_grad * centered_scaled, axis=1, keepdims=True)
        )
    ).astype(jnp.bfloat16)
    return (attended[None], token_gradient[None], modulation_grads[None], grad_wqkv)


def solution(mesh):
    placed = (P("dp", "tile", None), P("dp"), P(), P(), P("dp", "tile", None))
    return jax.shard_map(
        on_device,
        mesh=mesh,
        in_specs=placed,
        out_specs=(P("dp", "tile", None), P("dp", "tile", None), P("dp", None), P("tile", None)),
        check_vma=False,
    )
```

profile of v0, /device:TPU:1, one launch (start us, length us, event | category | flops | bytes accessed | tf_op | source)
XLA Modules:
  0.0 890.8 jit_solution(17950613946948972709)
XLA Ops:
  11.8 4.0 convolution_convert_fusion
  17.5 9.2 %all-to-all-start = ((bf16[32,2,2048]{2,1,0:T(2,128)(2,1)}), bf16[32,2,2048]{2,1,0:T(2,128)(2,1)S(1)}, u32[]{:S(2)}, u32[]{:S(2)}) async-start(bf16[32,2,2048]{2,1,0:T(2,128)(2,1)} %reshape.169), calls=%async_computation | async-start | bytes 524288 | tf_op jit(solution)/shard_map/all_to_all | solution.py:95
  28.3 7.0 all-to-all-done
  35.3 3.9 all-to-all-start.2
  39.9 7.6 all-to-all-done.2
  48.6 4.1 all-to-all-start.1
  54.5 12.9 %all-to-all-done.1 = bf16[32,128,128]{2,1,0:T(8,128)(2,1)S(1)} async-done(((bf16[32,128,128]{2,1,0:T(8,128)(2,1)}), bf16[32,128,128]{2,1,0:T(8,128)(2,1)S(1)}, u32[]{:S(2)}, u32[]{:S(2)}) %all-to-all-start.1) | async-done | bytes 1048608 | tf_op jit(solution)/shard_map/all_to_all | solution.py:97
  70.4 123.4 %while.17 = (s32[]{:T(128)}, f32[4096,64]{0,1:T(8,128)S(1)}, f32[4096,64]{0,1:T(8,128)}, f32[4,512,64]{1,0,2:T(4,128)}, f32[4,512,64]{1,0,2:T(4,128)}, /*index=5...) while((s32[]{:T(128)}, f32[4096,64]{0,1:T(8,128)S(1)}, ...), condition=%wide.region_5.6_spmd.clone, body=%wide.region_1.5_spmd.clone.sunk | while | flops 1639315968 | bytes 115554536 | solution.py:53
  77.6 3.8 multiply_convert_fusion.3
  84.6 5.3 convolution_add_fusion.2
  93.7 3.6 fusion.71
  97.4 3.6 dynamic_update_slice.12
  108.3 3.8 multiply_convert_fusion.3
  115.3 5.5 convolution_add_fusion.2
  124.6 3.6 fusion.71
  128.3 3.6 dynamic_update_slice.12
  139.2 3.8 multiply_convert_fusion.3
  146.2 5.5 convolution_add_fusion.2
  159.2 3.6 dynamic_update_slice.12
  170.1 3.8 multiply_convert_fusion.3
  177.1 5.5 convolution_add_fusion.2
  190.1 3.6 dynamic_update_slice.12
  198.2 5.7 all-to-all-start.3
  211.1 7.3 all-to-all-done.3
  218.4 5.4 all-to-all-start.4
  226.3 23.7 %all-to-all-done.4 = f32[1,4096,128]{2,0,1:T(1,128)S(1)} async-done(((f32[1,4096,128]{2,0,1:T(1,128)}), f32[1,4096,128]{2,0,1:T(1,128)S(1)}, u32[]{:S(2)}, u32[]{:S(2)}) %all-to-all-start.4) | async-done | bytes 2097184 | tf_op jit(solution)/shard_map/all_to_all | solution.py:106
  254.2 6.3 all-to-all-start.5
  261.7 5.1 multiply_reduce_fusion.2
  266.8 77.6 %psum.14 = f32[1,2048]{1,0:T(1,128)} all-reduce(f32[1,2048]{1,0:T(1,128)S(1)} %bitcast.151), channel_id=1, replica_groups=mesh['dp'=8,'tile'=32] {'tile'}, use_global_device_ids=true, to_apply=%region_10.11 | all-reduce | flops 2048 | bytes 16384 | tf_op jit(solution)/shard_map/psum | solution.py:137
  344.4 452.3 %all-gather.2.cloned.1.call-done = bf16[4096,3072]{0,1:T(8,128)(2,1)} async-done(((bf16[128,3072]{0,1:T(8,128)(2,1)}), bf16[4096,3072]{0,1:T(8,128)(2,1)}) %all-gather.2.cloned.1.call-update) | async-done | bytes 25165840 | tf_op jit(solution)/shard_map/all_gather | solution.py:129
  796.7 13.0 %convolution_convert_fusion.1 = bf16[32,3072]{1,0:T(8,128)(2,1)} fusion(bf16[4096,3072]{0,1:T(8,128)(2,1)} %all-gather.2.cloned.1.call-done, bf16[128,32,32]{0,2,1:T(8,128)(2,1)S(1)} %all-to-all-done.5), kind=kOutput, calls=%fused_computation.28 | convolution fusion | flops 805404672 | bytes 25624576 | tf_op jit(solution)/shard_map/dot_general | solution.py:127
  810.6 71.6 %all-reduce.2.cloned.1.call-done = bf16[32,3072]{1,0:T(8,128)(2,1)} async-done(((bf16[32,3072]{1,0:T(8,128)(2,1)}), bf16[32,3072]{1,0:T(8,128)(2,1)}) %all-reduce.2.cloned.1.call-update) | async-done | bytes 196624 | tf_op jit(solution)/shard_map/psum | solution.py:133
  (123 shorter events, 100.2 us)
Async XLA Ops:
  11.8 14.9 %copy-start.6 = (bf16[1,128,1024]{2,1,0:T(8,128)(2,1)S(1)}, bf16[1,128,1024]{2,1,0:T(8,128)(2,1)}, u32[]{:S(2)}) copy-start(bf16[1,128,1024]{2,1,0:T(8,128)(2,1)} %param.11) | copy-start | bytes 786436
  17.5 17.8 %all-to-all-start = ((bf16[32,2,2048]{2,1,0:T(2,128)(2,1)}), bf16[32,2,2048]{2,1,0:T(2,128)(2,1)S(1)}, u32[]{:S(2)}, u32[]{:S(2)}) async-start(bf16[32,2,2048]{2,1,0:T(2,128)(2,1)} %reshape.169), calls=%async_computation | async-start | bytes 524288 | tf_op jit(solution)/shard_map/all_to_all | solution.py:95
  35.3 12.2 %all-to-all-start.2 = ((bf16[32,2,2048]{2,1,0:T(2,128)(2,1)}), bf16[32,2,2048]{2,1,0:T(2,128)(2,1)S(1)}, u32[]{:S(2)}, u32[]{:S(2)}) async-start(bf16[32,2,2048]{2,1,0:T(2,128)(2,1)} %reshape.171), calls=%async_computation.2 | async-start | bytes 524288 | tf_op jit(solution)/shard_map/all_to_all | solution.py:96
  48.6 18.8 %all-to-all-start.1 = ((bf16[32,128,128]{2,1,0:T(8,128)(2,1)}), bf16[32,128,128]{2,1,0:T(8,128)(2,1)S(1)}, u32[]{:S(2)}, u32[]{:S(2)}) async-start(bf16[32,128,128]{2,1,0:T(8,128)(2,1)} %bitcast.9), calls=%async_computation.1 | async-start | bytes 2097152 | tf_op jit(solution)/shard_map/all_to_all | solution.py:97
  67.5 1.0 copy-start.1
  70.4 14.2 %copy-start.2 = (bf16[4,512,64]{1,2,0:T(8,128)(2,1)}, bf16[4,512,64]{1,2,0:T(8,128)(2,1)S(1)}, u32[]{:S(2)}) copy-start(bf16[4,512,64]{1,2,0:T(8,128)(2,1)S(1)} %get-tuple-element.256) | copy-start | bytes 786436 | tf_op jit(solution)/shard_map/while
  76.2 5.2 copy-start
  93.7 7.4 copy-start.3
  101.1 14.2 %copy-start.2 = (bf16[4,512,64]{1,2,0:T(8,128)(2,1)}, bf16[4,512,64]{1,2,0:T(8,128)(2,1)S(1)}, u32[]{:S(2)}) copy-start(bf16[4,512,64]{1,2,0:T(8,128)(2,1)S(1)} %get-tuple-element.256) | copy-start | bytes 786436 | tf_op jit(solution)/shard_map/while
  106.9 5.2 copy-start
  124.6 7.4 copy-start.3
  132.0 14.2 %copy-start.2 = (bf16[4,512,64]{1,2,0:T(8,128)(2,1)}, bf16[4,512,64]{1,2,0:T(8,128)(2,1)S(1)}, u32[]{:S(2)}) copy-start(bf16[4,512,64]{1,2,0:T(8,128)(2,1)S(1)} %get-tuple-element.256) | copy-start | bytes 786436 | tf_op jit(solution)/shard_map/while
  137.8 5.2 copy-start
  155.4 7.4 copy-start.3
  162.9 14.2 %copy-start.2 = (bf16[4,512,64]{1,2,0:T(8,128)(2,1)}, bf16[4,512,64]{1,2,0:T(8,128)(2,1)S(1)}, u32[]{:S(2)}) copy-start(bf16[4,512,64]{1,2,0:T(8,128)(2,1)S(1)} %get-tuple-element.256) | copy-start | bytes 786436 | tf_op jit(solution)/shard_map/while
  168.6 5.2 copy-start
  186.3 7.4 copy-start.3
  198.2 20.3 %all-to-all-start.3 = ((f32[1,2048,128]{2,0,1:T(1,128)}), f32[1,2048,128]{2,0,1:T(1,128)}, u32[]{:S(2)}, u32[]{:S(2)}) async-start(f32[1,2048,128]{2,0,1:T(1,128)} %copy.48), calls=%async_computation.3 | async-start | bytes 2097152 | tf_op jit(solution)/shard_map/all_to_all | solution.py:105
  218.4 31.6 %all-to-all-start.4 = ((f32[1,4096,128]{2,0,1:T(1,128)}), f32[1,4096,128]{2,0,1:T(1,128)S(1)}, u32[]{:S(2)}, u32[]{:S(2)}) async-start(f32[1,4096,128]{2,0,1:T(1,128)} %bitcast.25), calls=%async_computation.4 | async-start | bytes 4194304 | tf_op jit(solution)/shard_map/all_to_all | solution.py:106
  223.8 572.9 %all-gather.2.cloned.1.call-start = ((), (), s32[]{:S(2)}) async-start(), calls=%async_computation.6 | async-start | bytes 25952256 | tf_op jit(solution)/shard_map/all_gather | solution.py:129
  223.9 29.0 %copy-start.4 = (bf16[1,128,1024]{2,1,0:T(8,128)(2,1)S(1)}, bf16[1,128,1024]{2,1,0:T(8,128)(2,1)}, u32[]{:S(2)}) copy-start(bf16[1,128,1024]{2,1,0:T(8,128)(2,1)} %param.7) | copy-start | bytes 786436
  250.2 11.4 %copy-start.5 = (bf16[128,16,64]{0,2,1:T(8,128)(2,1)S(1)}, bf16[128,16,64]{0,2,1:T(8,128)(2,1)}, u32[]{:S(2)}) copy-start(bf16[128,16,64]{0,2,1:T(8,128)(2,1)} %copy.68) | copy-start | bytes 786436
  254.2 90.2 %all-to-all-start.5 = ((bf16[128,32,32]{0,2,1:T(8,128)(2,1)}), bf16[128,32,32]{0,2,1:T(8,128)(2,1)S(1)}, u32[]{:S(2)}, u32[]{:S(2)}) async-start(bf16[128,32,32]{0,2,1:T(8,128)(2,1)} %add_convert_fusion), calls=%async_computation.5 | async-start | bytes 524288 | tf_op jit(solution)/shard_map/all_to_all | solution.py:126
  260.5 621.7 %all-reduce.2.cloned.1.call-start = ((), (), s32[]{:S(2)}) async-start(), calls=%async_computation.7 | async-start | bytes 393216 | tf_op jit(solution)/shard_map/psum | solution.py:133
Sparse Core Ops, SparseCore 0:
  253.0 543.6 all-gather.1
  809.8 72.3 all-reduce.1
where the time goes:
time: 893 us; the launch traced here: 891 us
  waiting for transfers between devices  582 us (65%)
  matrix products  104 us (12%)
  blocking collectives  77.6 us (9%)
  local copies, waits for them, and re-layouts  51 us (6%)
  starting transfers between devices  34.7 us (4%)
  other arithmetic  25.6 us (3%)
  between operations  15 us (2%)
    all_gather x1, waiting for transfers between devices, on_device(): lax.all_gather(dqkv, 'tile', axis=0, tiled=True)  452 us
    psum x1, blocking collectives, on_device(): modulation_grads = lax.psum(local_modulation, 'tile')  77.6 us
    psum x1, waiting for transfers between devices, on_device(): lax.psum(partial_grad.astype(jnp.bfloat16), 'dp').astype(jnp.float32)  71.6 us
    dynamic_update_slice x16, local copies, waits for them, and re-layouts, head_pass(): lax.scan(step, start, (q_blocks, g_blocks))  30.1 us
    all_to_all x1, waiting for transfers between devices, on_device(): lax.all_to_all(second, 'tile', split_axis=1, concat_axis=0, tiled=True)  23.7 us
    dot_general x4, matrix products, step(): lax.dot_general(probs_low, g_part, (((0,), (0,)), ((), ())), preferred_el...  21.8 us
  transfers between devices with their start and end apart: 8, of which 7 were waited for; matrix products, arithmetic and copies ran while one was open for 2% of the time, Pallas kernels for 0%

commit v1 on v0

v1 whole, which is shorter than its diff:
```python
import functools

import jax
import jax.numpy as jnp
from jax import lax
from jax.experimental import pallas as pl
from jax.experimental.pallas import tpu as pltpu
from jax.sharding import PartitionSpec as P

HEADS = 16
DEPTH = 64
LOG2E = 1.4426950408889634
BF16 = jnp.bfloat16
F32 = jnp.float32
EVERY = ("dp", "tile")

SWAP = [
    ((zh * 2 + core) * 32 + yx * 2 + zl, (zh * 2 + zl) * 32 + yx * 2 + core)
    for zh in range(4)
    for core in range(2)
    for yx in range(16)
    for zl in range(2)
]
PLANE = [[yx * 2 + zl for yx in range(16)] for zl in range(2)]
OTHER_CORE = [(d, d ^ 1) for d in range(8)]


def swap(x):
    return lax.ppermute(x, EVERY, SWAP)


def plane_exchange(x):
    return lax.all_to_all(
        x, "tile", split_axis=0, concat_axis=0, tiled=True, axis_index_groups=PLANE
    )


def dot(a, b):
    return jnp.dot(a, b, preferred_element_type=F32)


def dot_t(a, b):
    return lax.dot_general(a, b, (((1,), (1,)), ((), ())), preferred_element_type=F32)


def low_lanes(shape):
    return lax.broadcasted_iota(jnp.int32, shape, 1) < DEPTH


def project_kernel(x_ref, g_ref, mod_ref, wq_ref, wk_ref, wv_ref, normed_ref, out_ref):
    @pl.when(pl.program_id(0) == 0)
    def _():
        x = x_ref[...].astype(F32)
        inv = 1.0 / jnp.sqrt(jnp.mean(x * x, axis=1, keepdims=True) + 1e-06)
        mod = mod_ref[...].astype(F32)
        normed_ref[...] = ((x * inv) * (1.0 + mod[0:1]) + mod[1:2]).astype(BF16)

    normed = normed_ref[...]
    q = dot(normed, wq_ref[...]).astype(BF16).astype(F32)
    k = dot(normed, wk_ref[...]).astype(BF16).astype(F32)
    v = dot(normed, wv_ref[...]).astype(BF16).astype(F32)
    g = g_ref[...].astype(F32)
    low = low_lanes(q.shape)
    out_ref[0, 0:128] = jnp.where(low, q, pltpu.roll(g, DEPTH, 1)).astype(BF16)
    out_ref[0, 128:256] = jnp.where(low, k, pltpu.roll(v, DEPTH, 1)).astype(BF16)
    out_ref[1, 0:128] = jnp.where(low, pltpu.roll(q, DEPTH, 1), g).astype(BF16)
    out_ref[1, 128:256] = jnp.where(low, pltpu.roll(k, DEPTH, 1), v).astype(BF16)


def project(x, g, mod, w):
    return pl.pallas_call(
        project_kernel,
        grid=(HEADS // 2,),
        in_specs=[
            pl.BlockSpec((128, 1024), lambda i: (0, 0)),
            pl.BlockSpec((128, 128), lambda i: (0, i)),
            pl.BlockSpec((2, 1024), lambda i: (0, 0)),
            pl.BlockSpec((1024, 128), lambda i: (0, i)),
            pl.BlockSpec((1024, 128), lambda i: (0, 8 + i)),
            pl.BlockSpec((1024, 128), lambda i: (0, 16 + i)),
        ],
        out_specs=[
            pl.BlockSpec((128, 1024), lambda i: (0, 0)),
            pl.BlockSpec((2, 256, 128), lambda i: (i, 0, 0)),
        ],
        out_shape=[
            jax.ShapeDtypeStruct((128, 1024), BF16),
            jax.ShapeDtypeStruct((HEADS, 256, 128), BF16),
        ],
        compiler_params=pltpu.CompilerParams(dimension_semantics=("arbitrary",)),
        cost_estimate=pl.CostEstimate(
            flops=2 * 128 * 1024 * 3072, bytes_accessed=8 << 20, transcendentals=0
        ),
        name="project",
    )(x, g, mod, w, w, w)


def attention_kernel(
    bq, kt, recv_ref, kvp_ref, dqo_ref, own_ref, other_ref, kv, kvt, acc, s_scr, dp_scr, pb_scr
):
    i = pl.program_id(0)
    nk = kv.shape[0]
    half = nk // 2
    tiles = [pl.ds(t * kt, kt) for t in range(nk // kt)]

    @pl.when(i == 0)
    def _():
        kv[:half] = recv_ref[:, 128:, :].reshape(half, 128)
        kv[half:] = kvp_ref[...].reshape(half, 128)
        acc[...] = jnp.zeros_like(acc)
        for t in tiles:
            kvt[:, t] = kv[t].T

    srcs = bq // 128
    qg = recv_ref[pl.ds(i * srcs, srcs), :128, :].reshape(bq, 128)
    low = low_lanes(qg.shape)
    zero = jnp.zeros_like(qg)
    q0 = jnp.where(low, qg * jnp.asarray(0.125, BF16), zero)
    g0 = jnp.where(low, zero, qg)
    q0t = q0.T
    g0t = g0.T
    top = jnp.full((8, bq), -jnp.inf, F32)
    for t in tiles:
        s = dot(kv[t], q0t)
        s_scr[t] = s
        top = jnp.maximum(top, jnp.max(s.reshape(kt // 8, 8, bq), axis=0))
    top = jnp.max(top, axis=0, keepdims=True)
    total = jnp.zeros((8, bq), F32)
    for t in tiles:
        e = jnp.exp2((s_scr[t] - top) * LOG2E)
        s_scr[t] = e
        total = total + jnp.sum(e.reshape(kt // 8, 8, bq), axis=0)
        dp_scr[t] = dot(kv[t], g0t)
    inv = 1.0 / jnp.sum(total, axis=0, keepdims=True)
    o_t = jnp.zeros((DEPTH, bq), F32)
    for t in tiles:
        pb = (s_scr[t] * inv).astype(BF16)
        pb_scr[t] = pb
        o_t = o_t + dot(kvt[DEPTH:, t], pb)
    delta = jnp.sum(o_t * g0t[DEPTH:].astype(F32), axis=0, keepdims=True)
    dq_t = jnp.zeros((DEPTH, bq), F32)
    for t in tiles:
        ds = ((s_scr[t] * inv) * (dp_scr[t] - delta)).astype(BF16)
        dq_t = dq_t + dot(kvt[:DEPTH, t], ds)
        acc[t] += dot(ds, q0) + dot(pb_scr[t], g0)
    dqo = jnp.concatenate([dq_t * 0.125, o_t], axis=0).T.astype(BF16)
    dqo_ref[...] = dqo.reshape(srcs, 128, 128)

    @pl.when(i == pl.num_programs(0) - 1)
    def _():
        own_ref[...] = acc[:half].reshape(16, 128, 128)
        other_ref[...] = acc[half:].astype(BF16).reshape(16, 128, 128)


def attention(recv, kvp, bq=512, kt=256):
    nq, nk = 2048, 4096
    srcs = bq // 128
    whole = lambda i: (0, 0, 0)
    return pl.pallas_call(
        functools.partial(attention_kernel, bq, kt),
        grid=(nq // bq,),
        in_specs=[
            pl.BlockSpec((16, 256, 128), whole),
            pl.BlockSpec((16, 128, 128), whole),
        ],
        out_specs=[
            pl.BlockSpec((srcs, 128, 128), lambda i: (i, 0, 0)),
            pl.BlockSpec((16, 128, 128), whole),
            pl.BlockSpec((16, 128, 128), whole),
        ],
        out_shape=[
            jax.ShapeDtypeStruct((16, 128, 128), BF16),
            jax.ShapeDtypeStruct((16, 128, 128), F32),
            jax.ShapeDtypeStruct((16, 128, 128), BF16),
        ],
        scratch_shapes=[
            pltpu.VMEM((nk, 128), BF16),
            pltpu.VMEM((128, nk), BF16),
            pltpu.VMEM((nk, 128), F32),
            pltpu.VMEM((nk, bq), F32),
            pltpu.VMEM((nk, bq), F32),
            pltpu.VMEM((nk, bq), BF16),
        ],
        compiler_params=pltpu.CompilerParams(
            vmem_limit_bytes=56 * 1024 * 1024, dimension_semantics=("arbitrary",)
        ),
        cost_estimate=pl.CostEstimate(
            flops=6 * 2 * nq * nk * 256, bytes_accessed=4 << 20, transcendentals=nq * nk
        ),
        name="attention",
    )(recv, kvp)


def weight_kernel(normed_ref, back_ref, out_ref, back_t):
    @pl.when(pl.program_id(0) == 0)
    def _():
        for s in range(16):
            back_t[:128, s * 128 : (s + 1) * 128] = back_ref[s, :128].T
            back_t[128:, s * 128 : (s + 1) * 128] = back_ref[s, 128:].T

    out_ref[...] = dot(back_t[...], normed_ref[...]).T.astype(BF16)


def weight_grad(normed, back):
    return pl.pallas_call(
        weight_kernel,
        grid=(4,),
        in_specs=[
            pl.BlockSpec((2048, 256), lambda i: (0, i)),
            pl.BlockSpec((16, 256, 128), lambda i: (0, 0, 0)),
        ],
        out_specs=pl.BlockSpec((256, 256), lambda i: (i, 0)),
        out_shape=jax.ShapeDtypeStruct((1024, 256), BF16),
        scratch_shapes=[pltpu.VMEM((256, 2048), BF16)],
        compiler_params=pltpu.CompilerParams(
            vmem_limit_bytes=32 * 1024 * 1024, dimension_semantics=("arbitrary",)
        ),
        cost_estimate=pl.CostEstimate(
            flops=2 * 2048 * 1024 * 256, bytes_accessed=6 << 20, transcendentals=0
        ),
        name="weight_grad",
    )(normed, back)


def token_kernel(
    x_ref, mod_ref, back_ref, wq_ref, wk_ref, wv_ref, att_ref, grad_ref, sums_ref, acc
):
    i = pl.program_id(0)
    low = low_lanes((128, 128))
    a = back_ref[0].astype(F32)
    b = back_ref[1].astype(F32)
    a_roll = pltpu.roll(a, DEPTH, 1)
    b_roll = pltpu.roll(b, DEPTH, 1)
    dq = jnp.where(low, a[:128], b_roll[:128]).astype(BF16)
    att_ref[...] = jnp.where(low, a_roll[:128], b[:128]).astype(BF16)
    dk = jnp.where(low, a[128:], b_roll[128:]).astype(BF16)
    dv = jnp.where(low, a_roll[128:], b[128:]).astype(BF16)
    part = dot_t(dq, wq_ref[...]) + dot_t(dk, wk_ref[...]) + dot_t(dv, wv_ref[...])

    @pl.when(i == 0)
    def _():
        acc[...] = part

    @pl.when(i > 0)
    def _():
        acc[...] += part

    @pl.when(i == pl.num_programs(0) - 1)
    def _():
        x = x_ref[...].astype(F32)
        inv = 1.0 / jnp.sqrt(jnp.mean(x * x, axis=1, keepdims=True) + 1e-06)
        xhat = x * inv
        dn = acc[...]
        sums_ref[0:1] = jnp.sum(dn * xhat, axis=0, keepdims=True)
        sums_ref[1:2] = jnp.sum(dn, axis=0, keepdims=True)
        gn = dn * (1.0 + mod_ref[0:1].astype(F32))
        grad_ref[...] = (
            inv * (gn - xhat * jnp.mean(gn * xhat, axis=1, keepdims=True))
        ).astype(BF16)


def token_grad(x, mod, back, w):
    return pl.pallas_call(
        token_kernel,
        grid=(HEADS // 2,),
        in_specs=[
            pl.BlockSpec((128, 1024), lambda i: (0, 0)),
            pl.BlockSpec((2, 1024), lambda i: (0, 0)),
            pl.BlockSpec((2, 256, 128), lambda i: (i, 0, 0)),
            pl.BlockSpec((1024, 128), lambda i: (0, i)),
            pl.BlockSpec((1024, 128), lambda i: (0, 8 + i)),
            pl.BlockSpec((1024, 128), lambda i: (0, 16 + i)),
        ],
        out_specs=[
            pl.BlockSpec((128, 128), lambda i: (0, i)),
            pl.BlockSpec((128, 1024), lambda i: (0, 0)),
            pl.BlockSpec((2, 1024), lambda i: (0, 0)),
        ],
        out_shape=[
            jax.ShapeDtypeStruct((128, 1024), BF16),
            jax.ShapeDtypeStruct((128, 1024), BF16),
            jax.ShapeDtypeStruct((2, 1024), F32),
        ],
        scratch_shapes=[pltpu.VMEM((128, 1024), F32)],
        compiler_params=pltpu.CompilerParams(dimension_semantics=("arbitrary",)),
        cost_estimate=pl.CostEstimate(
            flops=2 * 128 * 1024 * 3072, bytes_accessed=8 << 20, transcendentals=0
        ),
        name="token_grad",
    )(x, mod, back, w, w, w)


def on_device(tokens, timestep, table, w_qkv, grad_out):
    row = lax.dynamic_slice(table, (timestep[0], 0), (1, table.shape[1])).reshape(2, 1024)
    x = swap(tokens[0])
    mod = swap(row)
    g = swap(grad_out[0])
    normed, sent = project(x, g, mod, w_qkv)
    recv = plane_exchange(sent)
    normed_all = lax.all_gather(normed, "tile", axis_index_groups=PLANE, tiled=True)
    kvp = lax.ppermute(recv[:, 128:], "dp", OTHER_CORE)
    dqo, own, other = attention(recv, kvp)
    mine = lax.ppermute(other, "dp", OTHER_CORE)
    dkv = (own + mine.astype(F32)).astype(BF16)
    back = jnp.concatenate([dqo, dkv], axis=1)
    back_recv = plane_exchange(back)
    partial = weight_grad(normed_all, back)
    pieces = lax.all_to_all(
        partial.reshape(256, 4, 256), ("tile", "dp"), split_axis=0, concat_axis=0, tiled=True
    )
    attended, token_gradient, sums = token_grad(x, mod, back_recv, w_qkv)
    attended = swap(attended)
    token_gradient = swap(token_gradient)
    sums = sums + lax.ppermute(sums, "dp", OTHER_CORE)
    for bit in (2, 4, 8, 16):
        sums = sums + lax.ppermute(sums, "tile", [(t, t ^ bit) for t in range(32)])
    sums = swap(sums)
    rows = jnp.sum(pieces.astype(F32).reshape(16, 16, 4, 256), axis=1)
    rows = jnp.stack([rows[:, :, :64], rows[:, :, 128:192], rows[:, :, 192:]], axis=0)
    rows = rows.transpose(2, 0, 1, 3).reshape(4, 3072).astype(BF16)
    grad_wqkv = lax.all_gather(rows, "dp", tiled=True).astype(F32)
    return (
        attended[None],
        token_gradient[None],
        sums.reshape(1, 2048),
        grad_wqkv,
    )


def solution(mesh):
    placed = (P("dp", "tile", None), P("dp"), P(), P(), P("dp", "tile", None))
    return jax.shard_map(
        on_device,
        mesh=mesh,
        in_specs=placed,
        out_specs=(P("dp", "tile", None), P("dp", "tile", None), P("dp", None), P("tile", None)),
        check_vma=False,
    )
```

time: 893 us -> 192 us (0.22)
  waiting for transfers between devices: 582 us -> 24.3 us
  matrix products: 104 us -> 0 us
  Pallas kernels: 0 us -> 55.7 us
  blocking collectives: 77.6 us -> 34 us
  local copies, waits for them, and re-layouts: 51 us -> 9.13 us
  other arithmetic: 25.6 us -> 4.49 us
  starting transfers between devices: 34.7 us -> 48.1 us
    all_gather x1, waiting for transfers between devices: 452 us -> 0.02 us  [on_device(): lax.all_gather(normed, 'tile', axis_index_groups=PLANE, tiled=True)]
    dot_general x28 -> x0, matrix products: 104 us -> none  [the longest x4 21.8 us: step(): lax.dot_general(probs_low, g_part, (((0,), (0,)), ((), ())), preferred_el...]
    psum x1 -> x0, blocking collectives: 77.6 us -> none  [on_device(): modulation_grads = lax.psum(local_modulation, 'tile')]
    psum x1 -> x0, waiting for transfers between devices: 71.6 us -> none  [on_device(): lax.psum(partial_grad.astype(jnp.bfloat16), 'dp').astype(jnp.float32)]
    pallas_call x0 -> x4, Pallas kernels: none -> 55.7 us  [the longest x1 34.7 us: attention(): pl.pallas_call(functools.partial(attention_kernel, bq, kt), grid=(nq // b...]
    all_to_all x6 -> x2, waiting for transfers between devices: 58.6 us -> 11 us  [the longest x1 11 us: plane_exchange(): lax.all_to_all(x, 'tile', split_axis=0, concat_axis=0, tiled=True, axis_i...]
    ppermute x0 -> x13, starting transfers between devices: none -> 32.2 us  [the longest x6 24 us: swap(): return lax.ppermute(x, EVERY, SWAP)]
    dynamic_update_slice x16 -> x0, local copies, waits for them, and re-layouts: 30.1 us -> none  [head_pass(): lax.scan(step, start, (q_blocks, g_blocks))]
  transfers between devices with their start and end apart: 8 -> 16, of which waited for: 7 -> 10; matrix products, arithmetic and copies ran while one was open for 2% -> 3% of each run, Pallas kernels for 0% -> 25%
where the time goes in v1:
time: 192 us; the launch traced here: 191 us
  Pallas kernels  55.7 us (29%)
  starting transfers between devices  48.1 us (25%)
  blocking collectives  34 us (18%)
  waiting for transfers between devices  24.3 us (13%)
  between operations  14.9 us (8%)
  local copies, waits for them, and re-layouts  9.13 us (5%)
  other arithmetic  4.49 us (2%)
    pallas_call x1, Pallas kernels, attention(): pl.pallas_call(functools.partial(attention_kernel, bq, kt), grid=(nq // b...  34.7 us
    ppermute x6, starting transfers between devices, swap(): return lax.ppermute(x, EVERY, SWAP)  24 us
    all_to_all x1, blocking collectives, plane_exchange(): lax.all_to_all(x, 'tile', split_axis=0, concat_axis=0, tiled=True, axis_i...  18.7 us
    all_gather x1, blocking collectives, on_device(): grad_wqkv = lax.all_gather(rows, 'dp', tiled=True).astype(F32)  15.3 us
    all_to_all x1, starting transfers between devices, on_device(): lax.all_to_all(partial.reshape(256, 4, 256), ('tile', 'dp'), split_axis=0...  12 us
    all_to_all x1, waiting for transfers between devices, plane_exchange(): lax.all_to_all(x, 'tile', split_axis=0, concat_axis=0, tiled=True, axis_i...  11 us
    pallas_call x1, Pallas kernels, token_grad(): pl.pallas_call(token_kernel, grid=(HEADS // 2,), in_specs=[pl.BlockSpec((...  8.62 us
    pallas_call x1, Pallas kernels, project(): pl.pallas_call(project_kernel, grid=(HEADS // 2,), in_specs=[pl.BlockSpec...  8.31 us
  transfers between devices with their start and end apart: 16, of which 10 were waited for; matrix products, arithmetic and copies ran while one was open for 3% of the time, Pallas kernels for 25%

profile of v1, /device:TPU:1, one launch (start us, length us, event | category | flops | bytes accessed | tf_op | source)
XLA Modules:
  0.0 190.6 jit_solution(2688612503401783006)
XLA Ops:
  7.2 4.9 %collective-permute-start = (bf16[128,1024]{1,0:T(8,128)(2,1)}, bf16[128,1024]{1,0:T(8,128)(2,1)S(1)}, u32[]{:S(2)}, u32[]{:S(2)}) collective-permute-start(bf16[128,1024]{1,0:T(8,128)(2,1)} %bitcast.27), channel_id=1, source_target_pairs={{0,0},{1,32},{2,2},{3,34},{4,4},{5,36},{6,6},{7,38},{8,8},{9,40},{... | collective-permute-start | bytes 786440 | tf_op jit(solution)/shard_map/ppermute | solution.py:29
  12.2 1.9 %collective-permute-start.2 = (bf16[128,1024]{1,0:T(8,128)(2,1)}, bf16[128,1024]{1,0:T(8,128)(2,1)S(1)}, u32[]{:S(2)}, u32[]{:S(2)}) collective-permute-start(bf16[128,1024]{1,0:T(8,128)(2,1)} %bitcast.28), channel_id=1, source_target_pairs={{0,0},{1,32},{2,2},{3,34},{4,4},{5,36},{6,6},{7,38},{8,8},{9,40},{... | collective-permute-start | bytes 786440 | tf_op jit(solution)/shard_map/ppermute | solution.py:29
  15.5 3.6 %collective-permute-start.1 = (bf16[2,1024]{1,0:T(2,128)(2,1)S(1)}, bf16[2,1024]{1,0:T(2,128)(2,1)S(1)}, u32[]{:S(2)}, u32[]{:S(2)}) collective-permute-start(bf16[2,1024]{1,0:T(2,128)(2,1)S(1)} %reshape.25), channel_id=1, source_target_pairs={{0,0},{1,32},{2,2},{3,34},{4,4},{5,36},{6,6},{7,38},{8,8},{9,40},{... | collective-permute-start | bytes 12296 | tf_op jit(solution)/shard_map/ppermute | solution.py:29
  19.2 1.3 collective-permute-done.1.mod_ref
  21.9 8.3 %project.1 = (bf16[128,1024]{1,0:T(8,128)(2,1)}, bf16[16,256,128]{2,1,0:T(8,128)(2,1)}) custom-call(bf16[128,1024]{1,0:T(8,128)(2,1)} %copy-done.3, bf16[128,1024]{1,0:T(8,128)(2,1)} %copy-done.4, bf16[2,1024]{1,0:T(2,128)(2,1)} %copy-done.5, bf16[1024,3072]{1,0:T(8,128)(2,1)} %wv_ref.3, bf16[1024,3072]{1,0:T(8,128)(2,1)} %wv_ref.3, bf16[1024,3072]{1,0:T(8,128)(2,1)} %wv_ref.3), custom_call_target="tpu_custom_call" | custom-call | flops 805306368 | bytes 8388608 | tf_op jit(solution)/shard_map/project/pallas_call | solution.py:71
  30.2 18.7 %all_to_all.15.recv_ref = bf16[16,256,128]{2,1,0:T(8,128)(2,1)S(1)} all-to-all(bf16[16,256,128]{2,1,0:T(8,128)(2,1)} %get-tuple-element.12), channel_id=1, replica_groups={{0,2,4,6,8,10,12,14,16,18,20,22,24,26,28,30},{1,3,5,7,9,11,13,15,17,19,..., dimensions={0} | all-to-all | bytes 2097152 | tf_op jit(solution)/shard_map/all_to_all | solution.py:33
  49.0 1.9 collective-permute-done.3.kvp_ref
  51.7 34.7 %attention.1 = (bf16[16,128,128]{2,1,0:T(8,128)(2,1)}, f32[16,128,128]{2,1,0:T(8,128)}, bf16[16,128,128]{2,1,0:T(8,128)(2,1)}) custom-call(bf16[16,256,128]{2,1,0:T(8,128)(2,1)} %copy-done.2, bf16[16,128,128]{2,1,0:T(8,128)(2,1)} %copy-done.6), custom_call_target="tpu_custom_call" | custom-call | flops 25769803776 | bytes 4194304 | tf_op jit(solution)/shard_map/attention/pallas_call | solution.py:159
  86.5 2.0 %collective-permute-done.4 = bf16[16,128,128]{2,1,0:T(8,128)(2,1)S(1)} collective-permute-done((bf16[16,128,128]{2,1,0:T(8,128)(2,1)}, bf16[16,128,128]{2,1,0:T(8,128)(2,1)S(1)}, u32[]{:S(2)}, u32[]{:S(2)}) %collective-permute-start.4) | collective-permute-done | bytes 524320 | tf_op jit(solution)/shard_map/ppermute | solution.py:303
  88.5 1.4 add_convert_fusion
  89.9 2.1 %pad_maximum_fusion.back_ref = bf16[16,256,128]{2,1,0:T(8,128)(2,1)} fusion(bf16[16,128,128]{2,1,0:T(8,128)(2,1)S(1)} %add_convert_fusion, bf16[16,128,128]{2,1,0:T(8,128)(2,1)} %get-tuple-element.13), kind=kLoop, calls=%fused_computation | loop fusion | flops 2097152 | bytes 2097152 | tf_op jit(solution)/shard_map/concatenate | solution.py:305
  92.0 3.8 %all-to-all-start.1 = ((bf16[16,256,128]{2,1,0:T(8,128)(2,1)}), bf16[16,256,128]{2,1,0:T(8,128)(2,1)S(1)}, u32[]{:S(2)}, u32[]{:S(2)}) async-start(bf16[16,256,128]{2,1,0:T(8,128)(2,1)} %pad_maximum_fusion.back_ref), calls=%async_computation.1 | async-start | bytes 2097152 | tf_op jit(solution)/shard_map/all_to_all | solution.py:33
  95.9 2.2 %copy-done = bf16[2048,1024]{1,0:T(8,128)(2,1)S(1)} copy-done((bf16[2048,1024]{1,0:T(8,128)(2,1)S(1)}, bf16[2048,1024]{1,0:T(8,128)(2,1)}, u32[]{:S(2)}) %copy-start) | copy-done | bytes 4194328
  98.1 4.1 %weight_grad.1 = bf16[1024,256]{1,0:T(8,128)(2,1)S(1)} custom-call(bf16[2048,1024]{1,0:T(8,128)(2,1)S(1)} %copy-done, bf16[16,256,128]{2,1,0:T(8,128)(2,1)} %pad_maximum_fusion.back_ref), custom_call_target="tpu_custom_call" | custom-call | flops 1073741824 | bytes 6291456 | tf_op jit(solution)/shard_map/weight_grad/pallas_call | solution.py:205
  102.2 0.9 reshape.27
  103.1 11.0 %all-to-all-done.1.back_ref = bf16[16,256,128]{2,1,0:T(8,128)(2,1)S(1)} async-done(((bf16[16,256,128]{2,1,0:T(8,128)(2,1)}), bf16[16,256,128]{2,1,0:T(8,128)(2,1)S(1)}, u32[]{:S(2)}, u32[]{:S(2)}) %all-to-all-start.1) | async-done | bytes 1048608 | tf_op jit(solution)/shard_map/all_to_all | solution.py:33
  114.1 12.0 %all-to-all-start.2 = ((bf16[256,4,256]{2,1,0:T(4,128)(2,1)}), bf16[256,4,256]{2,1,0:T(4,128)(2,1)S(1)}, u32[]{:S(2)}, u32[]{:S(2)}) async-start(bf16[256,4,256]{2,1,0:T(4,128)(2,1)} %reshape.27), calls=%async_computation.2 | async-start | bytes 1048576 | tf_op jit(solution)/shard_map/all_to_all | solution.py:308
  126.1 8.6 %token_grad.1 = (bf16[128,1024]{1,0:T(8,128)(2,1)}, bf16[128,1024]{1,0:T(8,128)(2,1)}, f32[2,1024]{1,0:T(2,128)}) custom-call(bf16[128,1024]{1,0:T(8,128)(2,1)} %copy-done.3, bf16[2,1024]{1,0:T(2,128)(2,1)} %copy-done.5, bf16[16,256,128]{2,1,0:T(8,128)(2,1)} %copy-done.1, bf16[1024,3072]{1,0:T(8,128)(2,1)} %wv_ref.3, bf16[1024,3072]{1,0:T(8,128)(2,1)} %wv_ref.3, ...), custom_call_target="tpu_custom_call" | custom-call | flops 805306368 | bytes 8388608 | tf_op jit(solution)/shard_map/token_grad/pallas_call | solution.py:263
  134.8 3.7 %collective-permute-start.5 = (bf16[128,1024]{1,0:T(8,128)(2,1)}, bf16[128,1024]{1,0:T(8,128)(2,1)S(1)}, u32[]{:S(2)}, u32[]{:S(2)}) collective-permute-start(bf16[128,1024]{1,0:T(8,128)(2,1)} %get-tuple-element.16), channel_id=1, source_target_pairs={{0,0},{1,32},{2,2},{3,34},{4,4},{5,36},{6,6},{7,38},{8,8},{9,40},{... | collective-permute-start | bytes 786440 | tf_op jit(solution)/shard_map/ppermute | solution.py:29
  138.5 1.9 %collective-permute-start.6 = (bf16[128,1024]{1,0:T(8,128)(2,1)}, bf16[128,1024]{1,0:T(8,128)(2,1)S(1)}, u32[]{:S(2)}, u32[]{:S(2)}) collective-permute-start(bf16[128,1024]{1,0:T(8,128)(2,1)} %get-tuple-element.17), channel_id=1, source_target_pairs={{0,0},{1,32},{2,2},{3,34},{4,4},{5,36},{6,6},{7,38},{8,8},{9,40},{... | collective-permute-start | bytes 786440 | tf_op jit(solution)/shard_map/ppermute | solution.py:29
  140.5 1.4 collective-permute-done.7
  142.6 1.4 collective-permute-start.8
  143.9 1.4 collective-permute-done.8
  145.4 2.6 %collective-permute-start.9 = (f32[2,1024]{1,0:T(2,128)S(1)}, f32[2,1024]{1,0:T(2,128)S(1)}, u32[]{:S(2)}, u32[]{:S(2)}) collective-permute-start(f32[2,1024]{1,0:T(2,128)S(1)} %add.24), channel_id=1, source_target_pairs={{0,4},{1,5},{2,6},{3,7},{4,0},{5,1},{6,2},{7,3},{8,12},{9,13},{10,... | collective-permute-start | bytes 24584 | tf_op jit(solution)/shard_map/ppermute | solution.py:316
  148.0 1.4 collective-permute-done.9
  149.4 1.4 collective-permute-start.10
  150.7 1.1 collective-permute-done.10
  151.9 2.6 %collective-permute-start.11 = (f32[2,1024]{1,0:T(2,128)S(1)}, f32[2,1024]{1,0:T(2,128)S(1)}, u32[]{:S(2)}, u32[]{:S(2)}) collective-permute-start(f32[2,1024]{1,0:T(2,128)S(1)} %add.26), channel_id=1, source_target_pairs={{0,16},{1,17},{2,18},{3,19},{4,20},{5,21},{6,22},{7,23},{8,24},{9,... | collective-permute-start | bytes 24584 | tf_op jit(solution)/shard_map/ppermute | solution.py:316
  154.5 1.4 collective-permute-done.11
  155.9 7.9 %collective-permute-start.12 = (f32[2,1024]{1,0:T(2,128)S(1)}, f32[2,1024]{1,0:T(2,128)S(1)}, u32[]{:S(2)}, u32[]{:S(2)}) collective-permute-start(f32[2,1024]{1,0:T(2,128)S(1)} %add.27), channel_id=1, source_target_pairs={{0,0},{1,32},{2,2},{3,34},{4,4},{5,36},{6,6},{7,38},{8,8},{9,40},{... | collective-permute-start | bytes 24584 | tf_op jit(solution)/shard_map/ppermute | solution.py:29
  163.8 1.3 collective-permute-done.12
  166.2 15.3 %all-gather = bf16[8,4,3072]{2,1,0:T(4,128)(2,1)S(1)} all-gather(bf16[1,4,3072]{2,1,0:T(4,128)(2,1)S(1)} %reshape.30), channel_id=1, replica_groups=mesh['dp'=8,'tile'=32] {'dp'}, dimensions={0}, use_global_device_ids=true | all-gather | bytes 221184 | tf_op jit(solution)/shard_map/all_gather | solution.py:321
  (41 shorter events, 7.4 us)
Async XLA Ops:
  7.2 88.7 %all-gather.3.cloned.1.call-start = ((), (), s32[]{:S(2)}) async-start(), calls=%async_computation.3 | async-start | bytes 4456448 | tf_op jit(solution)/shard_map/all_gather | solution.py:300
  7.2 13.3 %collective-permute-start = (bf16[128,1024]{1,0:T(8,128)(2,1)}, bf16[128,1024]{1,0:T(8,128)(2,1)S(1)}, u32[]{:S(2)}, u32[]{:S(2)}) collective-permute-start(bf16[128,1024]{1,0:T(8,128)(2,1)} %bitcast.27), channel_id=1, source_target_pairs={{0,0},{1,32},{2,2},{3,34},{4,4},{5,36},{6,6},{7,38},{8,8},{9,40},{... | collective-permute-start | bytes 786440 | tf_op jit(solution)/shard_map/ppermute | solution.py:29
  12.2 8.3 %collective-permute-start.2 = (bf16[128,1024]{1,0:T(8,128)(2,1)}, bf16[128,1024]{1,0:T(8,128)(2,1)S(1)}, u32[]{:S(2)}, u32[]{:S(2)}) collective-permute-start(bf16[128,1024]{1,0:T(8,128)(2,1)} %bitcast.28), channel_id=1, source_target_pairs={{0,0},{1,32},{2,2},{3,34},{4,4},{5,36},{6,6},{7,38},{8,8},{9,40},{... | collective-permute-start | bytes 786440 | tf_op jit(solution)/shard_map/ppermute | solution.py:29
  15.5 4.9 %collective-permute-start.1 = (bf16[2,1024]{1,0:T(2,128)(2,1)S(1)}, bf16[2,1024]{1,0:T(2,128)(2,1)S(1)}, u32[]{:S(2)}, u32[]{:S(2)}) collective-permute-start(bf16[2,1024]{1,0:T(2,128)(2,1)S(1)} %reshape.25), channel_id=1, source_target_pairs={{0,0},{1,32},{2,2},{3,34},{4,4},{5,36},{6,6},{7,38},{8,8},{9,40},{... | collective-permute-start | bytes 12296 | tf_op jit(solution)/shard_map/ppermute | solution.py:29
  20.5 0.6 copy-start.5
  20.5 0.7 copy-start.3
  21.2 0.7 copy-start.4
  48.9 2.0 %copy-start.2 = (bf16[16,256,128]{2,1,0:T(8,128)(2,1)}, bf16[16,256,128]{2,1,0:T(8,128)(2,1)S(1)}, u32[]{:S(2)}) copy-start(bf16[16,256,128]{2,1,0:T(8,128)(2,1)S(1)} %all_to_all.15.recv_ref) | copy-start | bytes 3145732
  48.9 2.0 %collective-permute-start.3 = (bf16[16,128,128]{2,1,0:T(8,128)(2,1)S(1)}, bf16[16,128,128]{2,1,0:T(8,128)(2,1)S(1)}, u32[]{:S(2)}, u32[]{:S(2)}) collective-permute-start(bf16[16,128,128]{2,1,0:T(8,128)(2,1)S(1)} %slice.19), channel_id=1, source_target_pairs={{0,32},{32,0},{64,96},{96,64},{128,160},{160,128},{192,224},{224,1... | collective-permute-start | bytes 1572872 | tf_op jit(solution)/shard_map/ppermute | solution.py:301
  50.9 0.8 copy-start.6
  86.4 2.1 %collective-permute-start.4 = (bf16[16,128,128]{2,1,0:T(8,128)(2,1)}, bf16[16,128,128]{2,1,0:T(8,128)(2,1)S(1)}, u32[]{:S(2)}, u32[]{:S(2)}) collective-permute-start(bf16[16,128,128]{2,1,0:T(8,128)(2,1)} %get-tuple-element.15), channel_id=1, source_target_pairs={{0,32},{32,0},{64,96},{96,64},{128,160},{160,128},{192,224},{224,1... | collective-permute-start | bytes 1572872 | tf_op jit(solution)/shard_map/ppermute | solution.py:303
  92.0 22.1 %all-to-all-start.1 = ((bf16[16,256,128]{2,1,0:T(8,128)(2,1)}), bf16[16,256,128]{2,1,0:T(8,128)(2,1)S(1)}, u32[]{:S(2)}, u32[]{:S(2)}) async-start(bf16[16,256,128]{2,1,0:T(8,128)(2,1)} %pad_maximum_fusion.back_ref), calls=%async_computation.1 | async-start | bytes 2097152 | tf_op jit(solution)/shard_map/all_to_all | solution.py:33
  95.9 2.2 %copy-start = (bf16[2048,1024]{1,0:T(8,128)(2,1)S(1)}, bf16[2048,1024]{1,0:T(8,128)(2,1)}, u32[]{:S(2)}) copy-start(bf16[2048,1024]{1,0:T(8,128)(2,1)} %all-gather.3.cloned.1.call-done.normed_ref) | copy-start | bytes 12582916
  114.1 12.0 %copy-start.1 = (bf16[16,256,128]{2,1,0:T(8,128)(2,1)}, bf16[16,256,128]{2,1,0:T(8,128)(2,1)S(1)}, u32[]{:S(2)}) copy-start(bf16[16,256,128]{2,1,0:T(8,128)(2,1)S(1)} %all-to-all-done.1.back_ref) | copy-start | bytes 3145732
  114.1 51.6 %all-to-all-start.2 = ((bf16[256,4,256]{2,1,0:T(4,128)(2,1)}), bf16[256,4,256]{2,1,0:T(4,128)(2,1)S(1)}, u32[]{:S(2)}, u32[]{:S(2)}) async-start(bf16[256,4,256]{2,1,0:T(4,128)(2,1)} %reshape.27), calls=%async_computation.2 | async-start | bytes 1048576 | tf_op jit(solution)/shard_map/all_to_all | solution.py:308
  134.8 31.0 %collective-permute-start.5 = (bf16[128,1024]{1,0:T(8,128)(2,1)}, bf16[128,1024]{1,0:T(8,128)(2,1)S(1)}, u32[]{:S(2)}, u32[]{:S(2)}) collective-permute-start(bf16[128,1024]{1,0:T(8,128)(2,1)} %get-tuple-element.16), channel_id=1, source_target_pairs={{0,0},{1,32},{2,2},{3,34},{4,4},{5,36},{6,6},{7,38},{8,8},{9,40},{... | collective-permute-start | bytes 786440 | tf_op jit(solution)/shard_map/ppermute | solution.py:29
  138.5 27.3 %collective-permute-start.6 = (bf16[128,1024]{1,0:T(8,128)(2,1)}, bf16[128,1024]{1,0:T(8,128)(2,1)S(1)}, u32[]{:S(2)}, u32[]{:S(2)}) collective-permute-start(bf16[128,1024]{1,0:T(8,128)(2,1)} %get-tuple-element.17), channel_id=1, source_target_pairs={{0,0},{1,32},{2,2},{3,34},{4,4},{5,36},{6,6},{7,38},{8,8},{9,40},{... | collective-permute-start | bytes 786440 | tf_op jit(solution)/shard_map/ppermute | solution.py:29
  140.4 1.5 collective-permute-start.7
  142.6 2.8 %collective-permute-start.8 = (f32[2,1024]{1,0:T(2,128)S(1)}, f32[2,1024]{1,0:T(2,128)S(1)}, u32[]{:S(2)}, u32[]{:S(2)}) collective-permute-start(f32[2,1024]{1,0:T(2,128)S(1)} %add.23), channel_id=1, source_target_pairs={{0,2},{1,3},{2,0},{3,1},{4,6},{5,7},{6,4},{7,5},{8,10},{9,11},{10,... | collective-permute-start | bytes 24584 | tf_op jit(solution)/shard_map/ppermute | solution.py:316
  145.4 4.0 %collective-permute-start.9 = (f32[2,1024]{1,0:T(2,128)S(1)}, f32[2,1024]{1,0:T(2,128)S(1)}, u32[]{:S(2)}, u32[]{:S(2)}) collective-permute-start(f32[2,1024]{1,0:T(2,128)S(1)} %add.24), channel_id=1, source_target_pairs={{0,4},{1,5},{2,6},{3,7},{4,0},{5,1},{6,2},{7,3},{8,12},{9,13},{10,... | collective-permute-start | bytes 24584 | tf_op jit(solution)/shard_map/ppermute | solution.py:316
  149.4 2.5 %collective-permute-start.10 = (f32[2,1024]{1,0:T(2,128)S(1)}, f32[2,1024]{1,0:T(2,128)S(1)}, u32[]{:S(2)}, u32[]{:S(2)}) collective-permute-start(f32[2,1024]{1,0:T(2,128)S(1)} %add.25), channel_id=1, source_target_pairs={{0,8},{1,9},{2,10},{3,11},{4,12},{5,13},{6,14},{7,15},{8,0},{9,1},... | collective-permute-start | bytes 24584 | tf_op jit(solution)/shard_map/ppermute | solution.py:316
  151.9 4.0 %collective-permute-start.11 = (f32[2,1024]{1,0:T(2,128)S(1)}, f32[2,1024]{1,0:T(2,128)S(1)}, u32[]{:S(2)}, u32[]{:S(2)}) collective-permute-start(f32[2,1024]{1,0:T(2,128)S(1)} %add.26), channel_id=1, source_target_pairs={{0,16},{1,17},{2,18},{3,19},{4,20},{5,21},{6,22},{7,23},{8,24},{9,... | collective-permute-start | bytes 24584 | tf_op jit(solution)/shard_map/ppermute | solution.py:316
  155.9 9.3 %collective-permute-start.12 = (f32[2,1024]{1,0:T(2,128)S(1)}, f32[2,1024]{1,0:T(2,128)S(1)}, u32[]{:S(2)}, u32[]{:S(2)}) collective-permute-start(f32[2,1024]{1,0:T(2,128)S(1)} %add.27), channel_id=1, source_target_pairs={{0,0},{1,32},{2,2},{3,34},{4,4},{5,36},{6,6},{7,38},{8,8},{9,40},{... | collective-permute-start | bytes 24584 | tf_op jit(solution)/shard_map/ppermute | solution.py:29
Sparse Core Ops, SparseCore 0:
  30.3 58.5 all-gather.2

commit v2 on v1

v2 whole, which is shorter than its diff:
```python
import functools

import jax
import jax.numpy as jnp
from jax import lax
from jax.experimental import pallas as pl
from jax.experimental.pallas import tpu as pltpu
from jax.sharding import PartitionSpec as P

HEADS = 16
DEPTH = 64
WIDTH = 1024
TOK = 128
LOG2E = 1.4426950408889634
BF16 = jnp.bfloat16
F32 = jnp.float32
MIB = 1024 * 1024

SWAP = [
    ((zh * 2 + core) * 32 + yx * 2 + zl, (zh * 2 + zl) * 32 + yx * 2 + core)
    for zh in range(4)
    for core in range(2)
    for yx in range(16)
    for zl in range(2)
]
PLANE = [[yx * 2 + zl for yx in range(16)] for zl in range(2)]
OTHER_CORE = [(d, d ^ 1) for d in range(8)]


def swap(x):
    return lax.ppermute(x, ("dp", "tile"), SWAP)


def from_other_core(x):
    return lax.ppermute(x, "dp", OTHER_CORE)


def plane_exchange(x):
    return lax.all_to_all(
        x, "tile", split_axis=0, concat_axis=0, tiled=True, axis_index_groups=PLANE
    )


def dot(a, b):
    return jnp.dot(a, b, preferred_element_type=F32)


def dot_t(a, b):
    return lax.dot_general(a, b, (((1,), (1,)), ((), ())), preferred_element_type=F32)


def low_lanes(shape):
    return lax.broadcasted_iota(jnp.int32, shape, len(shape) - 1) < DEPTH


def pairs(low, a, b):
    axis = a.ndim - 1
    return jnp.where(low, a, pltpu.roll(b, DEPTH, axis)), jnp.where(
        low, pltpu.roll(a, DEPTH, axis), b
    )


def project_kernel(x_ref, g_ref, mod_ref, wq_ref, wk_ref, wv_ref, copies_ref, out_ref, normed_ref, xhat_ref):
    @pl.when(pl.program_id(0) == 0)
    def _():
        x = x_ref[...].astype(F32)
        inv = 1.0 / jnp.sqrt(jnp.mean(x * x, axis=1, keepdims=True) + 1e-06)
        mod = mod_ref[...].astype(F32)
        xhat = x * inv
        xhat_ref[...] = xhat.astype(BF16)
        normed_ref[...] = (xhat * (1.0 + mod[0:1]) + mod[1:2]).astype(BF16)

    normed = normed_ref[...]
    for c in range(copies_ref.shape[0]):
        copies_ref[c] = xhat_ref[...]
    q4 = dot(normed, wq_ref[...]).astype(BF16).astype(F32)
    k4 = dot(normed, wk_ref[...]).astype(BF16).astype(F32)
    v4 = dot(normed, wv_ref[...]).astype(BF16).astype(F32)
    g4 = g_ref[...].astype(F32)
    low = low_lanes((TOK, 128))
    for p in range(2):
        lanes = slice(p * 128, (p + 1) * 128)
        for rows, a, b in ((slice(0, TOK), q4, g4), (slice(TOK, 2 * TOK), k4, v4)):
            first, second = pairs(low, a[:, lanes], b[:, lanes])
            out_ref[2 * p, rows] = first.astype(BF16)
            out_ref[2 * p + 1, rows] = second.astype(BF16)


def weight_specs():
    return [pl.BlockSpec((WIDTH, 256), lambda i, c=c: (0, 4 * c + i)) for c in range(3)]


def project(packed, w):
    return pl.pallas_call(
        project_kernel,
        grid=(4,),
        in_specs=[
            pl.BlockSpec((TOK, WIDTH), lambda i: (0, 0)),
            pl.BlockSpec((TOK, 256), lambda i: (1, i)),
            pl.BlockSpec((16, WIDTH), lambda i: (16, 0)),
        ]
        + weight_specs(),
        out_specs=[
            pl.BlockSpec((4, TOK, WIDTH), lambda i: (i, 0, 0)),
            pl.BlockSpec((4, 2 * TOK, 128), lambda i: (i, 0, 0)),
        ],
        out_shape=[
            jax.ShapeDtypeStruct((HEADS, TOK, WIDTH), BF16),
            jax.ShapeDtypeStruct((HEADS, 2 * TOK, 128), BF16),
        ],
        scratch_shapes=[pltpu.VMEM((TOK, WIDTH), BF16)] * 2,
        compiler_params=pltpu.CompilerParams(
            vmem_limit_bytes=60 * MIB, dimension_semantics=("arbitrary",)
        ),
        cost_estimate=pl.CostEstimate(
            flops=2 * TOK * WIDTH * 3 * WIDTH, bytes_accessed=12 * MIB, transcendentals=0
        ),
        name="project",
    )(packed, packed, packed, w, w, w)


def attention_kernel(
    bq, kt, recv_ref, kvp_ref, back_ref, own_ref, other_ref, kv, kvt, acc, s_scr, dp_scr, pb_scr
):
    i = pl.program_id(0)
    nk = kv.shape[0]
    half = nk // 2
    tiles = [pl.ds(t * kt, kt) for t in range(nk // kt)]

    @pl.when(i == 0)
    def _():
        kv[:half] = recv_ref[:, 128:, :].reshape(half, 128)
        kv[half:] = kvp_ref[...].reshape(half, 128)
        acc[...] = jnp.zeros_like(acc)
        for t in tiles:
            kvt[:, t] = kv[t].T

    srcs = bq // 128
    qg = recv_ref[pl.ds(i * srcs, srcs), :128, :].reshape(bq, 128)
    low = low_lanes(qg.shape)
    zero = jnp.zeros_like(qg)
    q0 = jnp.where(low, qg * jnp.asarray(0.125, BF16), zero)
    g0 = jnp.where(low, zero, qg)
    q0t = q0.T
    g0t = g0.T
    top = jnp.full((8, bq), -jnp.inf, F32)
    for t in tiles:
        s = dot(kv[t], q0t)
        s_scr[t] = s
        top = jnp.maximum(top, jnp.max(s.reshape(kt // 8, 8, bq), axis=0))
    top = jnp.max(top, axis=0, keepdims=True)
    total = jnp.zeros((8, bq), F32)
    for t in tiles:
        e = jnp.exp2((s_scr[t] - top) * LOG2E)
        s_scr[t] = e
        total = total + jnp.sum(e.reshape(kt // 8, 8, bq), axis=0)
        dp_scr[t] = dot(kv[t], g0t)
    inv = 1.0 / jnp.sum(total, axis=0, keepdims=True)
    o_t = jnp.zeros((DEPTH, bq), F32)
    for t in tiles:
        pb = (s_scr[t] * inv).astype(BF16)
        pb_scr[t] = pb
        o_t = o_t + dot(kvt[DEPTH:, t], pb)
    delta = jnp.sum(o_t * g0t[DEPTH:].astype(F32), axis=0, keepdims=True)
    dq_t = jnp.zeros((DEPTH, bq), F32)
    for t in tiles:
        ds = ((s_scr[t] * inv) * (dp_scr[t] - delta)).astype(BF16)
        dq_t = dq_t + dot(kvt[:DEPTH, t], ds)
        acc[t] += dot(ds, q0) + dot(pb_scr[t], g0)
    dqo = jnp.concatenate([dq_t * 0.125, o_t], axis=0).T.astype(BF16)
    back_ref[:, :128] = dqo.reshape(srcs, 128, 128)

    @pl.when(i == pl.num_programs(0) - 1)
    def _():
        own_ref[...] = acc[:half].reshape(16, 128, 128)
        other_ref[...] = acc[half:].astype(BF16).reshape(16, 128, 128)


def attention(recv, kvp, bq=512, kt=256):
    nq, nk = 2048, 4096
    srcs = bq // 128
    whole = lambda i: (0, 0, 0)
    return pl.pallas_call(
        functools.partial(attention_kernel, bq, kt),
        grid=(nq // bq,),
        in_specs=[
            pl.BlockSpec((16, 256, 128), whole),
            pl.BlockSpec((16, 128, 128), whole),
        ],
        out_specs=[
            pl.BlockSpec((srcs, 256, 128), lambda i: (i, 0, 0)),
            pl.BlockSpec((16, 128, 128), whole),
            pl.BlockSpec((16, 128, 128), whole),
        ],
        out_shape=[
            jax.ShapeDtypeStruct((16, 256, 128), BF16),
            jax.ShapeDtypeStruct((16, 128, 128), F32),
            jax.ShapeDtypeStruct((16, 128, 128), BF16),
        ],
        scratch_shapes=[
            pltpu.VMEM((nk, 128), BF16),
            pltpu.VMEM((128, nk), BF16),
            pltpu.VMEM((nk, 128), F32),
            pltpu.VMEM((nk, bq), F32),
            pltpu.VMEM((nk, bq), F32),
            pltpu.VMEM((nk, bq), BF16),
        ],
        compiler_params=pltpu.CompilerParams(
            vmem_limit_bytes=48 * MIB, dimension_semantics=("arbitrary",)
        ),
        cost_estimate=pl.CostEstimate(
            flops=6 * 2 * nq * nk * 256, bytes_accessed=4 << 20, transcendentals=nq * nk
        ),
        name="attention",
    )(recv, kvp)


def combine_kernel(back_ref, own_ref, mine_ref, out_ref):
    out_ref[...] = (own_ref[...] + mine_ref[...].astype(F32)).astype(BF16)


def combine(back, own, mine):
    half = pl.BlockSpec((16, 128, 128), lambda i: (0, 0, 0))
    return pl.pallas_call(
        combine_kernel,
        grid=(1,),
        in_specs=[pl.BlockSpec(memory_space=pl.ANY), half, half],
        out_specs=pl.BlockSpec((16, 128, 128), lambda i: (0, 1, 0)),
        out_shape=jax.ShapeDtypeStruct((16, 256, 128), BF16),
        input_output_aliases={0: 0},
        compiler_params=pltpu.CompilerParams(vmem_limit_bytes=32 * MIB),
        cost_estimate=pl.CostEstimate(flops=1 << 18, bytes_accessed=2 * MIB, transcendentals=0),
        name="combine",
    )(back, own, mine)


def weight_kernel(
    place_ref, xhat_ref, back_ref, mod_ref, wq_ref, wk_ref, wv_ref, keep_ref, send_ref, sums_ref, back_t
):
    @pl.when(pl.program_id(0) == 0)
    def _():
        for s in range(16):
            tokens = slice(s * TOK, (s + 1) * TOK)
            back_t[:128, tokens] = back_ref[s, :TOK].T
            back_t[128:, tokens] = back_ref[s, TOK:].T

    lhs = back_t[...]
    grad_t = dot(lhs, xhat_ref[...])
    column = jnp.sum(lhs.astype(F32), axis=1, keepdims=True)
    odd = place_ref[1] == 1
    scale_sum = jnp.zeros((1, 256), F32)
    shift_sum = jnp.zeros((1, 256), F32)
    for w_ref, first in ((wq_ref, 0), (wk_ref, 128), (wv_ref, 192)):
        w_t = w_ref[...].astype(F32).T
        w_t = jnp.where(odd, w_t[DEPTH:], w_t[:DEPTH])
        rows = slice(first, first + DEPTH)
        scale_sum = scale_sum + jnp.sum(w_t * grad_t[rows], axis=0, keepdims=True)
        shift_sum = shift_sum + jnp.sum(w_t * column[rows], axis=0, keepdims=True)
    sums_ref[0:1] = scale_sum
    sums_ref[1:2] = shift_sum
    mod = mod_ref[...].astype(F32)
    grad = (grad_t * (1.0 + mod[0:1]) + column * mod[1:2]).T
    low = low_lanes((256, 128))
    dq_dk, dv = pairs(low, grad[:, :128], grad[:, 128:])
    dv = dv.reshape(8, 2, 2, 8, 128)
    low = low_lanes((8, 2, 8, 128))
    dv = jnp.where(low, pltpu.roll(dv[:, :, 0], DEPTH, 3), dv[:, :, 1])
    dq_dk = dq_dk.reshape(8, 2, 16, 128)

    def put(ref, half):
        ref[:, :16] = dq_dk[:, half]
        ref[:, 16:] = dv[:, half]

    @pl.when(place_ref[0] == 0)
    def _():
        put(keep_ref, 0)
        put(send_ref, 1)

    @pl.when(place_ref[0] == 1)
    def _():
        put(keep_ref, 1)
        put(send_ref, 0)


def weight_grad(place, xhat, back, packed, w):
    rows = pl.BlockSpec((8, 24, 128), lambda i, place: (i, 0, 0))
    return pl.pallas_call(
        weight_kernel,
        grid_spec=pltpu.PrefetchScalarGridSpec(
            num_scalar_prefetch=1,
            grid=(4,),
            in_specs=[
                pl.BlockSpec((2048, 256), lambda i, place: (0, i)),
                pl.BlockSpec((16, 256, 128), lambda i, place: (0, 0, 0)),
                pl.BlockSpec((16, 256), lambda i, place: (16, i)),
            ]
            + [pl.BlockSpec((256, 128), lambda i, place, c=c: (i, 8 * c + place[2])) for c in range(3)],
            out_specs=[rows, rows, pl.BlockSpec((2, 256), lambda i, place: (0, i))],
            scratch_shapes=[pltpu.VMEM((256, 2048), BF16)],
        ),
        out_shape=[jax.ShapeDtypeStruct((32, 24, 128), F32)] * 2
        + [jax.ShapeDtypeStruct((2, WIDTH), F32)],
        compiler_params=pltpu.CompilerParams(
            vmem_limit_bytes=60 * MIB, dimension_semantics=("arbitrary",)
        ),
        cost_estimate=pl.CostEstimate(
            flops=2 * 2048 * WIDTH * 256, bytes_accessed=6 * MIB, transcendentals=0
        ),
        name="weight_grad",
    )(place, xhat, back, packed, w, w, w)


def pack_kernel(keep_ref, got_ref, sums_ref, out_ref):
    sums = jnp.concatenate(
        [sums_ref[c : c + 1, j * 128 : (j + 1) * 128] for c in range(2) for j in range(8)], axis=0
    )
    high = sums.astype(BF16).astype(F32)
    low = sums - high
    for t in range(32):
        piece = keep_ref[t] + got_ref[t]
        out_ref[t] = jnp.concatenate([piece[:16], high, low, piece[16:]], axis=0).astype(BF16)


def pack(keep, got, sums):
    return pl.pallas_call(
        pack_kernel,
        out_shape=jax.ShapeDtypeStruct((32, 56, 128), BF16),
        cost_estimate=pl.CostEstimate(flops=1 << 18, bytes_accessed=MIB, transcendentals=0),
        name="pack",
    )(keep, got, sums)


def collect_kernel(place_ref, pieces_ref, rows_ref, send_ref, keep_ref, other_ref):
    low = low_lanes((16, 128))
    half = low_lanes((8, 128))
    sums = [jnp.zeros((16, 128), F32)] * 2
    for pair in range(HEADS // 2):
        heads = []
        for head in (2 * pair, 2 * pair + 1):
            first = pieces_ref[2 * head].astype(F32)
            second = pieces_ref[2 * head + 1].astype(F32)
            heads.append(first + second)
            for z, part in enumerate((first, second)):
                sums[z] = sums[z] + (part[16:32] + part[32:48])
        dq, dk = pairs(low, heads[0][:16], heads[1][:16])
        dv = jnp.concatenate(pairs(half, heads[0][48:], heads[1][48:]), axis=0)
        for c, part in enumerate((dq, dk, dv)):
            lanes = slice(c * WIDTH + pair * 128, c * WIDTH + (pair + 1) * 128)
            rows_ref[:, lanes] = part
            send_ref[:, lanes] = part.astype(BF16)
    core = place_ref[0] == 0
    keep = jnp.where(core, sums[0], sums[1])
    other = jnp.where(core, sums[1], sums[0])
    for r in range(16):
        keep_ref[:, r * 128 : (r + 1) * 128] = keep[r : r + 1]
        other_ref[:, r * 128 : (r + 1) * 128] = other[r : r + 1]


def collect(place, pieces):
    return pl.pallas_call(
        collect_kernel,
        grid_spec=pltpu.PrefetchScalarGridSpec(
            num_scalar_prefetch=1,
            grid=(1,),
            in_specs=[pl.BlockSpec((32, 56, 128), lambda i, core: (0, 0, 0))],
            out_specs=[
                pl.BlockSpec((16, 3 * WIDTH), lambda i, core: (0, 0)),
                pl.BlockSpec((16, 3 * WIDTH), lambda i, core: (0, 0)),
                pl.BlockSpec((1, 2 * WIDTH), lambda i, core: (0, 0)),
                pl.BlockSpec((1, 2 * WIDTH), lambda i, core: (0, 0)),
            ],
        ),
        out_shape=[
            jax.ShapeDtypeStruct((16, 3 * WIDTH), F32),
            jax.ShapeDtypeStruct((16, 3 * WIDTH), BF16),
            jax.ShapeDtypeStruct((1, 2 * WIDTH), F32),
            jax.ShapeDtypeStruct((1, 2 * WIDTH), F32),
        ],
        cost_estimate=pl.CostEstimate(flops=1 << 20, bytes_accessed=MIB, transcendentals=0),
        name="collect",
    )(place, pieces)


def token_kernel(x_ref, mod_ref, back_ref, wq_ref, wk_ref, wv_ref, out_ref, acc):
    i = pl.program_id(0)
    low = low_lanes((TOK, 128))
    dq, dk, dv = [], [], []
    for p in range(2):
        a = back_ref[2 * p].astype(F32)
        b = back_ref[2 * p + 1].astype(F32)
        dq_pair, attended = pairs(low, a[:TOK], b[:TOK])
        dk_pair, dv_pair = pairs(low, a[TOK:], b[TOK:])
        lanes = pl.ds(pl.multiple_of(i * 256 + p * 128, 128), 128)
        out_ref[0, :, lanes] = attended.astype(BF16)
        dq.append(dq_pair.astype(BF16))
        dk.append(dk_pair.astype(BF16))
        dv.append(dv_pair.astype(BF16))
    part = (
        dot_t(jnp.concatenate(dq, axis=1), wq_ref[...])
        + dot_t(jnp.concatenate(dk, axis=1), wk_ref[...])
        + dot_t(jnp.concatenate(dv, axis=1), wv_ref[...])
    )

    @pl.when(i == 0)
    def _():
        acc[...] = part

    @pl.when(i > 0)
    def _():
        acc[...] += part

    @pl.when(i == pl.num_programs(0) - 1)
    def _():
        x = x_ref[...].astype(F32)
        inv = 1.0 / jnp.sqrt(jnp.mean(x * x, axis=1, keepdims=True) + 1e-06)
        xhat = x * inv
        dn = acc[...]
        gn = dn * (1.0 + mod_ref[0:1].astype(F32))
        out_ref[1] = (
            inv * (gn - xhat * jnp.mean(gn * xhat, axis=1, keepdims=True))
        ).astype(BF16)


def token_grad(packed, back, w):
    return pl.pallas_call(
        token_kernel,
        grid=(4,),
        in_specs=[
            pl.BlockSpec((TOK, WIDTH), lambda i: (0, 0)),
            pl.BlockSpec((16, WIDTH), lambda i: (16, 0)),
            pl.BlockSpec((4, 2 * TOK, 128), lambda i: (i, 0, 0)),
        ]
        + weight_specs(),
        out_specs=pl.BlockSpec((2, TOK, WIDTH), lambda i: (0, 0, 0)),
        out_shape=jax.ShapeDtypeStruct((2, TOK, WIDTH), BF16),
        scratch_shapes=[pltpu.VMEM((TOK, WIDTH), F32)],
        compiler_params=pltpu.CompilerParams(
            vmem_limit_bytes=60 * MIB, dimension_semantics=("arbitrary",)
        ),
        cost_estimate=pl.CostEstimate(
            flops=2 * TOK * WIDTH * 3 * WIDTH, bytes_accessed=8 * MIB, transcendentals=0
        ),
        name="token_grad",
    )(packed, packed, back, w, w, w)


def on_device(tokens, timestep, table, w_qkv, grad_out):
    core = lax.axis_index("dp") % 2
    head = lax.axis_index("tile") // 2
    place = jnp.stack([core, head % 2, head // 2]).astype(jnp.int32)
    row = lax.dynamic_slice(table, (timestep[0], 0), (1, 2 * WIDTH)).reshape(2, WIDTH)
    packed = swap(
        jnp.concatenate([tokens[0], grad_out[0], row, jnp.zeros((14, WIDTH), BF16)], axis=0)
    )
    copies, sent = project(packed, w_qkv)
    recv = plane_exchange(sent)
    copies, recv = lax.optimization_barrier((copies, recv))
    kvp = from_other_core(recv[:, TOK:])
    xhat = plane_exchange(copies).reshape(16 * TOK, WIDTH)
    back, own, other = attention(recv, kvp)
    back = combine(back, own, from_other_core(other))
    back_recv = plane_exchange(back)
    keep, send, sums = weight_grad(place, xhat, back, packed, w_qkv)
    packed_grads = pack(keep, from_other_core(send), sums)
    packed_grads, back_recv = lax.optimization_barrier((packed_grads, back_recv))
    pieces = lax.all_to_all(packed_grads, "tile", split_axis=0, concat_axis=0, tiled=True)
    out = token_grad(packed, back_recv, w_qkv)
    pieces, out = lax.optimization_barrier((pieces, out))
    out = swap(out)
    rows, rows_low, modulation, modulation_other = collect(place, pieces)
    modulation = modulation + from_other_core(modulation_other)
    for k in (2, 4, 6):
        rows = rows + lax.ppermute(rows_low, "dp", [(d, d ^ k) for d in range(8)]).astype(F32)
    rows, out = lax.optimization_barrier((rows, out))
    other_rows = from_other_core(rows)
    grad_wqkv = jnp.concatenate(
        [jnp.where(core == 0, rows, other_rows), jnp.where(core == 0, other_rows, rows)], axis=0
    )
    return (out[0][None], out[1][None], modulation, grad_wqkv)


def solution(mesh):
    placed = (P("dp", "tile", None), P("dp"), P(), P(), P("dp", "tile", None))
    return jax.shard_map(
        on_device,
        mesh=mesh,
        in_specs=placed,
        out_specs=(P("dp", "tile", None), P("dp", "tile", None), P("dp", None), P("tile", None)),
        check_vma=False,
    )
```

time: 192 us -> 160 us (0.83)
  starting transfers between devices: 48.1 us -> 32.6 us
  blocking collectives: 34 us -> 18.6 us
  waiting for transfers between devices: 24.3 us -> 39.5 us
  between operations: 14.9 us -> 1.44 us
  local copies, waits for them, and re-layouts: 9.13 us -> 4.07 us
  Pallas kernels: 55.7 us -> 58.4 us
    all_gather x1 -> x0, blocking collectives: 15.3 us -> none  [on_device(): grad_wqkv = lax.all_gather(rows, 'dp', tiled=True).astype(F32)]
    ppermute x13 -> x10, starting transfers between devices: 32.2 us -> 17.6 us  [the longest x3 8.13 us: on_device(): lax.ppermute(rows_low, 'dp', [(d, d ^ k) for d in range(8)]).astype(F32)]
    ppermute x13 -> x10, waiting for transfers between devices: 13.3 us -> 20.6 us  [the longest x2 12.7 us: swap(): return lax.ppermute(x, ('dp', 'tile'), SWAP)]
    all_to_all x1, starting transfers between devices: 12 us -> 6.66 us  [on_device(): lax.all_to_all(packed_grads, 'tile', split_axis=0, concat_axis=0, tiled=T...]
    pallas_call x3 -> x6, Pallas kernels: 21 us -> 25.6 us  [the longest x1 6.92 us: weight_grad(): pl.pallas_call(weight_kernel, grid_spec=pltpu.PrefetchScalarGridSpec(num_...]
    all_to_all x1 -> x2, starting transfers between devices: 3.83 us -> 8.37 us  [plane_exchange(): lax.all_to_all(x, 'tile', split_axis=0, concat_axis=0, tiled=True, axis_i...]
    unnamed x18 -> x8, local copies, waits for them, and re-layouts: 6.5 us -> 2.32 us
    all_to_all x1, waiting for transfers between devices: 0.01 us -> 4.04 us  [on_device(): lax.all_to_all(packed_grads, 'tile', split_axis=0, concat_axis=0, tiled=T...]
  transfers between devices with their start and end apart: 16 -> 13, of which waited for: 10 -> 11; matrix products, arithmetic and copies ran while one was open for 3% -> 2% of each run, Pallas kernels for 25% -> 31%
where the time goes in v2:
time: 160 us
  Pallas kernels  58.4 us (36%)
  waiting for transfers between devices  39.5 us (25%)
  starting transfers between devices  32.6 us (20%)
  blocking collectives  18.6 us (12%)
  other arithmetic  4.91 us (3%)
  local copies, waits for them, and re-layouts  4.07 us (3%)
    pallas_call x1, Pallas kernels, attention(): pl.pallas_call(functools.partial(attention_kernel, bq, kt), grid=(nq // b...  32.8 us
    all_to_all x1, blocking collectives, plane_exchange(): lax.all_to_all(x, 'tile', split_axis=0, concat_axis=0, tiled=True, axis_i...  18.6 us
    all_to_all x2, waiting for transfers between devices, plane_exchange(): lax.all_to_all(x, 'tile', split_axis=0, concat_axis=0, tiled=True, axis_i...  14.8 us
    ppermute x2, waiting for transfers between devices, swap(): return lax.ppermute(x, ('dp', 'tile'), SWAP)  12.7 us
    all_to_all x2, starting transfers between devices, plane_exchange(): lax.all_to_all(x, 'tile', split_axis=0, concat_axis=0, tiled=True, axis_i...  8.37 us
    ppermute x3, starting transfers between devices, on_device(): lax.ppermute(rows_low, 'dp', [(d, d ^ k) for d in range(8)]).astype(F32)  8.13 us
    ppermute x2, starting transfers between devices, swap(): return lax.ppermute(x, ('dp', 'tile'), SWAP)  7.05 us
    pallas_call x1, Pallas kernels, weight_grad(): pl.pallas_call(weight_kernel, grid_spec=pltpu.PrefetchScalarGridSpec(num_...  6.92 us
  transfers between devices with their start and end apart: 13, of which 11 were waited for; matrix products, arithmetic and copies ran while one was open for 2% of the time, Pallas kernels for 31%

profile of v2, /device:TPU:1, one launch (start us, length us, event | category | flops | bytes accessed | tf_op | source)
XLA Modules:
  0.0 159.6 jit_solution(6766905051514394794)
XLA Ops:
  1.3 0.8 dynamic-slice_reduce_fusion
  2.2 1.2 maximum_maximum_fusion
  3.4 4.9 %collective-permute-start = (bf16[272,1024]{1,0:T(8,128)(2,1)S(1)}, bf16[272,1024]{1,0:T(8,128)(2,1)S(1)}, u32[]{:S(2)}, u32[]{:S(2)}) collective-permute-start(bf16[272,1024]{1,0:T(8,128)(2,1)S(1)} %maximum_maximum_fusion), channel_id=1, source_target_pairs={{0,0},{1,32},{2,2},{3,34},{4,4},{5,36},{6,6},{7,38},{8,8},{9,40},{... | collective-permute-start | bytes 1671176 | tf_op jit(solution)/shard_map/ppermute | solution.py:31
  8.3 7.2 %collective-permute-done.x_ref.g_ref.mod_ref = bf16[272,1024]{1,0:T(8,128)(2,1)S(1)} collective-permute-done((bf16[272,1024]{1,0:T(8,128)(2,1)S(1)}, bf16[272,1024]{1,0:T(8,128)(2,1)S(1)}, u32[]{:S(2)}, u32[]{:S(2)}) %collective-permute-start) | collective-permute-done | bytes 557088 | tf_op jit(solution)/shard_map/ppermute | solution.py:31
  15.5 0.8 copy-done
  16.3 6.8 %project.1 = (bf16[16,128,1024]{2,1,0:T(8,128)(2,1)}, bf16[16,256,128]{2,1,0:T(8,128)(2,1)}) custom-call(bf16[272,1024]{1,0:T(8,128)(2,1)} %copy-done, bf16[272,1024]{1,0:T(8,128)(2,1)} %copy-done, bf16[272,1024]{1,0:T(8,128)(2,1)} %copy-done, bf16[1024,3072]{1,0:T(8,128)(2,1)} %wv_ref.5, bf16[1024,3072]{1,0:T(8,128)(2,1)} %wv_ref.5, bf16[1024,3072]{1,0:T(8,128)(2,1)} %wv_ref.5), custom_call_target="tpu_custom_call" | custom-call | flops 805306368 | bytes 12582912 | tf_op jit(solution)/shard_map/project/pallas_call | solution.py:94
  23.1 18.6 %all_to_all.20.recv_ref = bf16[16,256,128]{2,1,0:T(8,128)(2,1)S(1)} all-to-all(bf16[16,256,128]{2,1,0:T(8,128)(2,1)} %get-tuple-element.25), channel_id=1, replica_groups={{0,2,4,6,8,10,12,14,16,18,20,22,24,26,28,30},{1,3,5,7,9,11,13,15,17,19,..., dimensions={0} | all-to-all | bytes 2097152 | tf_op jit(solution)/shard_map/all_to_all | solution.py:39
  41.7 4.5 %all-to-all-start.1 = ((bf16[16,128,1024]{2,1,0:T(8,128)(2,1)}), bf16[16,128,1024]{2,1,0:T(8,128)(2,1)}, u32[]{:S(2)}, u32[]{:S(2)}) async-start(bf16[16,128,1024]{2,1,0:T(8,128)(2,1)} %get-tuple-element.26), calls=%async_computation.1 | async-start | bytes 8388608 | tf_op jit(solution)/shard_map/all_to_all | solution.py:39
  46.4 1.9 %collective-permute-done.1.kvp_ref = bf16[16,128,128]{2,1,0:T(8,128)(2,1)S(1)} collective-permute-done((bf16[16,128,128]{2,1,0:T(8,128)(2,1)S(1)}, bf16[16,128,128]{2,1,0:T(8,128)(2,1)S(1)}, u32[]{:S(2)}, u32[]{:S(2)}) %collective-permute-start.1) | collective-permute-done | bytes 524320 | tf_op jit(solution)/shard_map/ppermute | solution.py:35
  48.3 32.8 %attention.1 = (bf16[16,256,128]{2,1,0:T(8,128)(2,1)}, f32[16,128,128]{2,1,0:T(8,128)S(1)}, bf16[16,128,128]{2,1,0:T(8,128)(2,1)S(1)}) custom-call(bf16[16,256,128]{2,1,0:T(8,128)(2,1)S(1)} %all_to_all.20.recv_ref, bf16[16,128,128]{2,1,0:T(8,128)(2,1)S(1)} %collective-permute-done.1.kvp_ref), custom_call_target="tpu_custom_call" | custom-call | flops 25769803776 | bytes 4194304 | tf_op jit(solution)/shard_map/attention/pallas_call | solution.py:183
  81.2 1.8 %collective-permute-done.2.mine_ref = bf16[16,128,128]{2,1,0:T(8,128)(2,1)S(1)} collective-permute-done((bf16[16,128,128]{2,1,0:T(8,128)(2,1)S(1)}, bf16[16,128,128]{2,1,0:T(8,128)(2,1)S(1)}, u32[]{:S(2)}, u32[]{:S(2)}) %collective-permute-start.2) | collective-permute-done | bytes 524320 | tf_op jit(solution)/shard_map/ppermute | solution.py:35
  83.0 0.9 combine.1.back_ref
  83.9 10.3 %all-to-all-done.1 = bf16[16,128,1024]{2,1,0:T(8,128)(2,1)} async-done(((bf16[16,128,1024]{2,1,0:T(8,128)(2,1)}), bf16[16,128,1024]{2,1,0:T(8,128)(2,1)}, u32[]{:S(2)}, u32[]{:S(2)}) %all-to-all-start.1) | async-done | bytes 4194336 | tf_op jit(solution)/shard_map/all_to_all | solution.py:39
  94.2 3.8 %all-to-all-start.2 = ((bf16[16,256,128]{2,1,0:T(8,128)(2,1)}), bf16[16,256,128]{2,1,0:T(8,128)(2,1)S(1)}, u32[]{:S(2)}, u32[]{:S(2)}) async-start(bf16[16,256,128]{2,1,0:T(8,128)(2,1)} %combine.1.back_ref), calls=%async_computation.2 | async-start | bytes 2097152 | tf_op jit(solution)/shard_map/all_to_all | solution.py:39
  98.7 6.9 %weight_grad.1 = (f32[32,24,128]{2,1,0:T(8,128)}, f32[32,24,128]{2,1,0:T(8,128)}, f32[2,1024]{1,0:T(2,128)}) custom-call(s32[3]{0:T(128)} %pad_add_fusion.place_ref, bf16[2048,1024]{1,0:T(8,128)(2,1)} %bitcast.6.xhat_ref, bf16[16,256,128]{2,1,0:T(8,128)(2,1)} %combine.1.back_ref, bf16[272,1024]{1,0:T(8,128)(2,1)} %copy-done, bf16[1024,3072]{1,0:T(8,128)(2,1)} %wv_ref.5, ...), custom_call_target="tpu_custom_call" | custom-call | flops 1073741824 | bytes 6291456 | tf_op jit(solution)/shard_map/weight_grad/pallas_call | solution.py:287
  105.6 1.9 %collective-permute-done.3.got_ref = f32[32,24,128]{2,1,0:T(8,128)S(1)} collective-permute-done((f32[32,24,128]{2,1,0:T(8,128)}, f32[32,24,128]{2,1,0:T(8,128)S(1)}, u32[]{:S(2)}, u32[]{:S(2)}) %collective-permute-start.3) | collective-permute-done | bytes 393248 | tf_op jit(solution)/shard_map/ppermute | solution.py:35
  108.3 2.0 %pack.1 = bf16[32,56,128]{2,1,0:T(8,128)(2,1)} custom-call(f32[32,24,128]{2,1,0:T(8,128)} %get-tuple-element.31.keep_ref, f32[32,24,128]{2,1,0:T(8,128)} %copy-done.3, f32[2,1024]{1,0:T(2,128)} %get-tuple-element.33.sums_ref), custom_call_target="tpu_custom_call" | custom-call | flops 262144 | bytes 1048576 | tf_op jit(solution)/shard_map/pack/pallas_call | solution.py:325
  110.3 4.6 %all-to-all-done.2.back_ref = bf16[16,256,128]{2,1,0:T(8,128)(2,1)S(1)} async-done(((bf16[16,256,128]{2,1,0:T(8,128)(2,1)}), bf16[16,256,128]{2,1,0:T(8,128)(2,1)S(1)}, u32[]{:S(2)}, u32[]{:S(2)}) %all-to-all-start.2) | async-done | bytes 1048608 | tf_op jit(solution)/shard_map/all_to_all | solution.py:39
  114.8 6.7 %all-to-all-start.3 = ((bf16[32,56,128]{2,1,0:T(8,128)(2,1)}), bf16[32,56,128]{2,1,0:T(8,128)(2,1)S(1)}, u32[]{:S(2)}, u32[]{:S(2)}) async-start(bf16[32,56,128]{2,1,0:T(8,128)(2,1)} %pack.1), calls=%async_computation.3 | async-start | bytes 917504 | tf_op jit(solution)/shard_map/all_to_all | solution.py:466
  121.5 6.5 %token_grad.1 = bf16[2,128,1024]{2,1,0:T(8,128)(2,1)} custom-call(bf16[272,1024]{1,0:T(8,128)(2,1)} %copy-done, bf16[272,1024]{1,0:T(8,128)(2,1)} %copy-done, bf16[16,256,128]{2,1,0:T(8,128)(2,1)} %copy-done.1, bf16[1024,3072]{1,0:T(8,128)(2,1)} %wv_ref.5, bf16[1024,3072]{1,0:T(8,128)(2,1)} %wv_ref.5, bf16[1024,3072]{1,0:T(8,128)(2,1)} %wv_ref.5), custom_call_target="tpu_custom_call" | custom-call | flops 805306368 | bytes 8388608 | tf_op jit(solution)/shard_map/token_grad/pallas_call | solution.py:425
  128.0 4.0 %all-to-all-done.3.pieces_ref = bf16[32,56,128]{2,1,0:T(8,128)(2,1)S(1)} async-done(((bf16[32,56,128]{2,1,0:T(8,128)(2,1)}), bf16[32,56,128]{2,1,0:T(8,128)(2,1)S(1)}, u32[]{:S(2)}, u32[]{:S(2)}) %all-to-all-start.3) | async-done | bytes 458784 | tf_op jit(solution)/shard_map/all_to_all | solution.py:466
  132.8 2.5 %collect.1 = (f32[16,3072]{1,0:T(8,128)}, bf16[16,3072]{1,0:T(8,128)(2,1)}, f32[1,2048]{1,0:T(1,128)}, f32[1,2048]{1,0:T(1,128)}) custom-call(s32[3]{0:T(128)} %pad_add_fusion.place_ref, bf16[32,56,128]{2,1,0:T(8,128)(2,1)} %copy-done.2), custom_call_target="tpu_custom_call" | custom-call | flops 1048576 | bytes 1048576 | tf_op jit(solution)/shard_map/collect/pallas_call | solution.py:360
  135.3 6.0 %collective-permute-start.6 = (bf16[16,3072]{1,0:T(8,128)(2,1)}, bf16[16,3072]{1,0:T(8,128)(2,1)S(1)}, u32[]{:S(2)}, u32[]{:S(2)}) collective-permute-start(bf16[16,3072]{1,0:T(8,128)(2,1)} %get-tuple-element.38), channel_id=1, source_target_pairs={{0,192},{32,224},{64,128},{96,160},{128,64},{160,96},{192,0},{224,... | collective-permute-start | bytes 294920 | tf_op jit(solution)/shard_map/ppermute | solution.py:473
  141.4 0.9 collective-permute-start.5
  142.3 1.2 collective-permute-start.4
  143.5 2.2 %collective-permute-start.8 = (f32[1,2048]{1,0:T(1,128)}, f32[1,2048]{1,0:T(1,128)S(1)}, u32[]{:S(2)}, u32[]{:S(2)}) collective-permute-start(f32[1,2048]{1,0:T(1,128)} %get-tuple-element.42), channel_id=1, source_target_pairs={{0,32},{32,0},{64,96},{96,64},{128,160},{160,128},{192,224},{224,1... | collective-permute-start | bytes 24584 | tf_op jit(solution)/shard_map/ppermute | solution.py:35
  145.7 2.1 %collective-permute-start.7 = (bf16[2,128,1024]{2,1,0:T(8,128)(2,1)}, bf16[2,128,1024]{2,1,0:T(8,128)(2,1)S(1)}, u32[]{:S(2)}, u32[]{:S(2)}) collective-permute-start(bf16[2,128,1024]{2,1,0:T(8,128)(2,1)} %token_grad.1), channel_id=1, source_target_pairs={{0,0},{1,32},{2,2},{3,34},{4,4},{5,36},{6,6},{7,38},{8,8},{9,40},{... | collective-permute-start | bytes 1572872 | tf_op jit(solution)/shard_map/ppermute | solution.py:31
  147.8 1.3 add.30
  149.8 1.1 collective-permute-done.5
  150.8 1.0 convert_add_fusion
  151.8 5.5 %collective-permute-done.7 = bf16[2,128,1024]{2,1,0:T(8,128)(2,1)S(1)} collective-permute-done((bf16[2,128,1024]{2,1,0:T(8,128)(2,1)}, bf16[2,128,1024]{2,1,0:T(8,128)(2,1)S(1)}, u32[]{:S(2)}, u32[]{:S(2)}) %collective-permute-start.7) | collective-permute-done | bytes 524320 | tf_op jit(solution)/shard_map/ppermute | solution.py:31
  157.3 0.8 fusion
  (22 shorter events, 4.6 us)
Async XLA Ops:
  3.4 12.1 %collective-permute-start = (bf16[272,1024]{1,0:T(8,128)(2,1)S(1)}, bf16[272,1024]{1,0:T(8,128)(2,1)S(1)}, u32[]{:S(2)}, u32[]{:S(2)}) collective-permute-start(bf16[272,1024]{1,0:T(8,128)(2,1)S(1)} %maximum_maximum_fusion), channel_id=1, source_target_pairs={{0,0},{1,32},{2,2},{3,34},{4,4},{5,36},{6,6},{7,38},{8,8},{9,40},{... | collective-permute-start | bytes 1671176 | tf_op jit(solution)/shard_map/ppermute | solution.py:31
  15.5 0.8 copy-start
  41.7 52.5 %all-to-all-start.1 = ((bf16[16,128,1024]{2,1,0:T(8,128)(2,1)}), bf16[16,128,1024]{2,1,0:T(8,128)(2,1)}, u32[]{:S(2)}, u32[]{:S(2)}) async-start(bf16[16,128,1024]{2,1,0:T(8,128)(2,1)} %get-tuple-element.26), calls=%async_computation.1 | async-start | bytes 8388608 | tf_op jit(solution)/shard_map/all_to_all | solution.py:39
  46.3 2.0 %collective-permute-start.1 = (bf16[16,128,128]{2,1,0:T(8,128)(2,1)S(1)}, bf16[16,128,128]{2,1,0:T(8,128)(2,1)S(1)}, u32[]{:S(2)}, u32[]{:S(2)}) collective-permute-start(bf16[16,128,128]{2,1,0:T(8,128)(2,1)S(1)} %slice.9), channel_id=1, source_target_pairs={{0,32},{32,0},{64,96},{96,64},{128,160},{160,128},{192,224},{224,1... | collective-permute-start | bytes 1572872 | tf_op jit(solution)/shard_map/ppermute | solution.py:35
  81.1 1.9 %collective-permute-start.2 = (bf16[16,128,128]{2,1,0:T(8,128)(2,1)S(1)}, bf16[16,128,128]{2,1,0:T(8,128)(2,1)S(1)}, u32[]{:S(2)}, u32[]{:S(2)}) collective-permute-start(bf16[16,128,128]{2,1,0:T(8,128)(2,1)S(1)} %get-tuple-element.30), channel_id=1, source_target_pairs={{0,32},{32,0},{64,96},{96,64},{128,160},{160,128},{192,224},{224,1... | collective-permute-start | bytes 1572872 | tf_op jit(solution)/shard_map/ppermute | solution.py:35
  94.2 20.7 %all-to-all-start.2 = ((bf16[16,256,128]{2,1,0:T(8,128)(2,1)}), bf16[16,256,128]{2,1,0:T(8,128)(2,1)S(1)}, u32[]{:S(2)}, u32[]{:S(2)}) async-start(bf16[16,256,128]{2,1,0:T(8,128)(2,1)} %combine.1.back_ref), calls=%async_computation.2 | async-start | bytes 2097152 | tf_op jit(solution)/shard_map/all_to_all | solution.py:39
  105.6 1.9 %collective-permute-start.3 = (f32[32,24,128]{2,1,0:T(8,128)}, f32[32,24,128]{2,1,0:T(8,128)S(1)}, u32[]{:S(2)}, u32[]{:S(2)}) collective-permute-start(f32[32,24,128]{2,1,0:T(8,128)} %get-tuple-element.32), channel_id=1, source_target_pairs={{0,32},{32,0},{64,96},{96,64},{128,160},{160,128},{192,224},{224,1... | collective-permute-start | bytes 1179656 | tf_op jit(solution)/shard_map/ppermute | solution.py:35
  107.6 0.7 copy-start.3
  114.8 6.7 %copy-start.1 = (bf16[16,256,128]{2,1,0:T(8,128)(2,1)}, bf16[16,256,128]{2,1,0:T(8,128)(2,1)S(1)}, u32[]{:S(2)}) copy-start(bf16[16,256,128]{2,1,0:T(8,128)(2,1)S(1)} %all-to-all-done.2.back_ref) | copy-start | bytes 3145732
  114.8 17.2 %all-to-all-start.3 = ((bf16[32,56,128]{2,1,0:T(8,128)(2,1)}), bf16[32,56,128]{2,1,0:T(8,128)(2,1)S(1)}, u32[]{:S(2)}, u32[]{:S(2)}) async-start(bf16[32,56,128]{2,1,0:T(8,128)(2,1)} %pack.1), calls=%async_computation.3 | async-start | bytes 917504 | tf_op jit(solution)/shard_map/all_to_all | solution.py:466
  132.1 0.8 copy-start.2
  135.3 14.4 %collective-permute-start.6 = (bf16[16,3072]{1,0:T(8,128)(2,1)}, bf16[16,3072]{1,0:T(8,128)(2,1)S(1)}, u32[]{:S(2)}, u32[]{:S(2)}) collective-permute-start(bf16[16,3072]{1,0:T(8,128)(2,1)} %get-tuple-element.38), channel_id=1, source_target_pairs={{0,192},{32,224},{64,128},{96,160},{128,64},{160,96},{192,0},{224,... | collective-permute-start | bytes 294920 | tf_op jit(solution)/shard_map/ppermute | solution.py:473
  141.4 9.4 %collective-permute-start.5 = (bf16[16,3072]{1,0:T(8,128)(2,1)}, bf16[16,3072]{1,0:T(8,128)(2,1)S(1)}, u32[]{:S(2)}, u32[]{:S(2)}) collective-permute-start(bf16[16,3072]{1,0:T(8,128)(2,1)} %get-tuple-element.38), channel_id=1, source_target_pairs={{0,128},{32,160},{64,192},{96,224},{128,0},{160,32},{192,64},{224,... | collective-permute-start | bytes 294920 | tf_op jit(solution)/shard_map/ppermute | solution.py:473
  142.3 8.5 %collective-permute-start.4 = (bf16[16,3072]{1,0:T(8,128)(2,1)}, bf16[16,3072]{1,0:T(8,128)(2,1)S(1)}, u32[]{:S(2)}, u32[]{:S(2)}) collective-permute-start(bf16[16,3072]{1,0:T(8,128)(2,1)} %get-tuple-element.38), channel_id=1, source_target_pairs={{0,64},{32,96},{64,0},{96,32},{128,192},{160,224},{192,128},{224,1... | collective-permute-start | bytes 294920 | tf_op jit(solution)/shard_map/ppermute | solution.py:473
  143.5 4.3 %collective-permute-start.8 = (f32[1,2048]{1,0:T(1,128)}, f32[1,2048]{1,0:T(1,128)S(1)}, u32[]{:S(2)}, u32[]{:S(2)}) collective-permute-start(f32[1,2048]{1,0:T(1,128)} %get-tuple-element.42), channel_id=1, source_target_pairs={{0,32},{32,0},{64,96},{96,64},{128,160},{160,128},{192,224},{224,1... | collective-permute-start | bytes 24584 | tf_op jit(solution)/shard_map/ppermute | solution.py:35
  145.7 11.7 %collective-permute-start.7 = (bf16[2,128,1024]{2,1,0:T(8,128)(2,1)}, bf16[2,128,1024]{2,1,0:T(8,128)(2,1)S(1)}, u32[]{:S(2)}, u32[]{:S(2)}) collective-permute-start(bf16[2,128,1024]{2,1,0:T(8,128)(2,1)} %token_grad.1), channel_id=1, source_target_pairs={{0,0},{1,32},{2,2},{3,34},{4,4},{5,36},{6,6},{7,38},{8,8},{9,40},{... | collective-permute-start | bytes 1572872 | tf_op jit(solution)/shard_map/ppermute | solution.py:31
  157.3 1.4 collective-permute-start.9

commit v3 on v2

--- a/solution.py
+++ b/solution.py
@@ -60,63 +60,73 @@
     )
 
 
-def project_kernel(x_ref, g_ref, mod_ref, wq_ref, wk_ref, wv_ref, copies_ref, out_ref, normed_ref, xhat_ref):
-    @pl.when(pl.program_id(0) == 0)
-    def _():
-        x = x_ref[...].astype(F32)
-        inv = 1.0 / jnp.sqrt(jnp.mean(x * x, axis=1, keepdims=True) + 1e-06)
-        mod = mod_ref[...].astype(F32)
-        xhat = x * inv
-        xhat_ref[...] = xhat.astype(BF16)
-        normed_ref[...] = (xhat * (1.0 + mod[0:1]) + mod[1:2]).astype(BF16)
-
-    normed = normed_ref[...]
-    for c in range(copies_ref.shape[0]):
-        copies_ref[c] = xhat_ref[...]
-    q4 = dot(normed, wq_ref[...]).astype(BF16).astype(F32)
-    k4 = dot(normed, wk_ref[...]).astype(BF16).astype(F32)
-    v4 = dot(normed, wv_ref[...]).astype(BF16).astype(F32)
-    g4 = g_ref[...].astype(F32)
+def weight_copies(w_ref, w_vmem, sems):
+    blocks = [pl.ds(i * 256, 256) for i in range(4)]
+    return [
+        pltpu.make_async_copy(w_ref.at[rows], w_vmem.at[rows], sems.at[i])
+        for i, rows in enumerate(blocks)
+    ]
+
+
+def project_kernel(packed_ref, w_ref, copies_ref, out_ref, w_vmem, xhat_vmem, acc, w_sems, out_sems):
+    loads = weight_copies(w_ref, w_vmem, w_sems)
+    for load in loads:
+        load.start()
+    x = packed_ref[:TOK].astype(F32)
+    inv = 1.0 / jnp.sqrt(jnp.mean(x * x, axis=1, keepdims=True) + 1e-06)
+    xhat = x * inv
+    xhat_vmem[...] = xhat.astype(BF16)
+    stores = [
+        pltpu.make_async_copy(xhat_vmem, copies_ref.at[t], out_sems.at[t]) for t in range(HEADS)
+    ]
+    for store in stores:
+        store.start()
+    mod = packed_ref[2 * TOK :].astype(F32)
+    normed = (xhat * (1.0 + mod[0:1]) + mod[1:2]).astype(BF16)
+    for i, load in enumerate(loads):
+        load.wait()
+        rows = slice(i * 256, (i + 1) * 256)
+        part = dot(normed[:, rows], w_vmem[rows])
+        if i == 0:
+            acc[...] = part
+        elif i < 3:
+            acc[...] += part
     low = low_lanes((TOK, 128))
-    for p in range(2):
-        lanes = slice(p * 128, (p + 1) * 128)
-        for rows, a, b in ((slice(0, TOK), q4, g4), (slice(TOK, 2 * TOK), k4, v4)):
-            first, second = pairs(low, a[:, lanes], b[:, lanes])
+    for p in range(HEADS // 2):
+        lanes = [slice(c * WIDTH + p * 128, c * WIDTH + (p + 1) * 128) for c in range(3)]
+        q, k, v = [(acc[:, lane] + part[:, lane]).astype(BF16).astype(F32) for lane in lanes]
+        g = packed_ref[TOK : 2 * TOK, lanes[0]].astype(F32)
+        for rows, a, b in ((slice(0, TOK), q, g), (slice(TOK, 2 * TOK), k, v)):
+            first, second = pairs(low, a, b)
             out_ref[2 * p, rows] = first.astype(BF16)
             out_ref[2 * p + 1, rows] = second.astype(BF16)
-
-
-def weight_specs():
-    return [pl.BlockSpec((WIDTH, 256), lambda i, c=c: (0, 4 * c + i)) for c in range(3)]
+    for store in stores:
+        store.wait()
 
 
 def project(packed, w):
+    vmem = pl.BlockSpec(memory_space=pltpu.VMEM)
     return pl.pallas_call(
         project_kernel,
-        grid=(4,),
-        in_specs=[
-            pl.BlockSpec((TOK, WIDTH), lambda i: (0, 0)),
-            pl.BlockSpec((TOK, 256), lambda i: (1, i)),
-            pl.BlockSpec((16, WIDTH), lambda i: (16, 0)),
-        ]
-        + weight_specs(),
-        out_specs=[
-            pl.BlockSpec((4, TOK, WIDTH), lambda i: (i, 0, 0)),
-            pl.BlockSpec((4, 2 * TOK, 128), lambda i: (i, 0, 0)),
-        ],
+        in_specs=[vmem, pl.BlockSpec(memory_space=pl.ANY)],
+        out_specs=[pl.BlockSpec(memory_space=pl.ANY), vmem],
         out_shape=[
             jax.ShapeDtypeStruct((HEADS, TOK, WIDTH), BF16),
             jax.ShapeDtypeStruct((HEADS, 2 * TOK, 128), BF16),
         ],
-        scratch_shapes=[pltpu.VMEM((TOK, WIDTH), BF16)] * 2,
-        compiler_params=pltpu.CompilerParams(
-            vmem_limit_bytes=60 * MIB, dimension_semantics=("arbitrary",)
-        ),
+        scratch_shapes=[
+            pltpu.VMEM((WIDTH, 3 * WIDTH), BF16),
+            pltpu.VMEM((TOK, WIDTH), BF16),
+            pltpu.VMEM((TOK, 3 * WIDTH), F32),
+            pltpu.SemaphoreType.DMA((4,)),
+            pltpu.SemaphoreType.DMA((HEADS,)),
+        ],
+        compiler_params=pltpu.CompilerParams(vmem_limit_bytes=59 * MIB),
         cost_estimate=pl.CostEstimate(
-            flops=2 * TOK * WIDTH * 3 * WIDTH, bytes_accessed=12 * MIB, transcendentals=0
+            flops=2 * TOK * WIDTH * 3 * WIDTH, bytes_accessed=8 * MIB, transcendentals=0
         ),
         name="project",
-    )(packed, packed, packed, w, w, w)
+    )(packed, w)
 
 
 def attention_kernel(
@@ -325,6 +335,7 @@
     return pl.pallas_call(
         pack_kernel,
         out_shape=jax.ShapeDtypeStruct((32, 56, 128), BF16),
+        compiler_params=pltpu.CompilerParams(vmem_limit_bytes=16 * MIB),
         cost_estimate=pl.CostEstimate(flops=1 << 18, bytes_accessed=MIB, transcendentals=0),
         name="pack",
     )(keep, got, sums)
@@ -351,9 +362,9 @@
     core = place_ref[0] == 0
     keep = jnp.where(core, sums[0], sums[1])
     other = jnp.where(core, sums[1], sums[0])
+    other_ref[...] = other
     for r in range(16):
         keep_ref[:, r * 128 : (r + 1) * 128] = keep[r : r + 1]
-        other_ref[:, r * 128 : (r + 1) * 128] = other[r : r + 1]
 
 
 def collect(place, pieces):
@@ -367,81 +378,79 @@
                 pl.BlockSpec((16, 3 * WIDTH), lambda i, core: (0, 0)),
                 pl.BlockSpec((16, 3 * WIDTH), lambda i, core: (0, 0)),
                 pl.BlockSpec((1, 2 * WIDTH), lambda i, core: (0, 0)),
-                pl.BlockSpec((1, 2 * WIDTH), lambda i, core: (0, 0)),
+                pl.BlockSpec((16, 128), lambda i, core: (0, 0)),
             ],
         ),
         out_shape=[
             jax.ShapeDtypeStruct((16, 3 * WIDTH), F32),
             jax.ShapeDtypeStruct((16, 3 * WIDTH), BF16),
             jax.ShapeDtypeStruct((1, 2 * WIDTH), F32),
-            jax.ShapeDtypeStruct((1, 2 * WIDTH), F32),
-        ],
+            jax.ShapeDtypeStruct((16, 128), F32),
+        ],
+        compiler_params=pltpu.CompilerParams(vmem_limit_bytes=16 * MIB),
         cost_estimate=pl.CostEstimate(flops=1 << 20, bytes_accessed=MIB, transcendentals=0),
         name="collect",
     )(place, pieces)
 
 
-def token_kernel(x_ref, mod_ref, back_ref, wq_ref, wk_ref, wv_ref, out_ref, acc):
-    i = pl.program_id(0)
+def weight_column_copies(w_ref, w_vmem, sems):
+    groups = []
+    for i in range(4):
+        group = []
+        for c in range(3):
+            lanes = slice(c * WIDTH + i * 256, c * WIDTH + (i + 1) * 256)
+            group.append(
+                pltpu.make_async_copy(w_ref.at[:, lanes], w_vmem.at[:, lanes], sems.at[3 * i + c])
+            )
+        groups.append(group)
+    return groups
+
+
+def token_kernel(packed_ref, back_ref, w_ref, out_ref, w_vmem, w_sems):
+    loads = weight_column_copies(w_ref, w_vmem, w_sems)
+    for group in loads:
+        for load in group:
+            load.start()
     low = low_lanes((TOK, 128))
-    dq, dk, dv = [], [], []
-    for p in range(2):
-        a = back_ref[2 * p].astype(F32)
-        b = back_ref[2 * p + 1].astype(F32)
-        dq_pair, attended = pairs(low, a[:TOK], b[:TOK])
-        dk_pair, dv_pair = pairs(low, a[TOK:], b[TOK:])
-        lanes = pl.ds(pl.multiple_of(i * 256 + p * 128, 128), 128)
-        out_ref[0, :, lanes] = attended.astype(BF16)
-        dq.append(dq_pair.astype(BF16))
-        dk.append(dk_pair.astype(BF16))
-        dv.append(dv_pair.astype(BF16))
-    part = (
-        dot_t(jnp.concatenate(dq, axis=1), wq_ref[...])
-        + dot_t(jnp.concatenate(dk, axis=1), wk_ref[...])
-        + dot_t(jnp.concatenate(dv, axis=1), wv_ref[...])
-    )
-
-    @pl.when(i == 0)
-    def _():
-        acc[...] = part
-
-    @pl.when(i > 0)
-    def _():
-        acc[...] += part
-
-    @pl.when(i == pl.num_programs(0) - 1)
-    def _():
-        x = x_ref[...].astype(F32)
-        inv = 1.0 / jnp.sqrt(jnp.mean(x * x, axis=1, keepdims=True) + 1e-06)
-        xhat = x * inv
-        dn = acc[...]
-        gn = dn * (1.0 + mod_ref[0:1].astype(F32))
-        out_ref[1] = (
-            inv * (gn - xhat * jnp.mean(gn * xhat, axis=1, keepdims=True))
-        ).astype(BF16)
+    dn = jnp.zeros((TOK, WIDTH), F32)
+    for i, group in enumerate(loads):
+        parts = [[], [], []]
+        for p in range(2):
+            a = back_ref[4 * i + 2 * p].astype(F32)
+            b = back_ref[4 * i + 2 * p + 1].astype(F32)
+            dq_pair, attended = pairs(low, a[:TOK], b[:TOK])
+            dk_pair, dv_pair = pairs(low, a[TOK:], b[TOK:])
+            out_ref[0, :, i * 256 + p * 128 : i * 256 + (p + 1) * 128] = attended.astype(BF16)
+            for part, pair in zip(parts, (dq_pair, dk_pair, dv_pair)):
+                part.append(pair.astype(BF16))
+        for c, load in enumerate(group):
+            load.wait()
+            lanes = slice(c * WIDTH + i * 256, c * WIDTH + (i + 1) * 256)
+            dn = dn + dot_t(jnp.concatenate(parts[c], axis=1), w_vmem[:, lanes])
+    x = packed_ref[:TOK].astype(F32)
+    inv = 1.0 / jnp.sqrt(jnp.mean(x * x, axis=1, keepdims=True) + 1e-06)
+    xhat = x * inv
+    gn = dn * (1.0 + packed_ref[2 * TOK :].astype(F32)[0:1])
+    out_ref[1] = (inv * (gn - xhat * jnp.mean(gn * xhat, axis=1, keepdims=True))).astype(BF16)
 
 
 def token_grad(packed, back, w):
+    vmem = pl.BlockSpec(memory_space=pltpu.VMEM)
     return pl.pallas_call(
         token_kernel,
-        grid=(4,),
-        in_specs=[
-            pl.BlockSpec((TOK, WIDTH), lambda i: (0, 0)),
-            pl.BlockSpec((16, WIDTH), lambda i: (16, 0)),
-            pl.BlockSpec((4, 2 * TOK, 128), lambda i: (i, 0, 0)),
-        ]
-        + weight_specs(),
-        out_specs=pl.BlockSpec((2, TOK, WIDTH), lambda i: (0, 0, 0)),
+        in_specs=[vmem, vmem, pl.BlockSpec(memory_space=pl.ANY)],
+        out_specs=vmem,
         out_shape=jax.ShapeDtypeStruct((2, TOK, WIDTH), BF16),
-        scratch_shapes=[pltpu.VMEM((TOK, WIDTH), F32)],
-        compiler_params=pltpu.CompilerParams(
-            vmem_limit_bytes=60 * MIB, dimension_semantics=("arbitrary",)
-        ),
+        scratch_shapes=[
+            pltpu.VMEM((WIDTH, 3 * WIDTH), BF16),
+            pltpu.SemaphoreType.DMA((12,)),
+        ],
+        compiler_params=pltpu.CompilerParams(vmem_limit_bytes=59 * MIB),
         cost_estimate=pl.CostEstimate(
             flops=2 * TOK * WIDTH * 3 * WIDTH, bytes_accessed=8 * MIB, transcendentals=0
         ),
         name="token_grad",
-    )(packed, packed, back, w, w, w)
+    )(packed, back, w)
 
 
 def on_device(tokens, timestep, table, w_qkv, grad_out):
@@ -468,11 +477,12 @@
     pieces, out = lax.optimization_barrier((pieces, out))
     out = swap(out)
     rows, rows_low, modulation, modulation_other = collect(place, pieces)
-    modulation = modulation + from_other_core(modulation_other)
     for k in (2, 4, 6):
         rows = rows + lax.ppermute(rows_low, "dp", [(d, d ^ k) for d in range(8)]).astype(F32)
-    rows, out = lax.optimization_barrier((rows, out))
-    other_rows = from_other_core(rows)
+    other_rows = from_other_core(jnp.concatenate([rows, modulation_other], axis=1))
+    modulation = modulation + other_rows[:, 3 * WIDTH :].reshape(1, 2 * WIDTH)
+    other_rows = other_rows[:, : 3 * WIDTH]
+    other_rows, out = lax.optimization_barrier((other_rows, out))
     grad_wqkv = jnp.concatenate(
         [jnp.where(core == 0, rows, other_rows), jnp.where(core == 0, other_rows, rows)], axis=0
     )

time: 160 us -> 157 us (0.981)
  starting transfers between devices: 32.6 us -> 36.6 us
  Pallas kernels: 58.4 us -> 55.3 us
  waiting for transfers between devices: 39.5 us -> 36.5 us
  other arithmetic: 4.91 us -> 3.26 us
    ppermute x2, waiting for transfers between devices: 12.7 us -> 7.7 us  [swap(): return lax.ppermute(x, ('dp', 'tile'), SWAP)]
    ppermute x2, starting transfers between devices: 7.05 us -> 9.21 us  [swap(): return lax.ppermute(x, ('dp', 'tile'), SWAP)]
    pallas_call x1, Pallas kernels: 2.51 us -> 0.66 us  [collect(): pl.pallas_call(collect_kernel, grid_spec=pltpu.PrefetchScalarGridSpec(num...]
    ppermute x5 -> x4, starting transfers between devices: 2.4 us -> 3.97 us  [from_other_core(): return lax.ppermute(x, 'dp', OTHER_CORE)]
    ppermute x5 -> x4, waiting for transfers between devices: 6.21 us -> 6.68 us  [from_other_core(): return lax.ppermute(x, 'dp', OTHER_CORE)]
  transfers between devices with their start and end apart: 13 -> 12, of which waited for: 11 -> 11; matrix products, arithmetic and copies ran while one was open for 2% -> 1% of each run, Pallas kernels for 31% -> 31%
where the time goes in v3:
time: 157 us; the launch traced here: 156 us
  Pallas kernels  55.3 us (35%)
  starting transfers between devices  36.6 us (23%)
  waiting for transfers between devices  36.5 us (23%)
  blocking collectives  18.6 us (12%)
  local copies, waits for them, and re-layouts  4.26 us (3%)
  other arithmetic  3.26 us (2%)
    pallas_call x1, Pallas kernels, attention(): pl.pallas_call(functools.partial(attention_kernel, bq, kt), grid=(nq // b...  32.8 us
    all_to_all x1, blocking collectives, plane_exchange(): lax.all_to_all(x, 'tile', split_axis=0, concat_axis=0, tiled=True, axis_i...  18.6 us
    all_to_all x2, waiting for transfers between devices, plane_exchange(): lax.all_to_all(x, 'tile', split_axis=0, concat_axis=0, tiled=True, axis_i...  15 us
    ppermute x2, starting transfers between devices, swap(): return lax.ppermute(x, ('dp', 'tile'), SWAP)  9.21 us
    ppermute x3, starting transfers between devices, on_device(): lax.ppermute(rows_low, 'dp', [(d, d ^ k) for d in range(8)]).astype(F32)  8.62 us
    all_to_all x2, starting transfers between devices, plane_exchange(): lax.all_to_all(x, 'tile', split_axis=0, concat_axis=0, tiled=True, axis_i...  8.37 us
    ppermute x2, waiting for transfers between devices, swap(): return lax.ppermute(x, ('dp', 'tile'), SWAP)  7.7 us
    pallas_call x1, Pallas kernels, project(): pl.pallas_call(project_kernel, in_specs=[vmem, pl.BlockSpec(memory_space=...  7.07 us
  transfers between devices with their start and end apart: 12, of which 11 were waited for; matrix products, arithmetic and copies ran while one was open for 1% of the time, Pallas kernels for 31%

profile of v3, /device:TPU:1, one launch (start us, length us, event | category | flops | bytes accessed | tf_op | source)
XLA Modules:
  0.0 156.1 jit_solution(1274568458267826172)
XLA Ops:
  1.3 0.8 dynamic-slice_reduce_fusion
  2.2 1.2 maximum_maximum_fusion
  3.4 4.9 %collective-permute-start = (bf16[272,1024]{1,0:T(8,128)(2,1)S(1)}, bf16[272,1024]{1,0:T(8,128)(2,1)S(1)}, u32[]{:S(2)}, u32[]{:S(2)}) collective-permute-start(bf16[272,1024]{1,0:T(8,128)(2,1)S(1)} %maximum_maximum_fusion), channel_id=1, source_target_pairs={{0,0},{1,32},{2,2},{3,34},{4,4},{5,36},{6,6},{7,38},{8,8},{9,40},{... | collective-permute-start | bytes 1671176 | tf_op jit(solution)/shard_map/ppermute | solution.py:31
  8.3 7.2 %collective-permute-done.packed_ref.mod_ref = bf16[272,1024]{1,0:T(8,128)(2,1)S(1)} collective-permute-done((bf16[272,1024]{1,0:T(8,128)(2,1)S(1)}, bf16[272,1024]{1,0:T(8,128)(2,1)S(1)}, u32[]{:S(2)}, u32[]{:S(2)}) %collective-permute-start) | collective-permute-done | bytes 557088 | tf_op jit(solution)/shard_map/ppermute | solution.py:31
  15.5 0.8 copy-done.3
  16.3 7.1 %project.1 = (bf16[16,128,1024]{2,1,0:T(8,128)(2,1)}, bf16[16,256,128]{2,1,0:T(8,128)(2,1)}) custom-call(bf16[272,1024]{1,0:T(8,128)(2,1)} %copy-done.3, bf16[1024,3072]{1,0:T(8,128)(2,1)} %w_ref.3), custom_call_target="tpu_custom_call" | custom-call | flops 805306368 | bytes 8388608 | tf_op jit(solution)/shard_map/project/pallas_call | solution.py:109
  23.4 18.6 %all_to_all.20.recv_ref = bf16[16,256,128]{2,1,0:T(8,128)(2,1)S(1)} all-to-all(bf16[16,256,128]{2,1,0:T(8,128)(2,1)} %get-tuple-element.25), channel_id=1, replica_groups={{0,2,4,6,8,10,12,14,16,18,20,22,24,26,28,30},{1,3,5,7,9,11,13,15,17,19,..., dimensions={0} | all-to-all | bytes 2097152 | tf_op jit(solution)/shard_map/all_to_all | solution.py:39
  42.0 4.5 %all-to-all-start.1 = ((bf16[16,128,1024]{2,1,0:T(8,128)(2,1)}), bf16[16,128,1024]{2,1,0:T(8,128)(2,1)}, u32[]{:S(2)}, u32[]{:S(2)}) async-start(bf16[16,128,1024]{2,1,0:T(8,128)(2,1)} %get-tuple-element.26), calls=%async_computation.1 | async-start | bytes 8388608 | tf_op jit(solution)/shard_map/all_to_all | solution.py:39
  46.7 1.9 %collective-permute-done.1.kvp_ref = bf16[16,128,128]{2,1,0:T(8,128)(2,1)S(1)} collective-permute-done((bf16[16,128,128]{2,1,0:T(8,128)(2,1)S(1)}, bf16[16,128,128]{2,1,0:T(8,128)(2,1)S(1)}, u32[]{:S(2)}, u32[]{:S(2)}) %collective-permute-start.1) | collective-permute-done | bytes 524320 | tf_op jit(solution)/shard_map/ppermute | solution.py:35
  48.6 32.8 %attention.1 = (bf16[16,256,128]{2,1,0:T(8,128)(2,1)}, f32[16,128,128]{2,1,0:T(8,128)S(1)}, bf16[16,128,128]{2,1,0:T(8,128)(2,1)S(1)}) custom-call(bf16[16,256,128]{2,1,0:T(8,128)(2,1)S(1)} %all_to_all.20.recv_ref, bf16[16,128,128]{2,1,0:T(8,128)(2,1)S(1)} %collective-permute-done.1.kvp_ref), custom_call_target="tpu_custom_call" | custom-call | flops 25769803776 | bytes 4194304 | tf_op jit(solution)/shard_map/attention/pallas_call | solution.py:193
  81.5 1.8 %collective-permute-done.2.mine_ref = bf16[16,128,128]{2,1,0:T(8,128)(2,1)S(1)} collective-permute-done((bf16[16,128,128]{2,1,0:T(8,128)(2,1)S(1)}, bf16[16,128,128]{2,1,0:T(8,128)(2,1)S(1)}, u32[]{:S(2)}, u32[]{:S(2)}) %collective-permute-start.2) | collective-permute-done | bytes 524320 | tf_op jit(solution)/shard_map/ppermute | solution.py:35
  83.3 0.9 combine.1.back_ref
  84.2 10.3 %all-to-all-done.1 = bf16[16,128,1024]{2,1,0:T(8,128)(2,1)} async-done(((bf16[16,128,1024]{2,1,0:T(8,128)(2,1)}), bf16[16,128,1024]{2,1,0:T(8,128)(2,1)}, u32[]{:S(2)}, u32[]{:S(2)}) %all-to-all-start.1) | async-done | bytes 4194336 | tf_op jit(solution)/shard_map/all_to_all | solution.py:39
  94.5 3.8 %all-to-all-start.2 = ((bf16[16,256,128]{2,1,0:T(8,128)(2,1)}), bf16[16,256,128]{2,1,0:T(8,128)(2,1)S(1)}, u32[]{:S(2)}, u32[]{:S(2)}) async-start(bf16[16,256,128]{2,1,0:T(8,128)(2,1)} %combine.1.back_ref), calls=%async_computation.2 | async-start | bytes 2097152 | tf_op jit(solution)/shard_map/all_to_all | solution.py:39
  99.0 6.9 %weight_grad.1 = (f32[32,24,128]{2,1,0:T(8,128)}, f32[32,24,128]{2,1,0:T(8,128)}, f32[2,1024]{1,0:T(2,128)}) custom-call(s32[3]{0:T(128)} %pad_add_fusion.place_ref, bf16[2048,1024]{1,0:T(8,128)(2,1)} %bitcast.6.xhat_ref, bf16[16,256,128]{2,1,0:T(8,128)(2,1)} %combine.1.back_ref, bf16[272,1024]{1,0:T(8,128)(2,1)} %copy-done.3, bf16[1024,3072]{1,0:T(8,128)(2,1)} %w_ref.3, ...), custom_call_target="tpu_custom_call" | custom-call | flops 1073741824 | bytes 6291456 | tf_op jit(solution)/shard_map/weight_grad/pallas_call | solution.py:297
  105.9 1.9 %collective-permute-done.3.got_ref = f32[32,24,128]{2,1,0:T(8,128)S(1)} collective-permute-done((f32[32,24,128]{2,1,0:T(8,128)}, f32[32,24,128]{2,1,0:T(8,128)S(1)}, u32[]{:S(2)}, u32[]{:S(2)}) %collective-permute-start.3) | collective-permute-done | bytes 393248 | tf_op jit(solution)/shard_map/ppermute | solution.py:35
  107.8 1.0 copy-done
  109.5 0.9 pack.1
  110.4 4.8 %all-to-all-done.2.back_ref = bf16[16,256,128]{2,1,0:T(8,128)(2,1)S(1)} async-done(((bf16[16,256,128]{2,1,0:T(8,128)(2,1)}), bf16[16,256,128]{2,1,0:T(8,128)(2,1)S(1)}, u32[]{:S(2)}, u32[]{:S(2)}) %all-to-all-start.2) | async-done | bytes 1048608 | tf_op jit(solution)/shard_map/all_to_all | solution.py:39
  115.1 6.4 %all-to-all-start.3 = ((bf16[32,56,128]{2,1,0:T(8,128)(2,1)}), bf16[32,56,128]{2,1,0:T(8,128)(2,1)S(1)}, u32[]{:S(2)}, u32[]{:S(2)}) async-start(bf16[32,56,128]{2,1,0:T(8,128)(2,1)} %pack.1), calls=%async_computation.3 | async-start | bytes 917504 | tf_op jit(solution)/shard_map/all_to_all | solution.py:475
  121.6 6.1 %token_grad.1 = bf16[2,128,1024]{2,1,0:T(8,128)(2,1)} custom-call(bf16[272,1024]{1,0:T(8,128)(2,1)} %copy-done.3, bf16[16,256,128]{2,1,0:T(8,128)(2,1)} %copy-done.4, bf16[1024,3072]{1,0:T(8,128)(2,1)} %w_ref.3), custom_call_target="tpu_custom_call" | custom-call | flops 805306368 | bytes 8388608 | tf_op jit(solution)/shard_map/token_grad/pallas_call | solution.py:439
  127.8 4.3 %all-to-all-done.3.pieces_ref = bf16[32,56,128]{2,1,0:T(8,128)(2,1)S(1)} async-done(((bf16[32,56,128]{2,1,0:T(8,128)(2,1)}), bf16[32,56,128]{2,1,0:T(8,128)(2,1)S(1)}, u32[]{:S(2)}, u32[]{:S(2)}) %all-to-all-start.3) | async-done | bytes 458784 | tf_op jit(solution)/shard_map/all_to_all | solution.py:475
  132.7 6.4 %collective-permute-start.6 = (bf16[16,3072]{1,0:T(8,128)(2,1)S(1)}, bf16[16,3072]{1,0:T(8,128)(2,1)S(1)}, u32[]{:S(2)}, u32[]{:S(2)}) collective-permute-start(bf16[16,3072]{1,0:T(8,128)(2,1)S(1)} %get-tuple-element.38), channel_id=1, source_target_pairs={{0,192},{32,224},{64,128},{96,160},{128,64},{160,96},{192,0},{224,... | collective-permute-start | bytes 294920 | tf_op jit(solution)/shard_map/ppermute | solution.py:481
  139.2 1.0 collective-permute-start.5
  140.2 1.2 collective-permute-start.4
  141.4 4.3 %collective-permute-start.8 = (bf16[2,128,1024]{2,1,0:T(8,128)(2,1)}, bf16[2,128,1024]{2,1,0:T(8,128)(2,1)S(1)}, u32[]{:S(2)}, u32[]{:S(2)}) collective-permute-start(bf16[2,128,1024]{2,1,0:T(8,128)(2,1)} %token_grad.1), channel_id=1, source_target_pairs={{0,0},{1,32},{2,2},{3,34},{4,4},{5,36},{6,6},{7,38},{8,8},{9,40},{... | collective-permute-start | bytes 1572872 | tf_op jit(solution)/shard_map/ppermute | solution.py:31
  145.6 1.6 %collective-permute-done.6 = bf16[16,3072]{1,0:T(8,128)(2,1)S(1)} collective-permute-done((bf16[16,3072]{1,0:T(8,128)(2,1)S(1)}, bf16[16,3072]{1,0:T(8,128)(2,1)S(1)}, u32[]{:S(2)}, u32[]{:S(2)}) %collective-permute-start.6) | collective-permute-done | bytes 98336 | tf_op jit(solution)/shard_map/ppermute | solution.py:481
  147.3 1.1 collective-permute-done.5
  148.5 3.7 %collective-permute-start.7 = (f32[16,3200]{1,0:T(8,128)S(1)}, f32[16,3200]{1,0:T(8,128)S(1)}, u32[]{:S(2)}, u32[]{:S(2)}) collective-permute-start(f32[16,3200]{1,0:T(8,128)S(1)} %pad_maximum_fusion.1), channel_id=1, source_target_pairs={{0,32},{32,0},{64,96},{96,64},{128,160},{160,128},{192,224},{224,1... | collective-permute-start | bytes 614408 | tf_op jit(solution)/shard_map/ppermute | solution.py:35
  152.2 1.1 collective-permute-done.7
  154.4 0.8 fusion
  155.3 0.8 pad_maximum_fusion
  (25 shorter events, 3.5 us)
Async XLA Ops:
  3.4 12.1 %collective-permute-start = (bf16[272,1024]{1,0:T(8,128)(2,1)S(1)}, bf16[272,1024]{1,0:T(8,128)(2,1)S(1)}, u32[]{:S(2)}, u32[]{:S(2)}) collective-permute-start(bf16[272,1024]{1,0:T(8,128)(2,1)S(1)} %maximum_maximum_fusion), channel_id=1, source_target_pairs={{0,0},{1,32},{2,2},{3,34},{4,4},{5,36},{6,6},{7,38},{8,8},{9,40},{... | collective-permute-start | bytes 1671176 | tf_op jit(solution)/shard_map/ppermute | solution.py:31
  15.5 0.8 copy-start.3
  42.0 52.5 %all-to-all-start.1 = ((bf16[16,128,1024]{2,1,0:T(8,128)(2,1)}), bf16[16,128,1024]{2,1,0:T(8,128)(2,1)}, u32[]{:S(2)}, u32[]{:S(2)}) async-start(bf16[16,128,1024]{2,1,0:T(8,128)(2,1)} %get-tuple-element.26), calls=%async_computation.1 | async-start | bytes 8388608 | tf_op jit(solution)/shard_map/all_to_all | solution.py:39
  46.6 2.0 %collective-permute-start.1 = (bf16[16,128,128]{2,1,0:T(8,128)(2,1)S(1)}, bf16[16,128,128]{2,1,0:T(8,128)(2,1)S(1)}, u32[]{:S(2)}, u32[]{:S(2)}) collective-permute-start(bf16[16,128,128]{2,1,0:T(8,128)(2,1)S(1)} %slice.15), channel_id=1, source_target_pairs={{0,32},{32,0},{64,96},{96,64},{128,160},{160,128},{192,224},{224,1... | collective-permute-start | bytes 1572872 | tf_op jit(solution)/shard_map/ppermute | solution.py:35
  81.4 1.9 %collective-permute-start.2 = (bf16[16,128,128]{2,1,0:T(8,128)(2,1)S(1)}, bf16[16,128,128]{2,1,0:T(8,128)(2,1)S(1)}, u32[]{:S(2)}, u32[]{:S(2)}) collective-permute-start(bf16[16,128,128]{2,1,0:T(8,128)(2,1)S(1)} %get-tuple-element.30), channel_id=1, source_target_pairs={{0,32},{32,0},{64,96},{96,64},{128,160},{160,128},{192,224},{224,1... | collective-permute-start | bytes 1572872 | tf_op jit(solution)/shard_map/ppermute | solution.py:35
  94.5 20.6 %all-to-all-start.2 = ((bf16[16,256,128]{2,1,0:T(8,128)(2,1)}), bf16[16,256,128]{2,1,0:T(8,128)(2,1)S(1)}, u32[]{:S(2)}, u32[]{:S(2)}) async-start(bf16[16,256,128]{2,1,0:T(8,128)(2,1)} %combine.1.back_ref), calls=%async_computation.2 | async-start | bytes 2097152 | tf_op jit(solution)/shard_map/all_to_all | solution.py:39
  105.9 1.9 %collective-permute-start.3 = (f32[32,24,128]{2,1,0:T(8,128)}, f32[32,24,128]{2,1,0:T(8,128)S(1)}, u32[]{:S(2)}, u32[]{:S(2)}) collective-permute-start(f32[32,24,128]{2,1,0:T(8,128)} %get-tuple-element.32), channel_id=1, source_target_pairs={{0,32},{32,0},{64,96},{96,64},{128,160},{160,128},{192,224},{224,1... | collective-permute-start | bytes 1179656 | tf_op jit(solution)/shard_map/ppermute | solution.py:35
  107.8 1.0 copy-start
  108.8 0.7 copy-start.1
  115.1 6.5 %copy-start.4 = (bf16[16,256,128]{2,1,0:T(8,128)(2,1)}, bf16[16,256,128]{2,1,0:T(8,128)(2,1)S(1)}, u32[]{:S(2)}) copy-start(bf16[16,256,128]{2,1,0:T(8,128)(2,1)S(1)} %all-to-all-done.2.back_ref) | copy-start | bytes 3145732
  115.1 17.0 %all-to-all-start.3 = ((bf16[32,56,128]{2,1,0:T(8,128)(2,1)}), bf16[32,56,128]{2,1,0:T(8,128)(2,1)S(1)}, u32[]{:S(2)}, u32[]{:S(2)}) async-start(bf16[32,56,128]{2,1,0:T(8,128)(2,1)} %pack.1), calls=%async_computation.3 | async-start | bytes 917504 | tf_op jit(solution)/shard_map/all_to_all | solution.py:475
  121.6 10.5 %copy-start.2 = (s32[3]{0:T(128)S(1)}, s32[3]{0:T(128)}, u32[]{:S(2)}) copy-start(s32[3]{0:T(128)} %pad_add_fusion.place_ref) | copy-start | bytes 40
  132.7 14.5 %collective-permute-start.6 = (bf16[16,3072]{1,0:T(8,128)(2,1)S(1)}, bf16[16,3072]{1,0:T(8,128)(2,1)S(1)}, u32[]{:S(2)}, u32[]{:S(2)}) collective-permute-start(bf16[16,3072]{1,0:T(8,128)(2,1)S(1)} %get-tuple-element.38), channel_id=1, source_target_pairs={{0,192},{32,224},{64,128},{96,160},{128,64},{160,96},{192,0},{224,... | collective-permute-start | bytes 294920 | tf_op jit(solution)/shard_map/ppermute | solution.py:481
  139.2 9.2 %collective-permute-start.5 = (bf16[16,3072]{1,0:T(8,128)(2,1)S(1)}, bf16[16,3072]{1,0:T(8,128)(2,1)S(1)}, u32[]{:S(2)}, u32[]{:S(2)}) collective-permute-start(bf16[16,3072]{1,0:T(8,128)(2,1)S(1)} %get-tuple-element.38), channel_id=1, source_target_pairs={{0,128},{32,160},{64,192},{96,224},{128,0},{160,32},{192,64},{224,... | collective-permute-start | bytes 294920 | tf_op jit(solution)/shard_map/ppermute | solution.py:481
  140.2 8.2 %collective-permute-start.4 = (bf16[16,3072]{1,0:T(8,128)(2,1)S(1)}, bf16[16,3072]{1,0:T(8,128)(2,1)S(1)}, u32[]{:S(2)}, u32[]{:S(2)}) collective-permute-start(bf16[16,3072]{1,0:T(8,128)(2,1)S(1)} %get-tuple-element.38), channel_id=1, source_target_pairs={{0,64},{32,96},{64,0},{96,32},{128,192},{160,224},{192,128},{224,1... | collective-permute-start | bytes 294920 | tf_op jit(solution)/shard_map/ppermute | solution.py:481
  141.4 13.1 %collective-permute-start.8 = (bf16[2,128,1024]{2,1,0:T(8,128)(2,1)}, bf16[2,128,1024]{2,1,0:T(8,128)(2,1)S(1)}, u32[]{:S(2)}, u32[]{:S(2)}) collective-permute-start(bf16[2,128,1024]{2,1,0:T(8,128)(2,1)} %token_grad.1), channel_id=1, source_target_pairs={{0,0},{1,32},{2,2},{3,34},{4,4},{5,36},{6,6},{7,38},{8,8},{9,40},{... | collective-permute-start | bytes 1572872 | tf_op jit(solution)/shard_map/ppermute | solution.py:31
  148.5 4.8 %collective-permute-start.7 = (f32[16,3200]{1,0:T(8,128)S(1)}, f32[16,3200]{1,0:T(8,128)S(1)}, u32[]{:S(2)}, u32[]{:S(2)}) collective-permute-start(f32[16,3200]{1,0:T(8,128)S(1)} %pad_maximum_fusion.1), channel_id=1, source_target_pairs={{0,32},{32,0},{64,96},{96,64},{128,160},{160,128},{192,224},{224,1... | collective-permute-start | bytes 614408 | tf_op jit(solution)/shard_map/ppermute | solution.py:35

commit v4 on v3

--- a/solution.py
+++ b/solution.py
@@ -81,7 +81,7 @@
     ]
     for store in stores:
         store.start()
-    mod = packed_ref[2 * TOK :].astype(F32)
+    mod = packed_ref[TOK:].astype(F32)
     normed = (xhat * (1.0 + mod[0:1]) + mod[1:2]).astype(BF16)
     for i, load in enumerate(loads):
         load.wait()
@@ -95,11 +95,11 @@
     for p in range(HEADS // 2):
         lanes = [slice(c * WIDTH + p * 128, c * WIDTH + (p + 1) * 128) for c in range(3)]
         q, k, v = [(acc[:, lane] + part[:, lane]).astype(BF16).astype(F32) for lane in lanes]
-        g = packed_ref[TOK : 2 * TOK, lanes[0]].astype(F32)
-        for rows, a, b in ((slice(0, TOK), q, g), (slice(TOK, 2 * TOK), k, v)):
-            first, second = pairs(low, a, b)
-            out_ref[2 * p, rows] = first.astype(BF16)
-            out_ref[2 * p + 1, rows] = second.astype(BF16)
+        out_ref[2 * p, :TOK] = q.astype(BF16)
+        out_ref[2 * p + 1, :TOK] = pltpu.roll(q, DEPTH, 1).astype(BF16)
+        first, second = pairs(low, k, v)
+        out_ref[2 * p, TOK:] = first.astype(BF16)
+        out_ref[2 * p + 1, TOK:] = second.astype(BF16)
     for store in stores:
         store.wait()
 
@@ -127,6 +127,29 @@
         ),
         name="project",
     )(packed, w)
+
+
+def cotangent_kernel(queries_ref, g_ref, out_ref):
+    low = low_lanes((TOK, 128))
+    for p in range(HEADS // 2):
+        g = g_ref[:, p * 128 : (p + 1) * 128].astype(F32)
+        for head, part in ((2 * p, pltpu.roll(g, DEPTH, 1)), (2 * p + 1, g)):
+            out_ref[head] = jnp.where(low, queries_ref[head].astype(F32), part).astype(BF16)
+
+
+def add_cotangents(sent, g):
+    queries = pl.BlockSpec((HEADS, TOK, 128), lambda i: (0, 0, 0))
+    return pl.pallas_call(
+        cotangent_kernel,
+        grid=(1,),
+        in_specs=[queries, pl.BlockSpec((TOK, WIDTH), lambda i: (0, 0))],
+        out_specs=queries,
+        out_shape=jax.ShapeDtypeStruct((HEADS, 2 * TOK, 128), BF16),
+        input_output_aliases={0: 0},
+        compiler_params=pltpu.CompilerParams(vmem_limit_bytes=32 * MIB),
+        cost_estimate=pl.CostEstimate(flops=1 << 18, bytes_accessed=2 * MIB, transcendentals=0),
+        name="add_cotangents",
+    )(sent, g)
 
 
 def attention_kernel(
@@ -302,7 +325,7 @@
             in_specs=[
                 pl.BlockSpec((2048, 256), lambda i, place: (0, i)),
                 pl.BlockSpec((16, 256, 128), lambda i, place: (0, 0, 0)),
-                pl.BlockSpec((16, 256), lambda i, place: (16, i)),
+                pl.BlockSpec((16, 256), lambda i, place: (8, i)),
             ]
             + [pl.BlockSpec((256, 128), lambda i, place, c=c: (i, 8 * c + place[2])) for c in range(3)],
             out_specs=[rows, rows, pl.BlockSpec((2, 256), lambda i, place: (0, i))],
@@ -430,7 +453,7 @@
     x = packed_ref[:TOK].astype(F32)
     inv = 1.0 / jnp.sqrt(jnp.mean(x * x, axis=1, keepdims=True) + 1e-06)
     xhat = x * inv
-    gn = dn * (1.0 + packed_ref[2 * TOK :].astype(F32)[0:1])
+    gn = dn * (1.0 + packed_ref[TOK:].astype(F32)[0:1])
     out_ref[1] = (inv * (gn - xhat * jnp.mean(gn * xhat, axis=1, keepdims=True))).astype(BF16)
 
 
@@ -458,11 +481,10 @@
     head = lax.axis_index("tile") // 2
     place = jnp.stack([core, head % 2, head // 2]).astype(jnp.int32)
     row = lax.dynamic_slice(table, (timestep[0], 0), (1, 2 * WIDTH)).reshape(2, WIDTH)
-    packed = swap(
-        jnp.concatenate([tokens[0], grad_out[0], row, jnp.zeros((14, WIDTH), BF16)], axis=0)
-    )
+    packed = swap(jnp.concatenate([tokens[0], row, jnp.zeros((14, WIDTH), BF16)], axis=0))
+    g = swap(grad_out[0])
     copies, sent = project(packed, w_qkv)
-    recv = plane_exchange(sent)
+    recv = plane_exchange(add_cotangents(sent, g))
     copies, recv = lax.optimization_barrier((copies, recv))
     kvp = from_other_core(recv[:, TOK:])
     xhat = plane_exchange(copies).reshape(16 * TOK, WIDTH)

time: 157 us -> 163 us (1.038)
  waiting for transfers between devices: 36.5 us -> 41.8 us
    all_to_all x2, waiting for transfers between devices: 15 us -> 22.9 us  [plane_exchange(): lax.all_to_all(x, 'tile', split_axis=0, concat_axis=0, tiled=True, axis_i...]
    ppermute x2 -> x3, waiting for transfers between devices: 7.7 us -> 3.02 us  [swap(): return lax.ppermute(x, ('dp', 'tile'), SWAP)]
    all_to_all x1, starting transfers between devices: 6.45 us -> 3.89 us  [on_device(): lax.all_to_all(packed_grads, 'tile', split_axis=0, concat_axis=0, tiled=T...]
    all_to_all x1, waiting for transfers between devices: 4.32 us -> 6.02 us  [on_device(): lax.all_to_all(packed_grads, 'tile', split_axis=0, concat_axis=0, tiled=T...]
    unnamed x10 -> x12, local copies, waits for them, and re-layouts: 2.5 us -> 3.64 us
    ppermute x2 -> x3, starting transfers between devices: 9.21 us -> 9.81 us  [swap(): return lax.ppermute(x, ('dp', 'tile'), SWAP)]
  transfers between devices with their start and end apart: 12 -> 13, of which waited for: 11 -> 11; matrix products, arithmetic and copies ran while one was open for 1% -> 1% of each run, Pallas kernels for 31% -> 34%
where the time goes in v4:
time: 163 us
  Pallas kernels  55.6 us (34%)
  waiting for transfers between devices  41.8 us (26%)
  starting transfers between devices  35.8 us (22%)
  blocking collectives  19.3 us (12%)
  local copies, waits for them, and re-layouts  5.4 us (3%)
  other arithmetic  3.13 us (2%)
    pallas_call x1, Pallas kernels, attention(): pl.pallas_call(functools.partial(attention_kernel, bq, kt), grid=(nq // b...  32.8 us
    all_to_all x2, waiting for transfers between devices, plane_exchange(): lax.all_to_all(x, 'tile', split_axis=0, concat_axis=0, tiled=True, axis_i...  22.9 us
    all_to_all x1, blocking collectives, plane_exchange(): lax.all_to_all(x, 'tile', split_axis=0, concat_axis=0, tiled=True, axis_i...  19.3 us
    ppermute x3, starting transfers between devices, swap(): return lax.ppermute(x, ('dp', 'tile'), SWAP)  9.81 us
    ppermute x3, starting transfers between devices, on_device(): lax.ppermute(rows_low, 'dp', [(d, d ^ k) for d in range(8)]).astype(F32)  8.98 us
    all_to_all x2, starting transfers between devices, plane_exchange(): lax.all_to_all(x, 'tile', split_axis=0, concat_axis=0, tiled=True, axis_i...  8.6 us
    pallas_call x1, Pallas kernels, project(): pl.pallas_call(project_kernel, in_specs=[vmem, pl.BlockSpec(memory_space=...  6.97 us
    pallas_call x1, Pallas kernels, weight_grad(): pl.pallas_call(weight_kernel, grid_spec=pltpu.PrefetchScalarGridSpec(num_...  6.92 us
  transfers between devices with their start and end apart: 13, of which 11 were waited for; matrix products, arithmetic and copies ran while one was open for 1% of the time, Pallas kernels for 34%

profile of v4, /device:TPU:1, one launch (start us, length us, event | category | flops | bytes accessed | tf_op | source)
XLA Modules:
  0.0 162.6 jit_solution(3254255254206886082)
XLA Ops:
  1.3 0.8 dynamic-slice_reduce_fusion
  2.2 1.1 maximum_maximum_fusion
  3.2 4.9 %collective-permute-start = (bf16[144,1024]{1,0:T(8,128)(2,1)S(1)}, bf16[144,1024]{1,0:T(8,128)(2,1)S(1)}, u32[]{:S(2)}, u32[]{:S(2)}) collective-permute-start(bf16[144,1024]{1,0:T(8,128)(2,1)S(1)} %maximum_maximum_fusion), channel_id=1, source_target_pairs={{0,0},{1,32},{2,2},{3,34},{4,4},{5,36},{6,6},{7,38},{8,8},{9,40},{... | collective-permute-start | bytes 884744 | tf_op jit(solution)/shard_map/ppermute | solution.py:31
  8.2 1.9 %collective-permute-start.1 = (bf16[128,1024]{1,0:T(8,128)(2,1)}, bf16[128,1024]{1,0:T(8,128)(2,1)S(1)}, u32[]{:S(2)}, u32[]{:S(2)}) collective-permute-start(bf16[128,1024]{1,0:T(8,128)(2,1)} %bitcast.13), channel_id=1, source_target_pairs={{0,0},{1,32},{2,2},{3,34},{4,4},{5,36},{6,6},{7,38},{8,8},{9,40},{... | collective-permute-start | bytes 786440 | tf_op jit(solution)/shard_map/ppermute | solution.py:31
  10.1 2.5 %collective-permute-done.packed_ref.mod_ref = bf16[144,1024]{1,0:T(8,128)(2,1)S(1)} collective-permute-done((bf16[144,1024]{1,0:T(8,128)(2,1)S(1)}, bf16[144,1024]{1,0:T(8,128)(2,1)S(1)}, u32[]{:S(2)}, u32[]{:S(2)}) %collective-permute-start) | collective-permute-done | bytes 294944 | tf_op jit(solution)/shard_map/ppermute | solution.py:31
  13.3 7.0 %project.1 = (bf16[16,128,1024]{2,1,0:T(8,128)(2,1)}, bf16[16,256,128]{2,1,0:T(8,128)(2,1)}) custom-call(bf16[144,1024]{1,0:T(8,128)(2,1)} %copy-done.5, bf16[1024,3072]{1,0:T(8,128)(2,1)} %w_ref.3), custom_call_target="tpu_custom_call" | custom-call | flops 805306368 | bytes 8388608 | tf_op jit(solution)/shard_map/project/pallas_call | solution.py:109
  20.3 1.2 copy-done
  21.9 19.3 %all_to_all.20.recv_ref = bf16[16,256,128]{2,1,0:T(8,128)(2,1)S(1)} all-to-all(bf16[16,256,128]{2,1,0:T(8,128)(2,1)S(1)} %add_cotangents.1), channel_id=1, replica_groups={{0,2,4,6,8,10,12,14,16,18,20,22,24,26,28,30},{1,3,5,7,9,11,13,15,17,19,..., dimensions={0} | all-to-all | bytes 2097152 | tf_op jit(solution)/shard_map/all_to_all | solution.py:39
  41.2 4.5 %all-to-all-start.1 = ((bf16[16,128,1024]{2,1,0:T(8,128)(2,1)}), bf16[16,128,1024]{2,1,0:T(8,128)(2,1)}, u32[]{:S(2)}, u32[]{:S(2)}) async-start(bf16[16,128,1024]{2,1,0:T(8,128)(2,1)} %get-tuple-element.26), calls=%async_computation.1 | async-start | bytes 8388608 | tf_op jit(solution)/shard_map/all_to_all | solution.py:39
  45.9 1.9 %collective-permute-done.2.kvp_ref = bf16[16,128,128]{2,1,0:T(8,128)(2,1)S(1)} collective-permute-done((bf16[16,128,128]{2,1,0:T(8,128)(2,1)S(1)}, bf16[16,128,128]{2,1,0:T(8,128)(2,1)S(1)}, u32[]{:S(2)}, u32[]{:S(2)}) %collective-permute-start.2) | collective-permute-done | bytes 524320 | tf_op jit(solution)/shard_map/ppermute | solution.py:35
  47.8 32.8 %attention.1 = (bf16[16,256,128]{2,1,0:T(8,128)(2,1)}, f32[16,128,128]{2,1,0:T(8,128)S(1)}, bf16[16,128,128]{2,1,0:T(8,128)(2,1)S(1)}) custom-call(bf16[16,256,128]{2,1,0:T(8,128)(2,1)S(1)} %all_to_all.20.recv_ref, bf16[16,128,128]{2,1,0:T(8,128)(2,1)S(1)} %collective-permute-done.2.kvp_ref), custom_call_target="tpu_custom_call" | custom-call | flops 25769803776 | bytes 4194304 | tf_op jit(solution)/shard_map/attention/pallas_call | solution.py:216
  80.7 1.8 %collective-permute-done.3.mine_ref = bf16[16,128,128]{2,1,0:T(8,128)(2,1)S(1)} collective-permute-done((bf16[16,128,128]{2,1,0:T(8,128)(2,1)S(1)}, bf16[16,128,128]{2,1,0:T(8,128)(2,1)S(1)}, u32[]{:S(2)}, u32[]{:S(2)}) %collective-permute-start.3) | collective-permute-done | bytes 524320 | tf_op jit(solution)/shard_map/ppermute | solution.py:35
  82.5 0.9 combine.1.back_ref
  83.4 18.6 %all-to-all-done.1 = bf16[16,128,1024]{2,1,0:T(8,128)(2,1)} async-done(((bf16[16,128,1024]{2,1,0:T(8,128)(2,1)}), bf16[16,128,1024]{2,1,0:T(8,128)(2,1)}, u32[]{:S(2)}, u32[]{:S(2)}) %all-to-all-start.1) | async-done | bytes 4194336 | tf_op jit(solution)/shard_map/all_to_all | solution.py:39
  102.0 4.1 %all-to-all-start.2 = ((bf16[16,256,128]{2,1,0:T(8,128)(2,1)}), bf16[16,256,128]{2,1,0:T(8,128)(2,1)S(1)}, u32[]{:S(2)}, u32[]{:S(2)}) async-start(bf16[16,256,128]{2,1,0:T(8,128)(2,1)} %combine.1.back_ref), calls=%async_computation.2 | async-start | bytes 2097152 | tf_op jit(solution)/shard_map/all_to_all | solution.py:39
  106.7 6.9 %weight_grad.1 = (f32[32,24,128]{2,1,0:T(8,128)}, f32[32,24,128]{2,1,0:T(8,128)}, f32[2,1024]{1,0:T(2,128)}) custom-call(s32[3]{0:T(128)} %pad_add_fusion.place_ref, bf16[2048,1024]{1,0:T(8,128)(2,1)} %bitcast.6.xhat_ref, bf16[16,256,128]{2,1,0:T(8,128)(2,1)} %combine.1.back_ref, bf16[144,1024]{1,0:T(8,128)(2,1)} %copy-done.5, bf16[1024,3072]{1,0:T(8,128)(2,1)} %w_ref.3, ...), custom_call_target="tpu_custom_call" | custom-call | flops 1073741824 | bytes 6291456 | tf_op jit(solution)/shard_map/weight_grad/pallas_call | solution.py:320
  113.6 1.9 %collective-permute-done.4.got_ref = f32[32,24,128]{2,1,0:T(8,128)S(1)} collective-permute-done((f32[32,24,128]{2,1,0:T(8,128)}, f32[32,24,128]{2,1,0:T(8,128)S(1)}, u32[]{:S(2)}, u32[]{:S(2)}) %collective-permute-start.4) | collective-permute-done | bytes 393248 | tf_op jit(solution)/shard_map/ppermute | solution.py:35
  115.6 1.0 copy-done.1
  117.3 0.8 pack.1
  118.1 4.3 %all-to-all-done.2.back_ref = bf16[16,256,128]{2,1,0:T(8,128)(2,1)S(1)} async-done(((bf16[16,256,128]{2,1,0:T(8,128)(2,1)}), bf16[16,256,128]{2,1,0:T(8,128)(2,1)S(1)}, u32[]{:S(2)}, u32[]{:S(2)}) %all-to-all-start.2) | async-done | bytes 1048608 | tf_op jit(solution)/shard_map/all_to_all | solution.py:39
  122.4 3.9 %all-to-all-start.3 = ((bf16[32,56,128]{2,1,0:T(8,128)(2,1)}), bf16[32,56,128]{2,1,0:T(8,128)(2,1)S(1)}, u32[]{:S(2)}, u32[]{:S(2)}) async-start(bf16[32,56,128]{2,1,0:T(8,128)(2,1)} %pack.1), calls=%async_computation.3 | async-start | bytes 917504 | tf_op jit(solution)/shard_map/all_to_all | solution.py:497
  126.3 6.1 %token_grad.1 = bf16[2,128,1024]{2,1,0:T(8,128)(2,1)} custom-call(bf16[144,1024]{1,0:T(8,128)(2,1)} %copy-done.5, bf16[16,256,128]{2,1,0:T(8,128)(2,1)} %copy-done.4, bf16[1024,3072]{1,0:T(8,128)(2,1)} %w_ref.3), custom_call_target="tpu_custom_call" | custom-call | flops 805306368 | bytes 8388608 | tf_op jit(solution)/shard_map/token_grad/pallas_call | solution.py:462
  132.4 6.0 %all-to-all-done.3.pieces_ref = bf16[32,56,128]{2,1,0:T(8,128)(2,1)S(1)} async-done(((bf16[32,56,128]{2,1,0:T(8,128)(2,1)}), bf16[32,56,128]{2,1,0:T(8,128)(2,1)S(1)}, u32[]{:S(2)}, u32[]{:S(2)}) %all-to-all-start.3) | async-done | bytes 458784 | tf_op jit(solution)/shard_map/all_to_all | solution.py:497
  139.1 6.8 %collective-permute-start.7 = (bf16[16,3072]{1,0:T(8,128)(2,1)S(1)}, bf16[16,3072]{1,0:T(8,128)(2,1)S(1)}, u32[]{:S(2)}, u32[]{:S(2)}) collective-permute-start(bf16[16,3072]{1,0:T(8,128)(2,1)S(1)} %get-tuple-element.38), channel_id=1, source_target_pairs={{0,192},{32,224},{64,128},{96,160},{128,64},{160,96},{192,0},{224,... | collective-permute-start | bytes 294920 | tf_op jit(solution)/shard_map/ppermute | solution.py:503
  145.9 1.0 collective-permute-start.6
  146.9 1.2 collective-permute-start.5
  148.1 2.9 %collective-permute-start.9 = (bf16[2,128,1024]{2,1,0:T(8,128)(2,1)}, bf16[2,128,1024]{2,1,0:T(8,128)(2,1)S(1)}, u32[]{:S(2)}, u32[]{:S(2)}) collective-permute-start(bf16[2,128,1024]{2,1,0:T(8,128)(2,1)} %token_grad.1), channel_id=1, source_target_pairs={{0,0},{1,32},{2,2},{3,34},{4,4},{5,36},{6,6},{7,38},{8,8},{9,40},{... | collective-permute-start | bytes 1572872 | tf_op jit(solution)/shard_map/ppermute | solution.py:31
  151.0 2.8 %collective-permute-done.7 = bf16[16,3072]{1,0:T(8,128)(2,1)S(1)} collective-permute-done((bf16[16,3072]{1,0:T(8,128)(2,1)S(1)}, bf16[16,3072]{1,0:T(8,128)(2,1)S(1)}, u32[]{:S(2)}, u32[]{:S(2)}) %collective-permute-start.7) | collective-permute-done | bytes 98336 | tf_op jit(solution)/shard_map/ppermute | solution.py:503
  154.3 4.3 %collective-permute-start.8 = (f32[16,3200]{1,0:T(8,128)S(1)}, f32[16,3200]{1,0:T(8,128)S(1)}, u32[]{:S(2)}, u32[]{:S(2)}) collective-permute-start(f32[16,3200]{1,0:T(8,128)S(1)} %pad_maximum_fusion.1), channel_id=1, source_target_pairs={{0,32},{32,0},{64,96},{96,64},{128,160},{160,128},{192,224},{224,1... | collective-permute-start | bytes 614408 | tf_op jit(solution)/shard_map/ppermute | solution.py:35
  158.7 1.1 collective-permute-done.8
  160.9 0.8 fusion
  161.8 0.8 pad_maximum_fusion
  (30 shorter events, 5.1 us)
Async XLA Ops:
  3.2 9.3 %collective-permute-start = (bf16[144,1024]{1,0:T(8,128)(2,1)S(1)}, bf16[144,1024]{1,0:T(8,128)(2,1)S(1)}, u32[]{:S(2)}, u32[]{:S(2)}) collective-permute-start(bf16[144,1024]{1,0:T(8,128)(2,1)S(1)} %maximum_maximum_fusion), channel_id=1, source_target_pairs={{0,0},{1,32},{2,2},{3,34},{4,4},{5,36},{6,6},{7,38},{8,8},{9,40},{... | collective-permute-start | bytes 884744 | tf_op jit(solution)/shard_map/ppermute | solution.py:31
  8.2 12.1 %collective-permute-start.1 = (bf16[128,1024]{1,0:T(8,128)(2,1)}, bf16[128,1024]{1,0:T(8,128)(2,1)S(1)}, u32[]{:S(2)}, u32[]{:S(2)}) collective-permute-start(bf16[128,1024]{1,0:T(8,128)(2,1)} %bitcast.13), channel_id=1, source_target_pairs={{0,0},{1,32},{2,2},{3,34},{4,4},{5,36},{6,6},{7,38},{8,8},{9,40},{... | collective-permute-start | bytes 786440 | tf_op jit(solution)/shard_map/ppermute | solution.py:31
  12.6 0.7 copy-start.5
  20.3 1.2 copy-start
  41.2 60.8 %all-to-all-start.1 = ((bf16[16,128,1024]{2,1,0:T(8,128)(2,1)}), bf16[16,128,1024]{2,1,0:T(8,128)(2,1)}, u32[]{:S(2)}, u32[]{:S(2)}) async-start(bf16[16,128,1024]{2,1,0:T(8,128)(2,1)} %get-tuple-element.26), calls=%async_computation.1 | async-start | bytes 8388608 | tf_op jit(solution)/shard_map/all_to_all | solution.py:39
  45.8 2.0 %collective-permute-start.2 = (bf16[16,128,128]{2,1,0:T(8,128)(2,1)S(1)}, bf16[16,128,128]{2,1,0:T(8,128)(2,1)S(1)}, u32[]{:S(2)}, u32[]{:S(2)}) collective-permute-start(bf16[16,128,128]{2,1,0:T(8,128)(2,1)S(1)} %slice.15), channel_id=1, source_target_pairs={{0,32},{32,0},{64,96},{96,64},{128,160},{160,128},{192,224},{224,1... | collective-permute-start | bytes 1572872 | tf_op jit(solution)/shard_map/ppermute | solution.py:35
  80.6 1.9 %collective-permute-start.3 = (bf16[16,128,128]{2,1,0:T(8,128)(2,1)S(1)}, bf16[16,128,128]{2,1,0:T(8,128)(2,1)S(1)}, u32[]{:S(2)}, u32[]{:S(2)}) collective-permute-start(bf16[16,128,128]{2,1,0:T(8,128)(2,1)S(1)} %get-tuple-element.30), channel_id=1, source_target_pairs={{0,32},{32,0},{64,96},{96,64},{128,160},{160,128},{192,224},{224,1... | collective-permute-start | bytes 1572872 | tf_op jit(solution)/shard_map/ppermute | solution.py:35
  102.0 20.4 %all-to-all-start.2 = ((bf16[16,256,128]{2,1,0:T(8,128)(2,1)}), bf16[16,256,128]{2,1,0:T(8,128)(2,1)S(1)}, u32[]{:S(2)}, u32[]{:S(2)}) async-start(bf16[16,256,128]{2,1,0:T(8,128)(2,1)} %combine.1.back_ref), calls=%async_computation.2 | async-start | bytes 2097152 | tf_op jit(solution)/shard_map/all_to_all | solution.py:39
  113.6 1.9 %collective-permute-start.4 = (f32[32,24,128]{2,1,0:T(8,128)}, f32[32,24,128]{2,1,0:T(8,128)S(1)}, u32[]{:S(2)}, u32[]{:S(2)}) collective-permute-start(f32[32,24,128]{2,1,0:T(8,128)} %get-tuple-element.32), channel_id=1, source_target_pairs={{0,32},{32,0},{64,96},{96,64},{128,160},{160,128},{192,224},{224,1... | collective-permute-start | bytes 1179656 | tf_op jit(solution)/shard_map/ppermute | solution.py:35
  115.6 1.0 copy-start.1
  116.6 0.7 copy-start.2
  122.4 3.9 %copy-start.4 = (bf16[16,256,128]{2,1,0:T(8,128)(2,1)}, bf16[16,256,128]{2,1,0:T(8,128)(2,1)S(1)}, u32[]{:S(2)}) copy-start(bf16[16,256,128]{2,1,0:T(8,128)(2,1)S(1)} %all-to-all-done.2.back_ref) | copy-start | bytes 3145732
  122.4 16.0 %all-to-all-start.3 = ((bf16[32,56,128]{2,1,0:T(8,128)(2,1)}), bf16[32,56,128]{2,1,0:T(8,128)(2,1)S(1)}, u32[]{:S(2)}, u32[]{:S(2)}) async-start(bf16[32,56,128]{2,1,0:T(8,128)(2,1)} %pack.1), calls=%async_computation.3 | async-start | bytes 917504 | tf_op jit(solution)/shard_map/all_to_all | solution.py:497
  126.3 12.1 %copy-start.3 = (s32[3]{0:T(128)S(1)}, s32[3]{0:T(128)}, u32[]{:S(2)}) copy-start(s32[3]{0:T(128)} %pad_add_fusion.place_ref) | copy-start | bytes 40
  139.1 14.8 %collective-permute-start.7 = (bf16[16,3072]{1,0:T(8,128)(2,1)S(1)}, bf16[16,3072]{1,0:T(8,128)(2,1)S(1)}, u32[]{:S(2)}, u32[]{:S(2)}) collective-permute-start(bf16[16,3072]{1,0:T(8,128)(2,1)S(1)} %get-tuple-element.38), channel_id=1, source_target_pairs={{0,192},{32,224},{64,128},{96,160},{128,64},{160,96},{192,0},{224,... | collective-permute-start | bytes 294920 | tf_op jit(solution)/shard_map/ppermute | solution.py:503
  145.9 8.3 %collective-permute-start.6 = (bf16[16,3072]{1,0:T(8,128)(2,1)S(1)}, bf16[16,3072]{1,0:T(8,128)(2,1)S(1)}, u32[]{:S(2)}, u32[]{:S(2)}) collective-permute-start(bf16[16,3072]{1,0:T(8,128)(2,1)S(1)} %get-tuple-element.38), channel_id=1, source_target_pairs={{0,128},{32,160},{64,192},{96,224},{128,0},{160,32},{192,64},{224,... | collective-permute-start | bytes 294920 | tf_op jit(solution)/shard_map/ppermute | solution.py:503
  146.9 7.3 %collective-permute-start.5 = (bf16[16,3072]{1,0:T(8,128)(2,1)S(1)}, bf16[16,3072]{1,0:T(8,128)(2,1)S(1)}, u32[]{:S(2)}, u32[]{:S(2)}) collective-permute-start(bf16[16,3072]{1,0:T(8,128)(2,1)S(1)} %get-tuple-element.38), channel_id=1, source_target_pairs={{0,64},{32,96},{64,0},{96,32},{128,192},{160,224},{192,128},{224,1... | collective-permute-start | bytes 294920 | tf_op jit(solution)/shard_map/ppermute | solution.py:503
  148.1 12.8 %collective-permute-start.9 = (bf16[2,128,1024]{2,1,0:T(8,128)(2,1)}, bf16[2,128,1024]{2,1,0:T(8,128)(2,1)S(1)}, u32[]{:S(2)}, u32[]{:S(2)}) collective-permute-start(bf16[2,128,1024]{2,1,0:T(8,128)(2,1)} %token_grad.1), channel_id=1, source_target_pairs={{0,0},{1,32},{2,2},{3,34},{4,4},{5,36},{6,6},{7,38},{8,8},{9,40},{... | collective-permute-start | bytes 1572872 | tf_op jit(solution)/shard_map/ppermute | solution.py:31
  154.3 5.4 %collective-permute-start.8 = (f32[16,3200]{1,0:T(8,128)S(1)}, f32[16,3200]{1,0:T(8,128)S(1)}, u32[]{:S(2)}, u32[]{:S(2)}) collective-permute-start(f32[16,3200]{1,0:T(8,128)S(1)} %pad_maximum_fusion.1), channel_id=1, source_target_pairs={{0,32},{32,0},{64,96},{96,64},{128,160},{160,128},{192,224},{224,1... | collective-permute-start | bytes 614408 | tf_op jit(solution)/shard_map/ppermute | solution.py:35

commit v5 on v3

--- a/solution.py
+++ b/solution.py
@@ -68,7 +68,7 @@
     ]
 
 
-def project_kernel(packed_ref, w_ref, copies_ref, out_ref, w_vmem, xhat_vmem, acc, w_sems, out_sems):
+def project_kernel(packed_ref, g_ref, w_ref, copies_ref, out_ref, w_vmem, xhat_vmem, acc, w_sems, out_sems):
     loads = weight_copies(w_ref, w_vmem, w_sems)
     for load in loads:
         load.start()
@@ -81,7 +81,7 @@
     ]
     for store in stores:
         store.start()
-    mod = packed_ref[2 * TOK :].astype(F32)
+    mod = packed_ref[TOK:].astype(F32)
     normed = (xhat * (1.0 + mod[0:1]) + mod[1:2]).astype(BF16)
     for i, load in enumerate(loads):
         load.wait()
@@ -95,7 +95,7 @@
     for p in range(HEADS // 2):
         lanes = [slice(c * WIDTH + p * 128, c * WIDTH + (p + 1) * 128) for c in range(3)]
         q, k, v = [(acc[:, lane] + part[:, lane]).astype(BF16).astype(F32) for lane in lanes]
-        g = packed_ref[TOK : 2 * TOK, lanes[0]].astype(F32)
+        g = g_ref[:, lanes[0]].astype(F32)
         for rows, a, b in ((slice(0, TOK), q, g), (slice(TOK, 2 * TOK), k, v)):
             first, second = pairs(low, a, b)
             out_ref[2 * p, rows] = first.astype(BF16)
@@ -104,11 +104,11 @@
         store.wait()
 
 
-def project(packed, w):
+def project(packed, g, w):
     vmem = pl.BlockSpec(memory_space=pltpu.VMEM)
     return pl.pallas_call(
         project_kernel,
-        in_specs=[vmem, pl.BlockSpec(memory_space=pl.ANY)],
+        in_specs=[vmem, vmem, pl.BlockSpec(memory_space=pl.ANY)],
         out_specs=[pl.BlockSpec(memory_space=pl.ANY), vmem],
         out_shape=[
             jax.ShapeDtypeStruct((HEADS, TOK, WIDTH), BF16),
@@ -126,7 +126,7 @@
             flops=2 * TOK * WIDTH * 3 * WIDTH, bytes_accessed=8 * MIB, transcendentals=0
         ),
         name="project",
-    )(packed, w)
+    )(packed, g, w)
 
 
 def attention_kernel(
@@ -302,7 +302,7 @@
             in_specs=[
                 pl.BlockSpec((2048, 256), lambda i, place: (0, i)),
                 pl.BlockSpec((16, 256, 128), lambda i, place: (0, 0, 0)),
-                pl.BlockSpec((16, 256), lambda i, place: (16, i)),
+                pl.BlockSpec((16, 256), lambda i, place: (8, i)),
             ]
             + [pl.BlockSpec((256, 128), lambda i, place, c=c: (i, 8 * c + place[2])) for c in range(3)],
             out_specs=[rows, rows, pl.BlockSpec((2, 256), lambda i, place: (0, i))],
@@ -430,7 +430,7 @@
     x = packed_ref[:TOK].astype(F32)
     inv = 1.0 / jnp.sqrt(jnp.mean(x * x, axis=1, keepdims=True) + 1e-06)
     xhat = x * inv
-    gn = dn * (1.0 + packed_ref[2 * TOK :].astype(F32)[0:1])
+    gn = dn * (1.0 + packed_ref[TOK:].astype(F32)[0:1])
     out_ref[1] = (inv * (gn - xhat * jnp.mean(gn * xhat, axis=1, keepdims=True))).astype(BF16)
 
 
@@ -458,10 +458,9 @@
     head = lax.axis_index("tile") // 2
     place = jnp.stack([core, head % 2, head // 2]).astype(jnp.int32)
     row = lax.dynamic_slice(table, (timestep[0], 0), (1, 2 * WIDTH)).reshape(2, WIDTH)
-    packed = swap(
-        jnp.concatenate([tokens[0], grad_out[0], row, jnp.zeros((14, WIDTH), BF16)], axis=0)
-    )
-    copies, sent = project(packed, w_qkv)
+    packed = swap(jnp.concatenate([tokens[0], row, jnp.zeros((14, WIDTH), BF16)], axis=0))
+    g = swap(grad_out[0])
+    copies, sent = project(packed, g, w_qkv)
     recv = plane_exchange(sent)
     copies, recv = lax.optimization_barrier((copies, recv))
     kvp = from_other_core(recv[:, TOK:])

time: 157 us -> 159 us (1.013)
  starting transfers between devices: 36.6 us -> 38.5 us
    all_to_all x1, starting transfers between devices: 6.45 us -> 3.89 us  [on_device(): lax.all_to_all(packed_grads, 'tile', split_axis=0, concat_axis=0, tiled=T...]
    ppermute x2 -> x3, starting transfers between devices: 9.21 us -> 11.4 us  [swap(): return lax.ppermute(x, ('dp', 'tile'), SWAP)]
    ppermute x3, starting transfers between devices: 8.62 us -> 10.6 us  [on_device(): lax.ppermute(rows_low, 'dp', [(d, d ^ k) for d in range(8)]).astype(F32)]
    ppermute x2 -> x3, waiting for transfers between devices: 7.7 us -> 6.48 us  [swap(): return lax.ppermute(x, ('dp', 'tile'), SWAP)]
  transfers between devices with their start and end apart: 12 -> 13, of which waited for: 11 -> 11; matrix products, arithmetic and copies ran while one was open for 1% -> 1% of each run, Pallas kernels for 31% -> 30%
where the time goes in v5:
time: 159 us; the launch traced here: 158 us
  Pallas kernels  55.3 us (35%)
  starting transfers between devices  38.5 us (24%)
  waiting for transfers between devices  36.1 us (23%)
  blocking collectives  18.6 us (12%)
  local copies, waits for them, and re-layouts  4.88 us (3%)
  other arithmetic  3.13 us (2%)
    pallas_call x1, Pallas kernels, attention(): pl.pallas_call(functools.partial(attention_kernel, bq, kt), grid=(nq // b...  32.8 us
    all_to_all x1, blocking collectives, plane_exchange(): lax.all_to_all(x, 'tile', split_axis=0, concat_axis=0, tiled=True, axis_i...  18.6 us
    all_to_all x2, waiting for transfers between devices, plane_exchange(): lax.all_to_all(x, 'tile', split_axis=0, concat_axis=0, tiled=True, axis_i...  16.1 us
    ppermute x3, starting transfers between devices, swap(): return lax.ppermute(x, ('dp', 'tile'), SWAP)  11.4 us
    ppermute x3, starting transfers between devices, on_device(): lax.ppermute(rows_low, 'dp', [(d, d ^ k) for d in range(8)]).astype(F32)  10.6 us
    all_to_all x2, starting transfers between devices, plane_exchange(): lax.all_to_all(x, 'tile', split_axis=0, concat_axis=0, tiled=True, axis_i...  8.38 us
    pallas_call x1, Pallas kernels, project(): pl.pallas_call(project_kernel, in_specs=[vmem, vmem, pl.BlockSpec(memory_...  7.06 us
    pallas_call x1, Pallas kernels, weight_grad(): pl.pallas_call(weight_kernel, grid_spec=pltpu.PrefetchScalarGridSpec(num_...  6.92 us
  transfers between devices with their start and end apart: 13, of which 11 were waited for; matrix products, arithmetic and copies ran while one was open for 1% of the time, Pallas kernels for 30%

profile of v5, /device:TPU:1, one launch (start us, length us, event | category | flops | bytes accessed | tf_op | source)
XLA Modules:
  0.0 158.0 jit_solution(8410742619479072242)
XLA Ops:
  1.3 0.8 dynamic-slice_reduce_fusion
  2.2 1.1 maximum_maximum_fusion
  3.2 4.9 %collective-permute-start = (bf16[144,1024]{1,0:T(8,128)(2,1)S(1)}, bf16[144,1024]{1,0:T(8,128)(2,1)S(1)}, u32[]{:S(2)}, u32[]{:S(2)}) collective-permute-start(bf16[144,1024]{1,0:T(8,128)(2,1)S(1)} %maximum_maximum_fusion), channel_id=1, source_target_pairs={{0,0},{1,32},{2,2},{3,34},{4,4},{5,36},{6,6},{7,38},{8,8},{9,40},{... | collective-permute-start | bytes 884744 | tf_op jit(solution)/shard_map/ppermute | solution.py:31
  8.2 1.9 %collective-permute-start.1 = (bf16[128,1024]{1,0:T(8,128)(2,1)}, bf16[128,1024]{1,0:T(8,128)(2,1)S(1)}, u32[]{:S(2)}, u32[]{:S(2)}) collective-permute-start(bf16[128,1024]{1,0:T(8,128)(2,1)} %bitcast.13), channel_id=1, source_target_pairs={{0,0},{1,32},{2,2},{3,34},{4,4},{5,36},{6,6},{7,38},{8,8},{9,40},{... | collective-permute-start | bytes 786440 | tf_op jit(solution)/shard_map/ppermute | solution.py:31
  10.1 6.0 %collective-permute-done.1.g_ref = bf16[128,1024]{1,0:T(8,128)(2,1)S(1)} collective-permute-done((bf16[128,1024]{1,0:T(8,128)(2,1)}, bf16[128,1024]{1,0:T(8,128)(2,1)S(1)}, u32[]{:S(2)}, u32[]{:S(2)}) %collective-permute-start.1) | collective-permute-done | bytes 262176 | tf_op jit(solution)/shard_map/ppermute | solution.py:31
  17.5 7.1 %project.1 = (bf16[16,128,1024]{2,1,0:T(8,128)(2,1)}, bf16[16,256,128]{2,1,0:T(8,128)(2,1)}) custom-call(bf16[144,1024]{1,0:T(8,128)(2,1)} %copy-done.4, bf16[128,1024]{1,0:T(8,128)(2,1)} %copy-done.5, bf16[1024,3072]{1,0:T(8,128)(2,1)} %w_ref.3), custom_call_target="tpu_custom_call" | custom-call | flops 805306368 | bytes 8388608 | tf_op jit(solution)/shard_map/project/pallas_call | solution.py:109
  24.6 18.6 %all_to_all.20.recv_ref = bf16[16,256,128]{2,1,0:T(8,128)(2,1)S(1)} all-to-all(bf16[16,256,128]{2,1,0:T(8,128)(2,1)} %get-tuple-element.25), channel_id=1, replica_groups={{0,2,4,6,8,10,12,14,16,18,20,22,24,26,28,30},{1,3,5,7,9,11,13,15,17,19,..., dimensions={0} | all-to-all | bytes 2097152 | tf_op jit(solution)/shard_map/all_to_all | solution.py:39
  43.2 4.5 %all-to-all-start.1 = ((bf16[16,128,1024]{2,1,0:T(8,128)(2,1)}), bf16[16,128,1024]{2,1,0:T(8,128)(2,1)}, u32[]{:S(2)}, u32[]{:S(2)}) async-start(bf16[16,128,1024]{2,1,0:T(8,128)(2,1)} %get-tuple-element.26), calls=%async_computation.1 | async-start | bytes 8388608 | tf_op jit(solution)/shard_map/all_to_all | solution.py:39
  47.9 1.9 %collective-permute-done.2.kvp_ref = bf16[16,128,128]{2,1,0:T(8,128)(2,1)S(1)} collective-permute-done((bf16[16,128,128]{2,1,0:T(8,128)(2,1)S(1)}, bf16[16,128,128]{2,1,0:T(8,128)(2,1)S(1)}, u32[]{:S(2)}, u32[]{:S(2)}) %collective-permute-start.2) | collective-permute-done | bytes 524320 | tf_op jit(solution)/shard_map/ppermute | solution.py:35
  49.8 32.8 %attention.1 = (bf16[16,256,128]{2,1,0:T(8,128)(2,1)}, f32[16,128,128]{2,1,0:T(8,128)S(1)}, bf16[16,128,128]{2,1,0:T(8,128)(2,1)S(1)}) custom-call(bf16[16,256,128]{2,1,0:T(8,128)(2,1)S(1)} %all_to_all.20.recv_ref, bf16[16,128,128]{2,1,0:T(8,128)(2,1)S(1)} %collective-permute-done.2.kvp_ref), custom_call_target="tpu_custom_call" | custom-call | flops 25769803776 | bytes 4194304 | tf_op jit(solution)/shard_map/attention/pallas_call | solution.py:193
  82.7 1.8 %collective-permute-done.3.mine_ref = bf16[16,128,128]{2,1,0:T(8,128)(2,1)S(1)} collective-permute-done((bf16[16,128,128]{2,1,0:T(8,128)(2,1)S(1)}, bf16[16,128,128]{2,1,0:T(8,128)(2,1)S(1)}, u32[]{:S(2)}, u32[]{:S(2)}) %collective-permute-start.3) | collective-permute-done | bytes 524320 | tf_op jit(solution)/shard_map/ppermute | solution.py:35
  84.5 0.9 combine.1.back_ref
  85.4 10.4 %all-to-all-done.1 = bf16[16,128,1024]{2,1,0:T(8,128)(2,1)} async-done(((bf16[16,128,1024]{2,1,0:T(8,128)(2,1)}), bf16[16,128,1024]{2,1,0:T(8,128)(2,1)}, u32[]{:S(2)}, u32[]{:S(2)}) %all-to-all-start.1) | async-done | bytes 4194336 | tf_op jit(solution)/shard_map/all_to_all | solution.py:39
  95.8 3.8 %all-to-all-start.2 = ((bf16[16,256,128]{2,1,0:T(8,128)(2,1)}), bf16[16,256,128]{2,1,0:T(8,128)(2,1)S(1)}, u32[]{:S(2)}, u32[]{:S(2)}) async-start(bf16[16,256,128]{2,1,0:T(8,128)(2,1)} %combine.1.back_ref), calls=%async_computation.2 | async-start | bytes 2097152 | tf_op jit(solution)/shard_map/all_to_all | solution.py:39
  100.2 6.9 %weight_grad.1 = (f32[32,24,128]{2,1,0:T(8,128)}, f32[32,24,128]{2,1,0:T(8,128)}, f32[2,1024]{1,0:T(2,128)}) custom-call(s32[3]{0:T(128)} %pad_add_fusion.place_ref, bf16[2048,1024]{1,0:T(8,128)(2,1)} %bitcast.6.xhat_ref, bf16[16,256,128]{2,1,0:T(8,128)(2,1)} %combine.1.back_ref, bf16[144,1024]{1,0:T(8,128)(2,1)} %copy-done.4, bf16[1024,3072]{1,0:T(8,128)(2,1)} %w_ref.3, ...), custom_call_target="tpu_custom_call" | custom-call | flops 1073741824 | bytes 6291456 | tf_op jit(solution)/shard_map/weight_grad/pallas_call | solution.py:297
  107.2 1.9 %collective-permute-done.4.got_ref = f32[32,24,128]{2,1,0:T(8,128)S(1)} collective-permute-done((f32[32,24,128]{2,1,0:T(8,128)}, f32[32,24,128]{2,1,0:T(8,128)S(1)}, u32[]{:S(2)}, u32[]{:S(2)}) %collective-permute-start.4) | collective-permute-done | bytes 393248 | tf_op jit(solution)/shard_map/ppermute | solution.py:35
  109.1 1.0 copy-done
  110.8 0.8 pack.1
  111.6 5.8 %all-to-all-done.2.back_ref = bf16[16,256,128]{2,1,0:T(8,128)(2,1)S(1)} async-done(((bf16[16,256,128]{2,1,0:T(8,128)(2,1)}), bf16[16,256,128]{2,1,0:T(8,128)(2,1)S(1)}, u32[]{:S(2)}, u32[]{:S(2)}) %all-to-all-start.2) | async-done | bytes 1048608 | tf_op jit(solution)/shard_map/all_to_all | solution.py:39
  117.4 3.9 %all-to-all-start.3 = ((bf16[32,56,128]{2,1,0:T(8,128)(2,1)}), bf16[32,56,128]{2,1,0:T(8,128)(2,1)S(1)}, u32[]{:S(2)}, u32[]{:S(2)}) async-start(bf16[32,56,128]{2,1,0:T(8,128)(2,1)} %pack.1), calls=%async_computation.3 | async-start | bytes 917504 | tf_op jit(solution)/shard_map/all_to_all | solution.py:474
  121.3 6.1 %token_grad.1 = bf16[2,128,1024]{2,1,0:T(8,128)(2,1)} custom-call(bf16[144,1024]{1,0:T(8,128)(2,1)} %copy-done.4, bf16[16,256,128]{2,1,0:T(8,128)(2,1)} %copy-done.3, bf16[1024,3072]{1,0:T(8,128)(2,1)} %w_ref.3), custom_call_target="tpu_custom_call" | custom-call | flops 805306368 | bytes 8388608 | tf_op jit(solution)/shard_map/token_grad/pallas_call | solution.py:439
  127.4 4.4 %all-to-all-done.3.pieces_ref = bf16[32,56,128]{2,1,0:T(8,128)(2,1)S(1)} async-done(((bf16[32,56,128]{2,1,0:T(8,128)(2,1)}), bf16[32,56,128]{2,1,0:T(8,128)(2,1)S(1)}, u32[]{:S(2)}, u32[]{:S(2)}) %all-to-all-start.3) | async-done | bytes 458784 | tf_op jit(solution)/shard_map/all_to_all | solution.py:474
  132.5 8.4 %collective-permute-start.7 = (bf16[16,3072]{1,0:T(8,128)(2,1)S(1)}, bf16[16,3072]{1,0:T(8,128)(2,1)S(1)}, u32[]{:S(2)}, u32[]{:S(2)}) collective-permute-start(bf16[16,3072]{1,0:T(8,128)(2,1)S(1)} %get-tuple-element.38), channel_id=1, source_target_pairs={{0,192},{32,224},{64,128},{96,160},{128,64},{160,96},{192,0},{224,... | collective-permute-start | bytes 294920 | tf_op jit(solution)/shard_map/ppermute | solution.py:480
  140.9 1.0 collective-permute-start.6
  141.9 1.2 collective-permute-start.5
  143.1 4.5 %collective-permute-start.9 = (bf16[2,128,1024]{2,1,0:T(8,128)(2,1)}, bf16[2,128,1024]{2,1,0:T(8,128)(2,1)S(1)}, u32[]{:S(2)}, u32[]{:S(2)}) collective-permute-start(bf16[2,128,1024]{2,1,0:T(8,128)(2,1)} %token_grad.1), channel_id=1, source_target_pairs={{0,0},{1,32},{2,2},{3,34},{4,4},{5,36},{6,6},{7,38},{8,8},{9,40},{... | collective-permute-start | bytes 1572872 | tf_op jit(solution)/shard_map/ppermute | solution.py:31
  147.6 1.3 collective-permute-done.7
  148.8 1.1 collective-permute-done.6
  150.1 4.1 %collective-permute-start.8 = (f32[16,3200]{1,0:T(8,128)S(1)}, f32[16,3200]{1,0:T(8,128)S(1)}, u32[]{:S(2)}, u32[]{:S(2)}) collective-permute-start(f32[16,3200]{1,0:T(8,128)S(1)} %pad_maximum_fusion.1), channel_id=1, source_target_pairs={{0,32},{32,0},{64,96},{96,64},{128,160},{160,128},{192,224},{224,1... | collective-permute-start | bytes 614408 | tf_op jit(solution)/shard_map/ppermute | solution.py:35
  154.1 1.1 collective-permute-done.8
  156.4 0.8 fusion
  157.2 0.8 pad_maximum_fusion
  (29 shorter events, 5.0 us)
Async XLA Ops:
  3.2 12.9 %collective-permute-start = (bf16[144,1024]{1,0:T(8,128)(2,1)S(1)}, bf16[144,1024]{1,0:T(8,128)(2,1)S(1)}, u32[]{:S(2)}, u32[]{:S(2)}) collective-permute-start(bf16[144,1024]{1,0:T(8,128)(2,1)S(1)} %maximum_maximum_fusion), channel_id=1, source_target_pairs={{0,0},{1,32},{2,2},{3,34},{4,4},{5,36},{6,6},{7,38},{8,8},{9,40},{... | collective-permute-start | bytes 884744 | tf_op jit(solution)/shard_map/ppermute | solution.py:31
  8.2 7.9 %collective-permute-start.1 = (bf16[128,1024]{1,0:T(8,128)(2,1)}, bf16[128,1024]{1,0:T(8,128)(2,1)S(1)}, u32[]{:S(2)}, u32[]{:S(2)}) collective-permute-start(bf16[128,1024]{1,0:T(8,128)(2,1)} %bitcast.13), channel_id=1, source_target_pairs={{0,0},{1,32},{2,2},{3,34},{4,4},{5,36},{6,6},{7,38},{8,8},{9,40},{... | collective-permute-start | bytes 786440 | tf_op jit(solution)/shard_map/ppermute | solution.py:31
  16.1 0.7 copy-start.5
  16.8 0.7 copy-start.4
  43.2 52.6 %all-to-all-start.1 = ((bf16[16,128,1024]{2,1,0:T(8,128)(2,1)}), bf16[16,128,1024]{2,1,0:T(8,128)(2,1)}, u32[]{:S(2)}, u32[]{:S(2)}) async-start(bf16[16,128,1024]{2,1,0:T(8,128)(2,1)} %get-tuple-element.26), calls=%async_computation.1 | async-start | bytes 8388608 | tf_op jit(solution)/shard_map/all_to_all | solution.py:39
  47.8 2.0 %collective-permute-start.2 = (bf16[16,128,128]{2,1,0:T(8,128)(2,1)S(1)}, bf16[16,128,128]{2,1,0:T(8,128)(2,1)S(1)}, u32[]{:S(2)}, u32[]{:S(2)}) collective-permute-start(bf16[16,128,128]{2,1,0:T(8,128)(2,1)S(1)} %slice.15), channel_id=1, source_target_pairs={{0,32},{32,0},{64,96},{96,64},{128,160},{160,128},{192,224},{224,1... | collective-permute-start | bytes 1572872 | tf_op jit(solution)/shard_map/ppermute | solution.py:35
  82.6 1.9 %collective-permute-start.3 = (bf16[16,128,128]{2,1,0:T(8,128)(2,1)S(1)}, bf16[16,128,128]{2,1,0:T(8,128)(2,1)S(1)}, u32[]{:S(2)}, u32[]{:S(2)}) collective-permute-start(bf16[16,128,128]{2,1,0:T(8,128)(2,1)S(1)} %get-tuple-element.30), channel_id=1, source_target_pairs={{0,32},{32,0},{64,96},{96,64},{128,160},{160,128},{192,224},{224,1... | collective-permute-start | bytes 1572872 | tf_op jit(solution)/shard_map/ppermute | solution.py:35
  95.8 21.6 %all-to-all-start.2 = ((bf16[16,256,128]{2,1,0:T(8,128)(2,1)}), bf16[16,256,128]{2,1,0:T(8,128)(2,1)S(1)}, u32[]{:S(2)}, u32[]{:S(2)}) async-start(bf16[16,256,128]{2,1,0:T(8,128)(2,1)} %combine.1.back_ref), calls=%async_computation.2 | async-start | bytes 2097152 | tf_op jit(solution)/shard_map/all_to_all | solution.py:39
  107.2 1.9 %collective-permute-start.4 = (f32[32,24,128]{2,1,0:T(8,128)}, f32[32,24,128]{2,1,0:T(8,128)S(1)}, u32[]{:S(2)}, u32[]{:S(2)}) collective-permute-start(f32[32,24,128]{2,1,0:T(8,128)} %get-tuple-element.32), channel_id=1, source_target_pairs={{0,32},{32,0},{64,96},{96,64},{128,160},{160,128},{192,224},{224,1... | collective-permute-start | bytes 1179656 | tf_op jit(solution)/shard_map/ppermute | solution.py:35
  109.1 1.0 copy-start
  110.1 0.7 copy-start.1
  117.4 3.9 %copy-start.3 = (bf16[16,256,128]{2,1,0:T(8,128)(2,1)}, bf16[16,256,128]{2,1,0:T(8,128)(2,1)S(1)}, u32[]{:S(2)}) copy-start(bf16[16,256,128]{2,1,0:T(8,128)(2,1)S(1)} %all-to-all-done.2.back_ref) | copy-start | bytes 3145732
  117.4 14.4 %all-to-all-start.3 = ((bf16[32,56,128]{2,1,0:T(8,128)(2,1)}), bf16[32,56,128]{2,1,0:T(8,128)(2,1)S(1)}, u32[]{:S(2)}, u32[]{:S(2)}) async-start(bf16[32,56,128]{2,1,0:T(8,128)(2,1)} %pack.1), calls=%async_computation.3 | async-start | bytes 917504 | tf_op jit(solution)/shard_map/all_to_all | solution.py:474
  121.3 10.5 %copy-start.2 = (s32[3]{0:T(128)S(1)}, s32[3]{0:T(128)}, u32[]{:S(2)}) copy-start(s32[3]{0:T(128)} %pad_add_fusion.place_ref) | copy-start | bytes 40
  132.5 16.4 %collective-permute-start.7 = (bf16[16,3072]{1,0:T(8,128)(2,1)S(1)}, bf16[16,3072]{1,0:T(8,128)(2,1)S(1)}, u32[]{:S(2)}, u32[]{:S(2)}) collective-permute-start(bf16[16,3072]{1,0:T(8,128)(2,1)S(1)} %get-tuple-element.38), channel_id=1, source_target_pairs={{0,192},{32,224},{64,128},{96,160},{128,64},{160,96},{192,0},{224,... | collective-permute-start | bytes 294920 | tf_op jit(solution)/shard_map/ppermute | solution.py:480
  140.9 9.1 %collective-permute-start.6 = (bf16[16,3072]{1,0:T(8,128)(2,1)S(1)}, bf16[16,3072]{1,0:T(8,128)(2,1)S(1)}, u32[]{:S(2)}, u32[]{:S(2)}) collective-permute-start(bf16[16,3072]{1,0:T(8,128)(2,1)S(1)} %get-tuple-element.38), channel_id=1, source_target_pairs={{0,128},{32,160},{64,192},{96,224},{128,0},{160,32},{192,64},{224,... | collective-permute-start | bytes 294920 | tf_op jit(solution)/shard_map/ppermute | solution.py:480
  141.9 8.1 %collective-permute-start.5 = (bf16[16,3072]{1,0:T(8,128)(2,1)S(1)}, bf16[16,3072]{1,0:T(8,128)(2,1)S(1)}, u32[]{:S(2)}, u32[]{:S(2)}) collective-permute-start(bf16[16,3072]{1,0:T(8,128)(2,1)S(1)} %get-tuple-element.38), channel_id=1, source_target_pairs={{0,64},{32,96},{64,0},{96,32},{128,192},{160,224},{192,128},{224,1... | collective-permute-start | bytes 294920 | tf_op jit(solution)/shard_map/ppermute | solution.py:480
  143.1 13.3 %collective-permute-start.9 = (bf16[2,128,1024]{2,1,0:T(8,128)(2,1)}, bf16[2,128,1024]{2,1,0:T(8,128)(2,1)S(1)}, u32[]{:S(2)}, u32[]{:S(2)}) collective-permute-start(bf16[2,128,1024]{2,1,0:T(8,128)(2,1)} %token_grad.1), channel_id=1, source_target_pairs={{0,0},{1,32},{2,2},{3,34},{4,4},{5,36},{6,6},{7,38},{8,8},{9,40},{... | collective-permute-start | bytes 1572872 | tf_op jit(solution)/shard_map/ppermute | solution.py:31
  150.1 5.1 %collective-permute-start.8 = (f32[16,3200]{1,0:T(8,128)S(1)}, f32[16,3200]{1,0:T(8,128)S(1)}, u32[]{:S(2)}, u32[]{:S(2)}) collective-permute-start(f32[16,3200]{1,0:T(8,128)S(1)} %pad_maximum_fusion.1), channel_id=1, source_target_pairs={{0,32},{32,0},{64,96},{96,64},{128,160},{160,128},{192,224},{224,1... | collective-permute-start | bytes 614408 | tf_op jit(solution)/shard_map/ppermute | solution.py:35
